TPU v7x, 32 devices: a whole 2x2x4 slice. The times are simulated.
32 devices in a mesh: env: 4 (over y, x), wave: 8 (over z, core).
Axes of the slice: x: 2, y: 2, z: 4, core: 2. Of those that a mesh axis runs over, the one named last changes fastest.
Arguments:
- psi: bfloat16 [512, 128, 128], P('wave'), may hold values from -6 to 6
- left_env: bfloat16 [40, 8, 128, 128], P('env', 'wave'), may hold values from -0.5 to 0.5
- right_env: bfloat16 [40, 8, 128, 128], P('env', 'wave'), may hold values from -0.078125 to 0.078125
- left_sector: int32 [512, 1], P('wave'), may hold values from 0 to 7; in each aligned block of 64 rows (0 to 63, 64 to 127, ...) at most 16 rows name the same one
- right_sector: int32 [512, 1], P('wave'), may hold values from 0 to 7
- sector_owner: int32 [8], replicated, may hold values from 0 to 7, each once
- sector_rows: int32 [8], replicated, may hold values from 64 to 128
Outputs:
- h_psi: bfloat16 [512, 128, 128], P('wave', 'env')
Inputs may be any that keep to these rules, and one draw needn't show every extreme that they name: `left_sector`: among the 64 blocks of one wave index no left sector appears more than 16 times, and some sector appears exactly 16 times. `sector_owner`: each wave index holds the environments of exactly one sector.
All inputs are finite; a program needn't handle non-finite values.
Results may differ from a plain program's by a relative error of at most 0.013.
Values may be sent and summed in bfloat16 or wider, within the bound.
No kernel may reach another device: no remote copies, remote signals or barrier semaphores. Data moves between devices by JAX's collectives and lax.ppermute only.
A program may use at most 128 MiB of HBM per device.

v0:
```python
import jax
import jax.numpy as jnp
from jax import lax
from jax.sharding import PartitionSpec as P


def on_device(psi, left_env, right_env, left_sector, right_sector, sector_owner, sector_rows):
    nwave = lax.axis_size("wave")
    nenv = lax.axis_size("env")
    count = psi.shape[0]
    width = psi.shape[1]
    capacity = max(2, 2 * count // nwave)
    sectors = sector_owner.shape[0]
    labels = jnp.arange(sectors, dtype=jnp.int32)
    lsec = left_sector[:, 0]
    rsec = right_sector[:, 0]
    lhot = (lsec[:, None] == labels[None, :]).astype(jnp.int32)
    rhot = (rsec[:, None] == labels[None, :]).astype(jnp.int32)
    target = jnp.sum(lhot * sector_owner[None, :], axis=1)
    rplace = jnp.sum(rhot * sector_owner[None, :], axis=1)
    lrows = jnp.sum(lhot * sector_rows[None, :], axis=1)
    rrows = jnp.sum(rhot * sector_rows[None, :], axis=1)
    line = jnp.arange(width, dtype=jnp.int32)
    full_mask = (line[None, :, None] < lrows[:, None, None]) & (
        line[None, None, :] < rrows[:, None, None]
    )
    masked = jnp.where(full_mask, psi, jnp.zeros_like(psi))
    peers = jnp.arange(nwave, dtype=jnp.int32)
    dest_hot = (target[:, None] == peers[None, :]).astype(jnp.int32)
    rank = jnp.sum((jnp.cumsum(dest_hot, axis=0) - dest_hot) * dest_hot, axis=1)
    slot = target * capacity + rank
    outgoing = jnp.zeros((nwave * capacity, width, width), jnp.bfloat16).at[slot].set(masked)
    outgoing = outgoing.reshape(nwave, capacity, width, width)
    places = jnp.zeros((nwave * capacity,), jnp.int32).at[slot].set(rplace)
    places = places.reshape(nwave, capacity, 1)
    left_own = left_env[:, 0]
    right_all = lax.all_gather(right_env, "wave", axis=1, tiled=True)

    def slot_work(items):
        blocks, where = items
        inner = jnp.einsum("wab,nbc->nwac", left_own, blocks, preferred_element_type=jnp.float32)
        inner = inner.astype(jnp.bfloat16)
        chosen = jnp.take(right_all, where, axis=1)
        part = jnp.einsum("nwac,wncd->nad", inner, chosen, preferred_element_type=jnp.float32)
        return part.astype(jnp.bfloat16)

    blocks = lax.all_to_all(outgoing, "wave", split_axis=0, concat_axis=0, tiled=True)
    where = lax.all_to_all(places, "wave", split_axis=0, concat_axis=0, tiled=True)
    sources = blocks.shape[0]
    items = blocks.shape[1]
    groups = sources // 8
    flat_blocks = blocks.reshape(groups, 8 * items, width, width)
    flat_where = where.reshape(groups, 8 * items)
    parts = lax.map(slot_work, (flat_blocks, flat_where))
    parts = parts.reshape(sources, items, width, width)
    returned = lax.all_to_all(parts, "wave", split_axis=0, concat_axis=0, tiled=True)
    rows_here = returned.shape[2]
    home = returned.reshape(nwave * capacity, rows_here, width)[slot]
    total = lax.psum_scatter(
        home.astype(jnp.float32).astype(jnp.bfloat16), "env", scatter_dimension=1, tiled=True
    ).astype(jnp.float32)
    share = width // nenv
    base = lax.axis_index("env") * share
    row_line = base + jnp.arange(share, dtype=jnp.int32)
    out_mask = (row_line[None, :, None] < lrows[:, None, None]) & (
        line[None, None, :] < rrows[:, None, None]
    )
    return jnp.where(out_mask, total, jnp.zeros_like(total)).astype(jnp.bfloat16)


def solution(mesh):
    return jax.shard_map(
        on_device,
        mesh=mesh,
        in_specs=(
            P("wave", None, None),
            P("env", "wave", None, None),
            P("env", "wave", None, None),
            P("wave", None),
            P("wave", None),
            P(),
            P(),
        ),
        out_specs=P("wave", "env", None),
        check_vma=False,
    )
```

profile of v0, /device:TPU:0, one launch (start us, length us, event | category | flops | bytes accessed | tf_op | source)
XLA Modules:
  0.0 331.9 jit_solution(2731185620339510192)
XLA Ops:
  6.5 0.0 copy-start
  6.5 1.0 select_reduce_fusion.4
  7.5 0.1 fusion.15
  7.6 0.1 reduce_window_sum.11
  7.7 0.2 select_reduce_fusion.1
  7.9 0.8 scatter_custom_fusion.1
  8.7 0.7 reshape.163
  9.3 6.3 %all-to-all-start.1 = ((s32[8,16,1]{1,2,0:T(1,128)}), s32[8,16,1]{1,2,0:T(1,128)S(1)}, u32[]{:S(2)}, u32[]{:S(2)}) async-start(s32[8,16,1]{1,2,0:T(1,128)} %bitcast.11), calls=%async_computation.1 | async-start | bytes 8192 | tf_op jit(solution)/shard_map/all_to_all | solution.py:48
  15.7 0.1 iota_compare_fusion
  15.8 3.2 and_select_fusion
  19.0 3.0 broadcast_in_dim.25
  21.9 8.6 %scatter_fusion = bf16[128,128,128]{2,1,0:T(8,128)(2,1)} fusion(bf16[128,128,128]{2,1,0:T(8,128)(2,1)} %broadcast_in_dim.25, s32[64]{0:T(128)S(1)} %fusion.16, bf16[64,128,128]{2,1,0:T(8,128)(2,1)S(1)} %and_select_fusion), kind=kCustom, calls=%fused_computation.2 | custom fusion | bytes 6291712 | tf_op jit(solution)/shard_map/scatter | solution.py:32
  30.5 6.4 %copy.8 = bf16[8,16,128,128]{2,3,1,0:T(8,128)(2,1)} copy(bf16[8,16,128,128]{3,2,1,0:T(8,128)(2,1)} %bitcast.38) | data formatting | bytes 8388608 | tf_op jit(solution)/shard_map/reshape | solution.py:33
  36.9 0.0 all-to-all-done.1
  36.9 5.2 %all-to-all-start = ((bf16[8,16,128,128]{2,3,1,0:T(8,128)(2,1)}), bf16[8,16,128,128]{2,3,1,0:T(8,128)(2,1)}, u32[]{:S(2)}, u32[]{:S(2)}) async-start(bf16[8,16,128,128]{2,3,1,0:T(8,128)(2,1)} %copy.8), calls=%async_computation | async-start | bytes 8388608 | tf_op jit(solution)/shard_map/all_to_all | solution.py:47
  42.1 0.0 all-gather.2.cloned.1.call-start
  42.1 0.7 all-gather.2.cloned.1.call-update
  42.8 0.1 squeeze.18
  42.9 0.5 broadcast.159
  43.4 0.7 reduce.5
  44.1 0.1 squeeze.17
  44.2 59.4 %all-gather.2.cloned.1.call-done = bf16[10,8,128,128]{3,2,1,0:T(8,128)(2,1)} async-done(((bf16[10,1,128,128]{3,2,1,0:T(8,128)(2,1)}), bf16[10,8,128,128]{3,2,1,0:T(8,128)(2,1)}) %all-gather.2.cloned.1.call-update) | async-done | bytes 2621456 | tf_op jit(solution)/shard_map/all_gather | solution.py:37
  103.6 16.6 %gather_fusion = bf16[128,10,128,128]{3,2,1,0:T(8,128)(2,1)} fusion(bf16[10,8,128,128]{3,2,1,0:T(8,128)(2,1)} %all-gather.2.cloned.1.call-done, s32[1024]{0:T(1024)S(1)} %pad_clamp_fusion.1), kind=kCustom, calls=%fused_computation | custom fusion | bytes 83886592 | tf_op jit(solution)/shard_map/while/body/eval_jaxpr/jit(_take)/gather | solution.py:43
  120.2 37.1 %all-to-all-done = bf16[8,16,128,128]{2,3,1,0:T(8,128)(2,1)} async-done(((bf16[8,16,128,128]{2,3,1,0:T(8,128)(2,1)}), bf16[8,16,128,128]{2,3,1,0:T(8,128)(2,1)}, u32[]{:S(2)}, u32[]{:S(2)}) %all-to-all-start) | async-done | bytes 4194336 | tf_op jit(solution)/shard_map/all_to_all | solution.py:47
  157.3 0.0 copy-done
  157.3 28.5 %bitcast_convert_fusion = bf16[128,128,128]{2,1,0:T(8,128)(2,1)} fusion(bf16[128,10,128,128]{3,2,1,0:T(8,128)(2,1)} %gather_fusion, pred[128]{0:T(512)(128)(4,1)S(1)} %compare_and_fusion, bf16[128,128,128,1]{1,2,3,0:T(8,128)(2,1)} %bitcast.7, bf16[10,1,128,128]{3,2,1,0:T(8,128)(2,1)S(1)} %copy-done), kind=kOutput, calls=%fused_computation.12 | convolution fusion | flops 10781458432 | bytes 50659456 | tf_op jit(solution)/shard_map/while/body/eval_jaxpr/nwac,wncd->nad/dot_general | solution.py:44
  185.8 4.5 %all-to-all-start.2 = ((bf16[8,16,128,128]{3,2,1,0:T(8,128)(2,1)}), bf16[8,16,128,128]{3,2,1,0:T(8,128)(2,1)}, u32[]{:S(2)}, u32[]{:S(2)}) async-start(bf16[8,16,128,128]{3,2,1,0:T(8,128)(2,1)} %bitcast.39), calls=%async_computation.2 | async-start | bytes 8388608 | tf_op jit(solution)/shard_map/all_to_all | solution.py:56
  190.3 0.0 copy-start.1
  190.3 0.0 reduce-scatter.2.cloned.1.call-start
  190.4 93.9 %all-to-all-done.2 = bf16[8,16,128,128]{3,2,1,0:T(8,128)(2,1)} async-done(((bf16[8,16,128,128]{3,2,1,0:T(8,128)(2,1)}), bf16[8,16,128,128]{3,2,1,0:T(8,128)(2,1)}, u32[]{:S(2)}, u32[]{:S(2)}) %all-to-all-start.2) | async-done | bytes 4194336 | tf_op jit(solution)/shard_map/all_to_all | solution.py:56
  284.3 4.3 %gather_fusion.1 = bf16[64,128,128]{2,1,0:T(8,128)(2,1)} fusion(bf16[128,128,128]{2,1,0:T(8,128)(2,1)} %bitcast.17, s32[1024]{0:T(1024)S(1)} %pad_clamp_fusion), kind=kCustom, calls=%fused_computation.1 | custom fusion | bytes 4194560 | tf_op jit(solution)/shard_map/gather | solution.py:58
  288.6 0.0 reduce-scatter.2.cloned.1.call-update
  288.7 0.1 broadcast_compare_fusion
  288.8 34.1 %reduce-scatter.2.cloned.1.call-done = bf16[64,32,128]{2,1,0:T(8,128)(2,1)} async-done(((bf16[64,128,128]{2,1,0:T(8,128)(2,1)}), bf16[64,32,128]{2,1,0:T(8,128)(2,1)}) %reduce-scatter.2.cloned.1.call-update) | async-done | bytes 524304 | tf_op jit(solution)/shard_map/reduce_scatter | solution.py:59
  322.9 2.2 select_convert_fusion
  325.1 0.0 copy-done.1
  (6 shorter events, 0.0 us)
Async XLA Ops:
  6.5 150.8 %copy-start = (bf16[10,1,128,128]{3,2,1,0:T(8,128)(2,1)S(1)}, bf16[10,1,128,128]{3,2,1,0:T(8,128)(2,1)}, u32[]{:S(2)}) copy-start(bf16[10,1,128,128]{3,2,1,0:T(8,128)(2,1)} %param.8) | copy-start | bytes 983044
  9.3 27.6 %all-to-all-start.1 = ((s32[8,16,1]{1,2,0:T(1,128)}), s32[8,16,1]{1,2,0:T(1,128)S(1)}, u32[]{:S(2)}, u32[]{:S(2)}) async-start(s32[8,16,1]{1,2,0:T(1,128)} %bitcast.11), calls=%async_computation.1 | async-start | bytes 8192 | tf_op jit(solution)/shard_map/all_to_all | solution.py:48
  36.9 120.3 %all-to-all-start = ((bf16[8,16,128,128]{2,3,1,0:T(8,128)(2,1)}), bf16[8,16,128,128]{2,3,1,0:T(8,128)(2,1)}, u32[]{:S(2)}, u32[]{:S(2)}) async-start(bf16[8,16,128,128]{2,3,1,0:T(8,128)(2,1)} %copy.8), calls=%async_computation | async-start | bytes 8388608 | tf_op jit(solution)/shard_map/all_to_all | solution.py:47
  42.1 61.5 %all-gather.2.cloned.1.call-start = ((), (), s32[]{:S(2)}) async-start(), calls=%async_computation.4 | async-start | bytes 2949120 | tf_op jit(solution)/shard_map/all_gather | solution.py:37
  185.8 98.6 %all-to-all-start.2 = ((bf16[8,16,128,128]{3,2,1,0:T(8,128)(2,1)}), bf16[8,16,128,128]{3,2,1,0:T(8,128)(2,1)}, u32[]{:S(2)}, u32[]{:S(2)}) async-start(bf16[8,16,128,128]{3,2,1,0:T(8,128)(2,1)} %bitcast.39), calls=%async_computation.2 | async-start | bytes 8388608 | tf_op jit(solution)/shard_map/all_to_all | solution.py:56
  190.3 134.8 %copy-start.1 = (bf16[10,1,128,128]{3,2,1,0:T(8,128)(2,1)S(1)}, bf16[10,1,128,128]{3,2,1,0:T(8,128)(2,1)}, u32[]{:S(2)}) copy-start(bf16[10,1,128,128]{3,2,1,0:T(8,128)(2,1)} %param.8) | copy-start | bytes 983044
  190.3 132.6 %reduce-scatter.2.cloned.1.call-start = ((), (), s32[]{:S(2)}) async-start(), calls=%async_computation.5 | async-start | bytes 2621440 | tf_op jit(solution)/shard_map/reduce_scatter | solution.py:59
Sparse Core Ops, SparseCore 0:
  44.5 58.9 all-gather.1
  288.8 34.0 reduce-scatter.1
where the time goes:
time: 333 us; the launch traced here: 332 us
  waiting for transfers between devices  225 us (68%)
  local copies, waits for them, and re-layouts  41.1 us (12%)
  matrix products  28.5 us (9%)
  starting transfers between devices  16.1 us (5%)
  between operations  13.5 us (4%)
  other arithmetic  7.55 us (2%)
    all_to_all x1, waiting for transfers between devices, on_device(): lax.all_to_all(parts, 'wave', split_axis=0, concat_axis=0, tiled=True)  93.9 us
    all_gather x1, waiting for transfers between devices, on_device(): right_all = lax.all_gather(right_env, 'wave', axis=1, tiled=True)  59.4 us
    all_to_all x1, waiting for transfers between devices, on_device(): lax.all_to_all(outgoing, 'wave', split_axis=0, concat_axis=0, tiled=True)  37.1 us
    reduce_scatter x1, waiting for transfers between devices, on_device(): lax.psum_scatter(home.astype(jnp.float32).astype(jnp.bfloat16), 'env', sc...  34.1 us
    dot_general x1, matrix products, slot_work(): jnp.einsum('nwac,wncd->nad', inner, chosen, preferred_element_type=jnp.fl...  28.5 us
    gather x1, local copies, waits for them, and re-layouts, slot_work(): chosen = jnp.take(right_all, where, axis=1)  16.6 us
    scatter x1, local copies, waits for them, and re-layouts, on_device(): jnp.zeros((nwave * capacity, width, width), jnp.bfloat16).at[slot]  8.58 us
  transfers between devices with their start and end apart: 5, of which 4 were waited for; matrix products, arithmetic and copies ran while one was open for 12% of the time, Pallas kernels for 0%

commit v1 on v0

v1 whole, which is shorter than its diff:
```python
import functools

import jax
import jax.numpy as jnp
from jax import lax
from jax.experimental import pallas as pl
from jax.experimental.pallas import tpu as pltpu
from jax.sharding import PartitionSpec as P

CORES = 2
PARTS = 4


def block_kernel(unroll, first, nenv, chips, place, lsec, rsec, owner, live, psi, envs, out):
    blocks, width = out.shape[1], psi.shape[1]
    share = width // nenv
    channels = envs.shape[1] // 2
    chip, core, env = place[0], place[1], place[2]
    row = lax.broadcasted_iota(jnp.int32, (width, width), 0)
    col = lax.broadcasted_iota(jnp.int32, (width, width), 1)

    def slot_of(sector):
        where = owner[sector]
        away = lax.rem(where // CORES - chip + chips, chips)
        return away * CORES + lax.rem(where + core, CORES)

    def one(k):
        left, right = lsec[first + k], rsec[first + k]
        lslot, rslot = slot_of(left), slot_of(right)
        mask = (row < live[left]) & (col < live[right])
        block = psi[first + k]
        block = jnp.where(mask, block, jnp.zeros_like(block))
        lmat = envs[lslot, 0:channels].reshape(channels * width, width)
        y = jnp.dot(lmat, block, preferred_element_type=jnp.float32).astype(jnp.bfloat16)
        wide = jnp.concatenate([y[w * width:(w + 1) * width] for w in range(channels)], axis=1)
        rmat = envs[rslot, channels:2 * channels].reshape(channels * width, width)
        part = jnp.dot(wide, rmat, preferred_element_type=jnp.float32)
        part = jnp.where(mask, part, jnp.zeros_like(part)).astype(jnp.bfloat16)
        for e in range(nenv):
            out[env ^ e, k] = part[e * share:(e + 1) * share]

    def body(g, carry):
        for u in range(unroll):
            one(g * unroll + u)
        return carry

    lax.fori_loop(0, blocks // unroll, body, 0)


def on_device(psi, left_env, right_env, left_sector, right_sector, sector_owner, sector_rows):
    nwave = lax.axis_size("wave")
    nenv = lax.axis_size("env")
    count, width = psi.shape[0], psi.shape[1]
    channels = left_env.shape[0]
    chips = nwave // CORES
    wave = lax.axis_index("wave")
    env = lax.axis_index("env")
    place = jnp.stack([wave // CORES, wave % CORES, env]).astype(jnp.int32)

    up = [(i, (i + CORES) % nwave) for i in range(nwave)]
    down = [((i + CORES) % nwave, i) for i in range(nwave)]
    other = [(i, i ^ 1) for i in range(nwave)]
    swap = lambda x: lax.ppermute(x, "wave", other)

    own = jnp.concatenate([left_env[:, 0], right_env[:, 0]], axis=0)
    held = [[None, None] for _ in range(chips)]
    held[0] = [own, swap(own)]
    rising = falling = own
    for r in range(1, (chips - 1) // 2 + 1):
        rising = lax.ppermute(rising, "wave", up)
        falling = lax.ppermute(falling, "wave", down)
        held[chips - r] = [rising, swap(rising)]
        held[r] = [falling, swap(falling)]
    if chips % 2 == 0 and chips > 1:
        far_left = lax.ppermute(rising[:channels], "wave", up)
        far_right = lax.ppermute(falling[channels:], "wave", down)
        far = jnp.concatenate([far_left, far_right], axis=0)
        far_other = jnp.concatenate([swap(far_left), swap(far_right)], axis=0)
        held[chips // 2] = [far, far_other]
    envs = jnp.stack([piece for pair in held for piece in pair])

    blocks = count // PARTS
    smem = pl.BlockSpec(memory_space=pltpu.SMEM)
    vmem = pl.BlockSpec(memory_space=pltpu.VMEM)
    results = []
    for part in range(PARTS):
        sums = pl.pallas_call(
            functools.partial(block_kernel, 4, part * blocks, nenv, chips),
            out_shape=jax.ShapeDtypeStruct((nenv, blocks, width // nenv, width), jnp.bfloat16),
            in_specs=[smem] * 5 + [vmem] * 2,
            out_specs=vmem,
            compiler_params=pltpu.CompilerParams(vmem_limit_bytes=56 << 20),
            cost_estimate=pl.CostEstimate(
                flops=4 * blocks * channels * width ** 3, bytes_accessed=8 << 20, transcendentals=0
            ),
        )(place, left_sector[:, 0], right_sector[:, 0], sector_owner, sector_rows, psi, envs)
        total = sums[0].astype(jnp.float32)
        for d in range(1, nenv):
            total = total + lax.ppermute(sums[d], "env", [(i, i ^ d) for i in range(nenv)]).astype(jnp.float32)
        results.append(total.astype(jnp.bfloat16))
    return jnp.concatenate(results, axis=0)


def solution(mesh):
    return jax.shard_map(
        on_device,
        mesh=mesh,
        in_specs=(
            P("wave", None, None),
            P("env", "wave", None, None),
            P("env", "wave", None, None),
            P("wave", None),
            P("wave", None),
            P(),
            P(),
        ),
        out_specs=P("wave", "env", None),
        check_vma=False,
    )
```

time: 333 us -> 117 us (0.35)
  waiting for transfers between devices: 225 us -> 51.5 us
  local copies, waits for them, and re-layouts: 41.1 us -> 4.03 us
  Pallas kernels: 0 us -> 31.3 us
  matrix products: 28.5 us -> 0 us
  between operations: 13.5 us -> 0.15 us
  starting transfers between devices: 16.1 us -> 25.1 us
    all_to_all x3 -> x0, waiting for transfers between devices: 131 us -> none  [the longest x1 93.9 us: on_device(): lax.all_to_all(parts, 'wave', split_axis=0, concat_axis=0, tiled=True)]
    all_gather x1 -> x0, waiting for transfers between devices: 59.4 us -> none  [on_device(): right_all = lax.all_gather(right_env, 'wave', axis=1, tiled=True)]
    ppermute x0 -> x21, waiting for transfers between devices: none -> 51.5 us  [the longest x1 15.1 us: on_device(): falling = lax.ppermute(falling, 'wave', down)]
    reduce_scatter x1 -> x0, waiting for transfers between devices: 34.1 us -> none  [on_device(): lax.psum_scatter(home.astype(jnp.float32).astype(jnp.bfloat16), 'env', sc...]
    pallas_call x0 -> x4, Pallas kernels: none -> 31.3 us  [on_device(): pl.pallas_call(functools.partial(block_kernel, 4, part * blocks, nenv, ch...]
    dot_general x1 -> x0, matrix products: 28.5 us -> none  [slot_work(): jnp.einsum('nwac,wncd->nad', inner, chosen, preferred_element_type=jnp.fl...]
    ppermute x0 -> x21, starting transfers between devices: none -> 25.1 us  [the longest x12 16.1 us: on_device(): lax.ppermute(sums[d], 'env', [(i, i ^ d) for i in range(nenv)])]
    gather x2 -> x0, local copies, waits for them, and re-layouts: 21 us -> none  [the longest x1 16.6 us: slot_work(): chosen = jnp.take(right_all, where, axis=1)]
  transfers between devices with their start and end apart: 5 -> 21, of which waited for: 4 -> 12; matrix products, arithmetic and copies ran while one was open for 12% -> 3% of each run, Pallas kernels for 0% -> 0%
where the time goes in v1:
time: 117 us
  waiting for transfers between devices  51.5 us (44%)
  Pallas kernels  31.3 us (27%)
  starting transfers between devices  25.1 us (21%)
  other arithmetic  5.17 us (4%)
  local copies, waits for them, and re-layouts  4.03 us (3%)
    pallas_call x4, Pallas kernels, on_device(): pl.pallas_call(functools.partial(block_kernel, 4, part * blocks, nenv, ch...  31.3 us
    ppermute x12, starting transfers between devices, on_device(): lax.ppermute(sums[d], 'env', [(i, i ^ d) for i in range(nenv)])  16.1 us
    ppermute x1, waiting for transfers between devices, on_device(): falling = lax.ppermute(falling, 'wave', down)  15.1 us
    ppermute x1, waiting for transfers between devices, on_device(): rising = lax.ppermute(rising, 'wave', up)  12 us
    ppermute x12, waiting for transfers between devices, on_device(): lax.ppermute(sums[d], 'env', [(i, i ^ d) for i in range(nenv)])  10 us
    ppermute x1, waiting for transfers between devices, on_device(): far_left = lax.ppermute(rising[:channels], 'wave', up)  8.32 us
    ppermute x1, starting transfers between devices, on_device(): falling = lax.ppermute(falling, 'wave', down)  5.1 us
    ppermute x1, waiting for transfers between devices, on_device(): far_right = lax.ppermute(falling[channels:], 'wave', down)  4.62 us
  transfers between devices with their start and end apart: 21, of which 12 were waited for; matrix products, arithmetic and copies ran while one was open for 3% of the time, Pallas kernels for 0%

profile of v1, /device:TPU:0, one launch (start us, length us, event | category | flops | bytes accessed | tf_op | source)
XLA Modules:
  0.0 117.3 jit_solution(14769675748430282474)
XLA Ops:
  0.0 1.1 pad_maximum_fusion
  1.1 5.1 %collective-permute-start.1 = (bf16[20,128,128]{2,1,0:T(8,128)(2,1)S(1)}, bf16[20,128,128]{2,1,0:T(8,128)(2,1)S(1)}, u32[]{:S(2)}, u32[]{:S(2)}) collective-permute-start(bf16[20,128,128]{2,1,0:T(8,128)(2,1)S(1)} %pad_maximum_fusion), channel_id=1, source_target_pairs={{2,0},{3,1},{4,2},{5,3},{6,4},{7,5},{0,6},{1,7},{10,8},{11,9},{12,... | collective-permute-start | bytes 1966088 | tf_op jit(solution)/shard_map/ppermute | solution.py:71
  6.2 15.1 %collective-permute-done.1 = bf16[20,128,128]{2,1,0:T(8,128)(2,1)S(1)} collective-permute-done((bf16[20,128,128]{2,1,0:T(8,128)(2,1)S(1)}, bf16[20,128,128]{2,1,0:T(8,128)(2,1)S(1)}, u32[]{:S(2)}, u32[]{:S(2)}) %collective-permute-start.1) | collective-permute-done | bytes 655392 | tf_op jit(solution)/shard_map/ppermute | solution.py:71
  21.4 0.7 pad_add_fusion.place
  22.0 1.1 bitcast_dynamic-update-slice_fusion.5
  23.2 12.0 %collective-permute-done.3 = bf16[20,128,128]{2,1,0:T(8,128)(2,1)S(1)} collective-permute-done((bf16[20,128,128]{2,1,0:T(8,128)(2,1)S(1)}, bf16[20,128,128]{2,1,0:T(8,128)(2,1)S(1)}, u32[]{:S(2)}, u32[]{:S(2)}) %collective-permute-start.3) | collective-permute-done | bytes 655392 | tf_op jit(solution)/shard_map/ppermute | solution.py:70
  35.2 1.7 %collective-permute-start.4 = (bf16[10,128,128]{2,1,0:T(8,128)(2,1)S(1)}, bf16[10,128,128]{2,1,0:T(8,128)(2,1)S(1)}, u32[]{:S(2)}, u32[]{:S(2)}) collective-permute-start(bf16[10,128,128]{2,1,0:T(8,128)(2,1)S(1)} %slice.72), channel_id=1, source_target_pairs={{0,2},{1,3},{2,4},{3,5},{4,6},{5,7},{6,0},{7,1},{8,10},{9,11},{10,... | collective-permute-start | bytes 983048 | tf_op jit(solution)/shard_map/ppermute | solution.py:75
  36.9 2.3 %collective-permute-start.5 = (bf16[10,128,128]{2,1,0:T(8,128)(2,1)S(1)}, bf16[10,128,128]{2,1,0:T(8,128)(2,1)S(1)}, u32[]{:S(2)}, u32[]{:S(2)}) collective-permute-start(bf16[10,128,128]{2,1,0:T(8,128)(2,1)S(1)} %slice.73), channel_id=1, source_target_pairs={{2,0},{3,1},{4,2},{5,3},{6,4},{7,5},{0,6},{1,7},{10,8},{11,9},{12,... | collective-permute-start | bytes 983048 | tf_op jit(solution)/shard_map/ppermute | solution.py:76
  39.2 0.1 bitcast_dynamic-update-slice_fusion.4
  39.3 0.1 bitcast_dynamic-update-slice_fusion.3
  39.4 8.3 %collective-permute-done.4 = bf16[10,128,128]{2,1,0:T(8,128)(2,1)S(1)} collective-permute-done((bf16[10,128,128]{2,1,0:T(8,128)(2,1)S(1)}, bf16[10,128,128]{2,1,0:T(8,128)(2,1)S(1)}, u32[]{:S(2)}, u32[]{:S(2)}) %collective-permute-start.4) | collective-permute-done | bytes 327712 | tf_op jit(solution)/shard_map/ppermute | solution.py:75
  47.7 4.6 %collective-permute-done.5 = bf16[10,128,128]{2,1,0:T(8,128)(2,1)S(1)} collective-permute-done((bf16[10,128,128]{2,1,0:T(8,128)(2,1)S(1)}, bf16[10,128,128]{2,1,0:T(8,128)(2,1)S(1)}, u32[]{:S(2)}, u32[]{:S(2)}) %collective-permute-start.5) | collective-permute-done | bytes 327712 | tf_op jit(solution)/shard_map/ppermute | solution.py:76
  52.3 0.1 bitcast_dynamic-update-slice_fusion.2
  52.4 0.1 fusion
  52.6 1.4 %collective-permute-done.7 = bf16[10,128,128]{2,1,0:T(8,128)(2,1)S(1)} collective-permute-done((bf16[10,128,128]{2,1,0:T(8,128)(2,1)S(1)}, bf16[10,128,128]{2,1,0:T(8,128)(2,1)S(1)}, u32[]{:S(2)}, u32[]{:S(2)}) %collective-permute-start.7) | collective-permute-done | bytes 327712 | tf_op jit(solution)/shard_map/ppermute | solution.py:63
  54.0 0.1 fusion.1
  54.1 0.1 bitcast_dynamic-update-slice_fusion.1
  54.2 0.1 bitcast_dynamic-update-slice_fusion.envs
  54.3 2.3 %copy-done = bf16[8,20,128,128]{3,2,1,0:T(8,128)(2,1)} copy-done((bf16[8,20,128,128]{3,2,1,0:T(8,128)(2,1)}, bf16[8,20,128,128]{3,2,1,0:T(8,128)(2,1)S(1)}, u32[]{:S(2)}) %copy-start) | copy-done | bytes 5242904
  56.6 7.8 %shard_map.73 = bf16[4,16,32,128]{3,2,1,0:T(8,128)(2,1)} custom-call(s32[3]{0:T(128)} %pad_add_fusion.place, s32[64]{0:T(128)} %bitcast.75, s32[64]{0:T(128)} %bitcast.79, s32[8]{0:T(128)} %owner.7, s32[8]{0:T(128)} %live.7, bf16[64,128,128]{2,1,0:T(8,128)(2,1)} %psi.7, bf16[8,20,128,128]{3,2,1,0:T(8,128)(2,1)} %copy-done), custom_call_target="tpu_custom_call" | custom-call | flops 1342177280 | bytes 8388608 | tf_op jit(solution)/shard_map/pallas_call | solution.py:87
  64.4 7.8 %shard_map.74 = bf16[4,16,32,128]{3,2,1,0:T(8,128)(2,1)} custom-call(s32[3]{0:T(128)} %pad_add_fusion.place, s32[64]{0:T(128)} %bitcast.76, s32[64]{0:T(128)} %bitcast.80, s32[8]{0:T(128)} %owner.7, s32[8]{0:T(128)} %live.7, bf16[64,128,128]{2,1,0:T(8,128)(2,1)} %psi.7, bf16[8,20,128,128]{3,2,1,0:T(8,128)(2,1)} %copy-done), custom_call_target="tpu_custom_call" | custom-call | flops 1342177280 | bytes 8388608 | tf_op jit(solution)/shard_map/pallas_call | solution.py:87
  72.2 7.8 %shard_map.75 = bf16[4,16,32,128]{3,2,1,0:T(8,128)(2,1)} custom-call(s32[3]{0:T(128)} %pad_add_fusion.place, s32[64]{0:T(128)} %bitcast.77, s32[64]{0:T(128)} %bitcast.81, s32[8]{0:T(128)} %owner.7, s32[8]{0:T(128)} %live.7, bf16[64,128,128]{2,1,0:T(8,128)(2,1)} %psi.7, bf16[8,20,128,128]{3,2,1,0:T(8,128)(2,1)} %copy-done), custom_call_target="tpu_custom_call" | custom-call | flops 1342177280 | bytes 8388608 | tf_op jit(solution)/shard_map/pallas_call | solution.py:87
  80.1 7.9 %shard_map.76 = bf16[4,16,32,128]{3,2,1,0:T(8,128)(2,1)} custom-call(s32[3]{0:T(128)} %pad_add_fusion.place, s32[64]{0:T(128)} %bitcast.78, s32[64]{0:T(128)} %bitcast.82, s32[8]{0:T(128)} %owner.7, s32[8]{0:T(128)} %live.7, bf16[64,128,128]{2,1,0:T(8,128)(2,1)} %psi.7, bf16[8,20,128,128]{3,2,1,0:T(8,128)(2,1)} %copy-done), custom_call_target="tpu_custom_call" | custom-call | flops 1342177280 | bytes 8388608 | tf_op jit(solution)/shard_map/pallas_call | solution.py:87
  88.0 1.6 %collective-permute-start.10 = (bf16[16,32,128]{2,1,0:T(8,128)(2,1)S(1)}, bf16[16,32,128]{2,1,0:T(8,128)(2,1)S(1)}, u32[]{:S(2)}, u32[]{:S(2)}) collective-permute-start(bf16[16,32,128]{2,1,0:T(8,128)(2,1)S(1)} %get-tuple-element.7), channel_id=1, source_target_pairs={{0,16},{8,24},{16,0},{24,8},{1,17},{9,25},{17,1},{25,9},{2,18},{10... | collective-permute-start | bytes 393224 | tf_op jit(solution)/shard_map/ppermute | solution.py:99
  89.6 1.4 %collective-permute-start.11 = (bf16[16,32,128]{2,1,0:T(8,128)(2,1)S(1)}, bf16[16,32,128]{2,1,0:T(8,128)(2,1)S(1)}, u32[]{:S(2)}, u32[]{:S(2)}) collective-permute-start(bf16[16,32,128]{2,1,0:T(8,128)(2,1)S(1)} %get-tuple-element.6), channel_id=1, source_target_pairs={{0,24},{8,16},{16,8},{24,0},{1,25},{9,17},{17,9},{25,1},{2,26},{10... | collective-permute-start | bytes 393224 | tf_op jit(solution)/shard_map/ppermute | solution.py:99
  91.0 0.5 collective-permute-start.9
  91.6 1.6 %collective-permute-start.12 = (bf16[16,32,128]{2,1,0:T(8,128)(2,1)S(1)}, bf16[16,32,128]{2,1,0:T(8,128)(2,1)S(1)}, u32[]{:S(2)}, u32[]{:S(2)}) collective-permute-start(bf16[16,32,128]{2,1,0:T(8,128)(2,1)S(1)} %get-tuple-element.8), channel_id=1, source_target_pairs={{0,8},{8,0},{16,24},{24,16},{1,9},{9,1},{17,25},{25,17},{2,10},{10... | collective-permute-start | bytes 393224 | tf_op jit(solution)/shard_map/ppermute | solution.py:99
  93.1 1.5 %collective-permute-start.13 = (bf16[16,32,128]{2,1,0:T(8,128)(2,1)S(1)}, bf16[16,32,128]{2,1,0:T(8,128)(2,1)S(1)}, u32[]{:S(2)}, u32[]{:S(2)}) collective-permute-start(bf16[16,32,128]{2,1,0:T(8,128)(2,1)S(1)} %get-tuple-element.10), channel_id=1, source_target_pairs={{0,16},{8,24},{16,0},{24,8},{1,17},{9,25},{17,1},{25,9},{2,18},{10... | collective-permute-start | bytes 393224 | tf_op jit(solution)/shard_map/ppermute | solution.py:99
  94.7 1.1 slice_bitcast_fusion.2
  95.8 1.2 collective-permute-done.10
  96.9 2.7 %collective-permute-start.14 = (bf16[16,32,128]{2,1,0:T(8,128)(2,1)S(1)}, bf16[16,32,128]{2,1,0:T(8,128)(2,1)S(1)}, u32[]{:S(2)}, u32[]{:S(2)}) collective-permute-start(bf16[16,32,128]{2,1,0:T(8,128)(2,1)S(1)} %get-tuple-element.9), channel_id=1, source_target_pairs={{0,24},{8,16},{16,8},{24,0},{1,25},{9,17},{17,9},{25,1},{2,26},{10... | collective-permute-start | bytes 393224 | tf_op jit(solution)/shard_map/ppermute | solution.py:99
  99.7 0.5 collective-permute-start.15
  100.2 0.2 collective-permute-start.16
  100.4 0.1 fusion.13
  100.5 1.0 collective-permute-done.12
  101.5 2.4 %collective-permute-start.17 = (bf16[16,32,128]{2,1,0:T(8,128)(2,1)S(1)}, bf16[16,32,128]{2,1,0:T(8,128)(2,1)S(1)}, u32[]{:S(2)}, u32[]{:S(2)}) collective-permute-start(bf16[16,32,128]{2,1,0:T(8,128)(2,1)S(1)} %get-tuple-element.12), channel_id=1, source_target_pairs={{0,24},{8,16},{16,8},{24,0},{1,25},{9,17},{17,9},{25,1},{2,26},{10... | collective-permute-start | bytes 393224 | tf_op jit(solution)/shard_map/ppermute | solution.py:99
  104.0 0.5 collective-permute-start.18
  104.5 0.8 collective-permute-done.14
  105.3 0.8 collective-permute-start.19
  106.1 0.1 fusion.10
  106.1 1.3 %collective-permute-done.15 = bf16[16,32,128]{2,1,0:T(8,128)(2,1)S(1)} collective-permute-done((bf16[16,32,128]{2,1,0:T(8,128)(2,1)S(1)}, bf16[16,32,128]{2,1,0:T(8,128)(2,1)S(1)}, u32[]{:S(2)}, u32[]{:S(2)}) %collective-permute-start.15) | collective-permute-done | bytes 131104 | tf_op jit(solution)/shard_map/ppermute | solution.py:99
  107.4 2.2 %collective-permute-start.20 = (bf16[16,32,128]{2,1,0:T(8,128)(2,1)S(1)}, bf16[16,32,128]{2,1,0:T(8,128)(2,1)S(1)}, u32[]{:S(2)}, u32[]{:S(2)}) collective-permute-start(bf16[16,32,128]{2,1,0:T(8,128)(2,1)S(1)} %get-tuple-element.15), channel_id=1, source_target_pairs={{0,24},{8,16},{16,8},{24,0},{1,25},{9,17},{17,9},{25,1},{2,26},{10... | collective-permute-start | bytes 393224 | tf_op jit(solution)/shard_map/ppermute | solution.py:99
  109.6 1.3 %collective-permute-done.17 = bf16[16,32,128]{2,1,0:T(8,128)(2,1)S(1)} collective-permute-done((bf16[16,32,128]{2,1,0:T(8,128)(2,1)S(1)}, bf16[16,32,128]{2,1,0:T(8,128)(2,1)S(1)}, u32[]{:S(2)}, u32[]{:S(2)}) %collective-permute-start.17) | collective-permute-done | bytes 131104 | tf_op jit(solution)/shard_map/ppermute | solution.py:99
  110.9 0.1 fusion.7
  111.0 2.0 %collective-permute-done.18 = bf16[16,32,128]{2,1,0:T(8,128)(2,1)S(1)} collective-permute-done((bf16[16,32,128]{2,1,0:T(8,128)(2,1)S(1)}, bf16[16,32,128]{2,1,0:T(8,128)(2,1)S(1)}, u32[]{:S(2)}, u32[]{:S(2)}) %collective-permute-start.18) | collective-permute-done | bytes 131104 | tf_op jit(solution)/shard_map/ppermute | solution.py:99
  113.0 2.4 %collective-permute-done.20 = bf16[16,32,128]{2,1,0:T(8,128)(2,1)S(1)} collective-permute-done((bf16[16,32,128]{2,1,0:T(8,128)(2,1)S(1)}, bf16[16,32,128]{2,1,0:T(8,128)(2,1)S(1)}, u32[]{:S(2)}, u32[]{:S(2)}) %collective-permute-start.20) | collective-permute-done | bytes 131104 | tf_op jit(solution)/shard_map/ppermute | solution.py:99
  115.4 1.0 fusion.4
  116.4 0.9 pad_maximum_fusion.1
  (27 shorter events, 0.2 us)
Async XLA Ops:
  1.1 20.2 %collective-permute-start.1 = (bf16[20,128,128]{2,1,0:T(8,128)(2,1)S(1)}, bf16[20,128,128]{2,1,0:T(8,128)(2,1)S(1)}, u32[]{:S(2)}, u32[]{:S(2)}) collective-permute-start(bf16[20,128,128]{2,1,0:T(8,128)(2,1)S(1)} %pad_maximum_fusion), channel_id=1, source_target_pairs={{2,0},{3,1},{4,2},{5,3},{6,4},{7,5},{0,6},{1,7},{10,8},{11,9},{12,... | collective-permute-start | bytes 1966088 | tf_op jit(solution)/shard_map/ppermute | solution.py:71
  6.2 28.9 %collective-permute-start.3 = (bf16[20,128,128]{2,1,0:T(8,128)(2,1)S(1)}, bf16[20,128,128]{2,1,0:T(8,128)(2,1)S(1)}, u32[]{:S(2)}, u32[]{:S(2)}) collective-permute-start(bf16[20,128,128]{2,1,0:T(8,128)(2,1)S(1)} %pad_maximum_fusion), channel_id=1, source_target_pairs={{0,2},{1,3},{2,4},{3,5},{4,6},{5,7},{6,0},{7,1},{8,10},{9,11},{10,... | collective-permute-start | bytes 1966088 | tf_op jit(solution)/shard_map/ppermute | solution.py:70
  6.2 32.9 %collective-permute-start = (bf16[20,128,128]{2,1,0:T(8,128)(2,1)S(1)}, bf16[20,128,128]{2,1,0:T(8,128)(2,1)S(1)}, u32[]{:S(2)}, u32[]{:S(2)}) collective-permute-start(bf16[20,128,128]{2,1,0:T(8,128)(2,1)S(1)} %pad_maximum_fusion), channel_id=1, source_target_pairs={{0,1},{1,0},{2,3},{3,2},{4,5},{5,4},{6,7},{7,6},{8,9},{9,8},{10,11... | collective-permute-start | bytes 1966088 | tf_op jit(solution)/shard_map/ppermute | solution.py:63
  21.4 31.0 %collective-permute-start.2 = (bf16[20,128,128]{2,1,0:T(8,128)(2,1)S(1)}, bf16[20,128,128]{2,1,0:T(8,128)(2,1)S(1)}, u32[]{:S(2)}, u32[]{:S(2)}) collective-permute-start(bf16[20,128,128]{2,1,0:T(8,128)(2,1)S(1)} %collective-permute-done.1), channel_id=1, source_target_pairs={{0,1},{1,0},{2,3},{3,2},{4,5},{5,4},{6,7},{7,6},{8,9},{9,8},{10,11... | collective-permute-start | bytes 1966088 | tf_op jit(solution)/shard_map/ppermute | solution.py:63
  35.2 12.5 %collective-permute-start.4 = (bf16[10,128,128]{2,1,0:T(8,128)(2,1)S(1)}, bf16[10,128,128]{2,1,0:T(8,128)(2,1)S(1)}, u32[]{:S(2)}, u32[]{:S(2)}) collective-permute-start(bf16[10,128,128]{2,1,0:T(8,128)(2,1)S(1)} %slice.72), channel_id=1, source_target_pairs={{0,2},{1,3},{2,4},{3,5},{4,6},{5,7},{6,0},{7,1},{8,10},{9,11},{10,... | collective-permute-start | bytes 983048 | tf_op jit(solution)/shard_map/ppermute | solution.py:75
  36.9 15.4 %collective-permute-start.5 = (bf16[10,128,128]{2,1,0:T(8,128)(2,1)S(1)}, bf16[10,128,128]{2,1,0:T(8,128)(2,1)S(1)}, u32[]{:S(2)}, u32[]{:S(2)}) collective-permute-start(bf16[10,128,128]{2,1,0:T(8,128)(2,1)S(1)} %slice.73), channel_id=1, source_target_pairs={{2,0},{3,1},{4,2},{5,3},{6,4},{7,5},{0,6},{1,7},{10,8},{11,9},{12,... | collective-permute-start | bytes 983048 | tf_op jit(solution)/shard_map/ppermute | solution.py:76
  39.2 15.0 %collective-permute-start.8 = (bf16[20,128,128]{2,1,0:T(8,128)(2,1)S(1)}, bf16[20,128,128]{2,1,0:T(8,128)(2,1)S(1)}, u32[]{:S(2)}, u32[]{:S(2)}) collective-permute-start(bf16[20,128,128]{2,1,0:T(8,128)(2,1)S(1)} %collective-permute-done.3), channel_id=1, source_target_pairs={{0,1},{1,0},{2,3},{3,2},{4,5},{5,4},{6,7},{7,6},{8,9},{9,8},{10,11... | collective-permute-start | bytes 1966088 | tf_op jit(solution)/shard_map/ppermute | solution.py:63
  47.7 4.8 %collective-permute-start.6 = (bf16[10,128,128]{2,1,0:T(8,128)(2,1)S(1)}, bf16[10,128,128]{2,1,0:T(8,128)(2,1)S(1)}, u32[]{:S(2)}, u32[]{:S(2)}) collective-permute-start(bf16[10,128,128]{2,1,0:T(8,128)(2,1)S(1)} %collective-permute-done.4), channel_id=1, source_target_pairs={{0,1},{1,0},{2,3},{3,2},{4,5},{5,4},{6,7},{7,6},{8,9},{9,8},{10,11... | collective-permute-start | bytes 983048 | tf_op jit(solution)/shard_map/ppermute | solution.py:63
  52.3 1.6 %collective-permute-start.7 = (bf16[10,128,128]{2,1,0:T(8,128)(2,1)S(1)}, bf16[10,128,128]{2,1,0:T(8,128)(2,1)S(1)}, u32[]{:S(2)}, u32[]{:S(2)}) collective-permute-start(bf16[10,128,128]{2,1,0:T(8,128)(2,1)S(1)} %collective-permute-done.5), channel_id=1, source_target_pairs={{0,1},{1,0},{2,3},{3,2},{4,5},{5,4},{6,7},{7,6},{8,9},{9,8},{10,11... | collective-permute-start | bytes 983048 | tf_op jit(solution)/shard_map/ppermute | solution.py:63
  54.3 2.3 %copy-start = (bf16[8,20,128,128]{3,2,1,0:T(8,128)(2,1)}, bf16[8,20,128,128]{3,2,1,0:T(8,128)(2,1)S(1)}, u32[]{:S(2)}) copy-start(bf16[8,20,128,128]{3,2,1,0:T(8,128)(2,1)S(1)} %bitcast_dynamic-update-slice_fusion.envs) | copy-start | bytes 15728644
  80.1 7.9 %copy-start.3 = (bf16[4,16,32,128]{3,2,1,0:T(8,128)(2,1)S(1)}, bf16[4,16,32,128]{3,2,1,0:T(8,128)(2,1)}, u32[]{:S(2)}) copy-start(bf16[4,16,32,128]{3,2,1,0:T(8,128)(2,1)} %shard_map.73) | copy-start | bytes 1572868
  80.1 11.5 %copy-start.2 = (bf16[4,16,32,128]{3,2,1,0:T(8,128)(2,1)S(1)}, bf16[4,16,32,128]{3,2,1,0:T(8,128)(2,1)}, u32[]{:S(2)}) copy-start(bf16[4,16,32,128]{3,2,1,0:T(8,128)(2,1)} %shard_map.74) | copy-start | bytes 1572868
  80.1 14.6 %copy-start.1 = (bf16[4,16,32,128]{3,2,1,0:T(8,128)(2,1)S(1)}, bf16[4,16,32,128]{3,2,1,0:T(8,128)(2,1)}, u32[]{:S(2)}) copy-start(bf16[4,16,32,128]{3,2,1,0:T(8,128)(2,1)} %shard_map.75) | copy-start | bytes 1572868
  88.0 8.9 %collective-permute-start.10 = (bf16[16,32,128]{2,1,0:T(8,128)(2,1)S(1)}, bf16[16,32,128]{2,1,0:T(8,128)(2,1)S(1)}, u32[]{:S(2)}, u32[]{:S(2)}) collective-permute-start(bf16[16,32,128]{2,1,0:T(8,128)(2,1)S(1)} %get-tuple-element.7), channel_id=1, source_target_pairs={{0,16},{8,24},{16,0},{24,8},{1,17},{9,25},{17,1},{25,9},{2,18},{10... | collective-permute-start | bytes 393224 | tf_op jit(solution)/shard_map/ppermute | solution.py:99
  89.6 10.1 %collective-permute-start.11 = (bf16[16,32,128]{2,1,0:T(8,128)(2,1)S(1)}, bf16[16,32,128]{2,1,0:T(8,128)(2,1)S(1)}, u32[]{:S(2)}, u32[]{:S(2)}) collective-permute-start(bf16[16,32,128]{2,1,0:T(8,128)(2,1)S(1)} %get-tuple-element.6), channel_id=1, source_target_pairs={{0,24},{8,16},{16,8},{24,0},{1,25},{9,17},{17,9},{25,1},{2,26},{10... | collective-permute-start | bytes 393224 | tf_op jit(solution)/shard_map/ppermute | solution.py:99
  91.0 9.2 %collective-permute-start.9 = (bf16[16,32,128]{2,1,0:T(8,128)(2,1)S(1)}, bf16[16,32,128]{2,1,0:T(8,128)(2,1)S(1)}, u32[]{:S(2)}, u32[]{:S(2)}) collective-permute-start(bf16[16,32,128]{2,1,0:T(8,128)(2,1)S(1)} %get-tuple-element.5), channel_id=1, source_target_pairs={{0,8},{8,0},{16,24},{24,16},{1,9},{9,1},{17,25},{25,17},{2,10},{10... | collective-permute-start | bytes 393224 | tf_op jit(solution)/shard_map/ppermute | solution.py:99
  91.6 9.9 %collective-permute-start.12 = (bf16[16,32,128]{2,1,0:T(8,128)(2,1)S(1)}, bf16[16,32,128]{2,1,0:T(8,128)(2,1)S(1)}, u32[]{:S(2)}, u32[]{:S(2)}) collective-permute-start(bf16[16,32,128]{2,1,0:T(8,128)(2,1)S(1)} %get-tuple-element.8), channel_id=1, source_target_pairs={{0,8},{8,0},{16,24},{24,16},{1,9},{9,1},{17,25},{25,17},{2,10},{10... | collective-permute-start | bytes 393224 | tf_op jit(solution)/shard_map/ppermute | solution.py:99
  93.1 10.8 %collective-permute-start.13 = (bf16[16,32,128]{2,1,0:T(8,128)(2,1)S(1)}, bf16[16,32,128]{2,1,0:T(8,128)(2,1)S(1)}, u32[]{:S(2)}, u32[]{:S(2)}) collective-permute-start(bf16[16,32,128]{2,1,0:T(8,128)(2,1)S(1)} %get-tuple-element.10), channel_id=1, source_target_pairs={{0,16},{8,24},{16,0},{24,8},{1,17},{9,25},{17,1},{25,9},{2,18},{10... | collective-permute-start | bytes 393224 | tf_op jit(solution)/shard_map/ppermute | solution.py:99
  96.9 8.4 %collective-permute-start.14 = (bf16[16,32,128]{2,1,0:T(8,128)(2,1)S(1)}, bf16[16,32,128]{2,1,0:T(8,128)(2,1)S(1)}, u32[]{:S(2)}, u32[]{:S(2)}) collective-permute-start(bf16[16,32,128]{2,1,0:T(8,128)(2,1)S(1)} %get-tuple-element.9), channel_id=1, source_target_pairs={{0,24},{8,16},{16,8},{24,0},{1,25},{9,17},{17,9},{25,1},{2,26},{10... | collective-permute-start | bytes 393224 | tf_op jit(solution)/shard_map/ppermute | solution.py:99
  99.7 7.7 %collective-permute-start.15 = (bf16[16,32,128]{2,1,0:T(8,128)(2,1)S(1)}, bf16[16,32,128]{2,1,0:T(8,128)(2,1)S(1)}, u32[]{:S(2)}, u32[]{:S(2)}) collective-permute-start(bf16[16,32,128]{2,1,0:T(8,128)(2,1)S(1)} %get-tuple-element.11), channel_id=1, source_target_pairs={{0,8},{8,0},{16,24},{24,16},{1,9},{9,1},{17,25},{25,17},{2,10},{10... | collective-permute-start | bytes 393224 | tf_op jit(solution)/shard_map/ppermute | solution.py:99
  100.2 9.4 %collective-permute-start.16 = (bf16[16,32,128]{2,1,0:T(8,128)(2,1)S(1)}, bf16[16,32,128]{2,1,0:T(8,128)(2,1)S(1)}, u32[]{:S(2)}, u32[]{:S(2)}) collective-permute-start(bf16[16,32,128]{2,1,0:T(8,128)(2,1)S(1)} %get-tuple-element.13), channel_id=1, source_target_pairs={{0,16},{8,24},{16,0},{24,8},{1,17},{9,25},{17,1},{25,9},{2,18},{10... | collective-permute-start | bytes 393224 | tf_op jit(solution)/shard_map/ppermute | solution.py:99
  101.5 9.4 %collective-permute-start.17 = (bf16[16,32,128]{2,1,0:T(8,128)(2,1)S(1)}, bf16[16,32,128]{2,1,0:T(8,128)(2,1)S(1)}, u32[]{:S(2)}, u32[]{:S(2)}) collective-permute-start(bf16[16,32,128]{2,1,0:T(8,128)(2,1)S(1)} %get-tuple-element.12), channel_id=1, source_target_pairs={{0,24},{8,16},{16,8},{24,0},{1,25},{9,17},{17,9},{25,1},{2,26},{10... | collective-permute-start | bytes 393224 | tf_op jit(solution)/shard_map/ppermute | solution.py:99
  104.0 9.1 %collective-permute-start.18 = (bf16[16,32,128]{2,1,0:T(8,128)(2,1)S(1)}, bf16[16,32,128]{2,1,0:T(8,128)(2,1)S(1)}, u32[]{:S(2)}, u32[]{:S(2)}) collective-permute-start(bf16[16,32,128]{2,1,0:T(8,128)(2,1)S(1)} %get-tuple-element.14), channel_id=1, source_target_pairs={{0,8},{8,0},{16,24},{24,16},{1,9},{9,1},{17,25},{25,17},{2,10},{10... | collective-permute-start | bytes 393224 | tf_op jit(solution)/shard_map/ppermute | solution.py:99
  105.3 7.7 %collective-permute-start.19 = (bf16[16,32,128]{2,1,0:T(8,128)(2,1)S(1)}, bf16[16,32,128]{2,1,0:T(8,128)(2,1)S(1)}, u32[]{:S(2)}, u32[]{:S(2)}) collective-permute-start(bf16[16,32,128]{2,1,0:T(8,128)(2,1)S(1)} %get-tuple-element.16), channel_id=1, source_target_pairs={{0,16},{8,24},{16,0},{24,8},{1,17},{9,25},{17,1},{25,9},{2,18},{10... | collective-permute-start | bytes 393224 | tf_op jit(solution)/shard_map/ppermute | solution.py:99
  107.4 8.0 %collective-permute-start.20 = (bf16[16,32,128]{2,1,0:T(8,128)(2,1)S(1)}, bf16[16,32,128]{2,1,0:T(8,128)(2,1)S(1)}, u32[]{:S(2)}, u32[]{:S(2)}) collective-permute-start(bf16[16,32,128]{2,1,0:T(8,128)(2,1)S(1)} %get-tuple-element.15), channel_id=1, source_target_pairs={{0,24},{8,16},{16,8},{24,0},{1,25},{9,17},{17,9},{25,1},{2,26},{10... | collective-permute-start | bytes 393224 | tf_op jit(solution)/shard_map/ppermute | solution.py:99

commit v2 on v1

v2 whole, which is shorter than its diff:
```python
import functools

import jax
import jax.numpy as jnp
from jax import lax
from jax.experimental import pallas as pl
from jax.experimental.pallas import tpu as pltpu
from jax.sharding import PartitionSpec as P

CORES = 2
STACK = 4
SPLIT = 2
UNROLL = 6
NO_COST = pl.CostEstimate(flops=0, bytes_accessed=0, transcendentals=0)
SMEM = pl.BlockSpec(memory_space=pltpu.SMEM)
VMEM = pl.BlockSpec(memory_space=pltpu.VMEM)


def padded(n):
    return (n + UNROLL - 1) // UNROLL * UNROLL


class Lists:
    def __init__(self, blocks, sectors):
        used = min(sectors, blocks)
        self.blocks = blocks
        self.pairs = padded((blocks + used) // 2)
        self.groups = padded(min(blocks, (blocks + (STACK - 1) * used) // STACK))
        self.pair_slot = 2
        self.pair_pos = self.pair_slot + self.pairs
        self.group_slot = self.pair_pos + 2 * self.pairs
        self.group_start = self.group_slot + self.groups
        self.group_block = self.group_start + self.groups
        self.length = self.group_block + STACK * self.groups


def cut_kernel(groups, place, left, right, out):
    channels, width, rows = right.shape[0], right.shape[1], out.shape[1]
    for q in range(width // rows):
        for w in range(channels):
            out[w * (width // rows) + q] = right[w, q * rows:(q + 1) * rows, :]
    base = channels * (width // rows)
    for group in groups:
        for i, d in enumerate(group):
            start = pl.multiple_of((place[2] ^ d) * rows, rows)
            for w in range(channels):
                out[base + w * len(group) + i] = left[w, pl.ds(start, rows), :]
        base = base + channels * len(group)


def order_kernel(
    chips, at, place, lsec, rsec, owner, live, psi, lists, halves, lcount, rcount, lbase, rbase, rfirst, lrank, rrank, origin
):
    width = psi.shape[1]
    sectors = owner.shape[0]
    chip, core = place[0], place[1]
    row = lax.broadcasted_iota(jnp.int32, (width, width), 0)
    col = lax.broadcasted_iota(jnp.int32, (width, width), 1)
    zero = jnp.int32(0)

    def slot_of(sector):
        where = owner[sector]
        away = lax.rem(where // CORES - chip + chips, chips)
        return away * CORES + lax.rem(where + core, CORES)

    for part in range(SPLIT):
        base = part * at.length
        start = part * at.blocks

        def clear_sector(s, carry):
            lcount[s] = 0
            rcount[s] = 0
            return carry

        def clear_pair(p, carry):
            lists[base + at.pair_slot + p] = 0
            for h in range(2):
                lists[base + at.pair_pos + 2 * p + h] = at.blocks
                origin[2 * p + h] = 0
            return carry

        def clear_group(g, carry):
            lists[base + at.group_slot + g] = 0
            lists[base + at.group_start + g] = 0
            for j in range(STACK):
                lists[base + at.group_block + STACK * g + j] = at.blocks
            return carry

        def count(k, carry):
            left, right = lsec[start + k], rsec[start + k]
            lrank[k] = lcount[left]
            rrank[k] = rcount[right]
            lcount[left] = lcount[left] + 1
            rcount[right] = rcount[right] + 1
            return carry

        def bases(s, carry):
            pair, group, first = carry
            lbase[s] = pair
            rbase[s] = group
            rfirst[s] = first
            return pair + (lcount[s] + 1) // 2, group + (rcount[s] + STACK - 1) // STACK, first + rcount[s]

        def enter(k, carry):
            left, right = lsec[start + k], rsec[start + k]
            lr, rr = lrank[k], rrank[k]
            position = rfirst[right] + rr
            place_in = lax.rem(rr, STACK)
            group = rbase[right] + rr // STACK
            lists[base + at.group_slot + group] = slot_of(right)
            lists[base + at.group_start + group] = position - place_in
            lists[base + at.group_block + STACK * group + place_in] = k
            pair = lbase[left] + lr // 2
            lists[base + at.pair_slot + pair] = slot_of(left)
            lists[base + at.pair_pos + 2 * pair + lax.rem(lr, 2)] = position
            origin[2 * pair + lax.rem(lr, 2)] = k
            return carry

        lax.fori_loop(0, sectors, clear_sector, 0)
        lax.fori_loop(0, at.pairs, clear_pair, 0)
        lax.fori_loop(0, at.groups, clear_group, 0)
        lax.fori_loop(0, at.blocks, count, 0)
        pairs, groups, _ = lax.fori_loop(0, sectors, bases, (zero, zero, zero))
        lists[base] = (pairs + UNROLL - 1) // UNROLL
        lists[base + 1] = (groups + UNROLL - 1) // UNROLL
        lax.fori_loop(0, at.blocks, enter, 0)

        def fill(p, carry):
            for h in range(2):
                k = start + origin[2 * p + h]
                mask = (row < live[lsec[k]]) & (col < live[rsec[k]])
                block = psi[k]
                halves[part * at.pairs + p, :, h * width:(h + 1) * width] = jnp.where(mask, block, jnp.zeros_like(block))
            return carry

        lax.fori_loop(0, lists[base] * UNROLL, fill, 0)


def multiply_kernel(rows, first_chunk, parts, at, lists, halves, right, left, *rest):
    outs, inner = rest[:-1], rest[-1]
    width = halves.shape[1]
    span = inner.shape[1]
    channels = inner.shape[2] // width
    chunks = channels * span // rows
    spare = len(parts) * at.blocks

    for number, part in enumerate(parts):
        base = part * at.length

        def first(p):
            lmat = left[lists[base + at.pair_slot + p], first_chunk:first_chunk + chunks].reshape(channels * span, width)
            y = jnp.dot(lmat, halves[part * at.pairs + p], preferred_element_type=jnp.float32).astype(jnp.bfloat16)
            for h in range(2):
                where = lists[base + at.pair_pos + 2 * p + h]
                for w in range(channels):
                    inner[where, :, w * width:(w + 1) * width] = (
                        y[w * span:(w + 1) * span, h * width:(h + 1) * width]
                    )

        def second(g):
            rmat = right[lists[base + at.group_slot + g], 0:channels * width // rows].reshape(channels * width, width)
            stack = inner[pl.ds(lists[base + at.group_start + g], STACK)].reshape(STACK * span, channels * width)
            part_sum = jnp.dot(stack, rmat, preferred_element_type=jnp.float32).astype(jnp.bfloat16)
            for j in range(STACK):
                block = lists[base + at.group_block + STACK * g + j]
                block = jnp.where(block == at.blocks, spare, block + number * at.blocks)
                for i, out in enumerate(outs):
                    out[block] = part_sum[j * span + i * rows:j * span + (i + 1) * rows]

        def loop(step, trips):
            def body(i, carry):
                for u in range(UNROLL):
                    step(i * UNROLL + u)
                return carry

            lax.fori_loop(0, trips, body, 0)

        loop(first, lists[base])
        loop(second, lists[base + 1])


def sum_kernel(part, nenv, place, lsec, rsec, live, *rest):
    out, terms = rest[-1], rest[:nenv]
    blocks, rows, width = out.shape
    row = place[2] * rows + lax.broadcasted_iota(jnp.int32, (rows, width), 0)
    col = lax.broadcasted_iota(jnp.int32, (rows, width), 1)

    def body(k, carry):
        total = terms[0][k].astype(jnp.float32)
        for term in terms[1:]:
            total = total + term[k].astype(jnp.float32)
        mask = (row < live[lsec[part * blocks + k]]) & (col < live[rsec[part * blocks + k]])
        out[k] = jnp.where(mask, total, jnp.zeros_like(total)).astype(jnp.bfloat16)
        return carry

    lax.fori_loop(0, blocks, body, 0, unroll=8)


def on_device(psi, left_env, right_env, left_sector, right_sector, sector_owner, sector_rows):
    nwave = lax.axis_size("wave")
    nenv = lax.axis_size("env")
    count, width = psi.shape[0], psi.shape[1]
    channels = left_env.shape[0]
    sectors = sector_owner.shape[0]
    chips = nwave // CORES
    rows = width // nenv
    wave = lax.axis_index("wave")
    env = lax.axis_index("env")
    place = jnp.stack([wave // CORES, wave % CORES, env]).astype(jnp.int32)
    lsec, rsec = left_sector[:, 0], right_sector[:, 0]

    up = [(i, (i + CORES) % nwave) for i in range(nwave)]
    down = [((i + CORES) % nwave, i) for i in range(nwave)]
    other = [(i, i ^ 1) for i in range(nwave)]
    half = channels // 2
    swap = lambda x: lax.ppermute(x, "wave", other)

    def gate(*values):
        return lax.optimization_barrier(values)

    def ring(own):
        held = {0: own}
        rising = falling = own
        for r in range(1, (chips - 1) // 2 + 1):
            rising = lax.ppermute(rising, "wave", up)
            falling = lax.ppermute(falling, "wave", down)
            held[chips - r], held[r] = rising, falling
        return held, rising, falling

    def far(rising, falling, lo, hi):
        mid = (lo + hi) // 2
        return [lax.ppermute(rising[lo:mid], "wave", up), lax.ppermute(falling[mid:hi], "wave", down)]

    def stack(held, others, last, lo, hi):
        pieces = []
        for d in range(chips):
            if d in held:
                pieces += [held[d][lo:hi], others[d][lo:hi]]
            else:
                pieces += [jnp.concatenate(last), jnp.concatenate([swap(x) for x in last])]
        return jnp.stack(pieces)

    at = Lists(count // SPLIT, sectors)
    scratch = lambda n: pltpu.SMEM((n,), jnp.int32)
    lists, halves = pl.pallas_call(
        functools.partial(order_kernel, chips, at),
        out_shape=(
            jax.ShapeDtypeStruct((SPLIT * at.length,), jnp.int32),
            jax.ShapeDtypeStruct((SPLIT * at.pairs, width, 2 * width), jnp.bfloat16),
        ),
        in_specs=[SMEM] * 5 + [VMEM],
        out_specs=(SMEM, VMEM),
        scratch_shapes=[scratch(sectors)] * 5 + [scratch(at.blocks)] * 2 + [scratch(2 * at.pairs)],
    )(place, lsec, rsec, sector_owner, sector_rows, psi)

    def multiply(right, left, first_chunk, number, parts):
        span = number * rows
        blocks = len(parts) * at.blocks
        need = right.size + left.size + halves.size + (at.blocks + STACK) * span * channels * width
        need = 2 * (need + number * (blocks + 1) * rows * width) + (8 << 20)
        return pl.pallas_call(
            functools.partial(multiply_kernel, rows, first_chunk, parts, at),
            out_shape=[jax.ShapeDtypeStruct((blocks + 1, rows, width), jnp.bfloat16)] * number,
            in_specs=[SMEM] + [VMEM] * 3,
            out_specs=[VMEM] * number,
            scratch_shapes=[pltpu.VMEM((at.blocks + STACK, span, channels * width), jnp.bfloat16)],
            compiler_params=pltpu.CompilerParams(vmem_limit_bytes=min(need, 60 << 20)),
            cost_estimate=NO_COST,
        )(lists, halves, right, left)

    def send(x, d):
        return lax.ppermute(x[:-1], "env", [(i, i ^ d) for i in range(nenv)])

    lead, *rest = range(nenv - 1, 0, -1)
    everything = tuple(range(SPLIT))
    quarters = channels * nenv
    lead_end = quarters + channels
    rest_end = lead_end + channels * len(rest)
    end = rest_end + channels
    own = pl.pallas_call(
        functools.partial(cut_kernel, ([lead], rest, [0])),
        out_shape=jax.ShapeDtypeStruct((end, rows, width), jnp.bfloat16),
        in_specs=[SMEM, VMEM, VMEM],
        out_specs=VMEM,
    )(place, left_env[:, 0], right_env[:, 0])
    held, rising, falling = ring(own)
    others = {d: swap(x) for d, x in held.items()}
    last_one = far(rising, falling, 0, lead_end)
    last_two = far(rising, falling, lead_end, end)
    one = stack(held, others, last_one, 0, lead_end)
    two = stack(held, others, last_two, lead_end, end)
    here = [[] for _ in range(nenv)]
    for part in everything:
        (sums,) = multiply(one, one, quarters, 1, (part,))
        if part == SPLIT - 1:
            sums, two = gate(sums, two)
        here[lead].append(send(sums, lead))
    for part in everything:
        if part > 0:
            two, here[lead][part - 1] = gate(two, here[lead][part - 1])
        parts = multiply(one, two, 0, len(rest), (part,))
        if part == SPLIT - 1:
            *parts, two = gate(*parts, two)
        for x, d in zip(parts, rest):
            here[d].append(send(x, d))
    for part in everything:
        for d in [lead] if part == 0 else rest:
            at_part = SPLIT - 1 if part == 0 else part - 1
            two, here[d][at_part] = gate(two, here[d][at_part])
        here[0].append(multiply(one, two, rest_end - lead_end, 1, (part,))[0])

    out_shape = jax.ShapeDtypeStruct((count, rows, width), jnp.bfloat16)
    total = None
    for part in everything:
        args = [place, lsec, rsec, sector_rows] + [here[d][part] for d in range(nenv)]
        specs = [SMEM] * 4 + [VMEM] * nenv
        alias = {}
        if total is not None:
            alias = {len(args): 0}
            args.append(total)
            specs.append(pl.BlockSpec(memory_space=pl.ANY))
        total = pl.pallas_call(
            functools.partial(sum_kernel, part, nenv),
            grid=(1,),
            out_shape=out_shape,
            in_specs=specs,
            out_specs=pl.BlockSpec((at.blocks, rows, width), lambda i, part=part: (part, 0, 0)),
            input_output_aliases=alias,
        )(*args)
    return total


def solution(mesh):
    return jax.shard_map(
        on_device,
        mesh=mesh,
        in_specs=(
            P("wave", None, None),
            P("env", "wave", None, None),
            P("env", "wave", None, None),
            P("wave", None),
            P("wave", None),
            P(),
            P(),
        ),
        out_specs=P("wave", "env", None),
        check_vma=False,
    )
```

time: 117 us -> 93.5 us (0.80); the launches traced: 117 us -> 92.3 us
  waiting for transfers between devices: 51.5 us -> 15.7 us
  Pallas kernels: 31.3 us -> 40.5 us
  starting transfers between devices: 25.1 us -> 29.5 us
  other arithmetic: 5.17 us -> 0.8 us
  local copies, waits for them, and re-layouts: 4.03 us -> 5.43 us
    ppermute x16 -> x12, waiting for transfers between devices: 50.1 us -> 14.6 us  [the longest x2 8.48 us: far(): lax.ppermute(falling[mid:hi], 'wave', down)]
    pallas_call x4 -> x10, Pallas kernels: 31.3 us -> 40.5 us  [the longest x6 24.8 us: multiply(): pl.pallas_call(functools.partial(multiply_kernel, rows, first_chunk, part...]
    ppermute x16 -> x12, starting transfers between devices: 25.1 us -> 28.5 us  [the longest x2 13.5 us: far(): lax.ppermute(rising[lo:mid], 'wave', up)]
    unnamed x12 -> x30, local copies, waits for them, and re-layouts: 2.74 us -> 5.18 us
    concatenate x2 -> x0, other arithmetic: 1.99 us -> none  [the longest x1 1.13 us: on_device(): own = jnp.concatenate([left_env[:, 0], right_env[:, 0]], axis=0)]
    convert_element_type x4 -> x0, other arithmetic: 1.19 us -> none  [on_device(): results.append(total.astype(jnp.bfloat16))]
  transfers between devices with their start and end apart: 21 -> 19, of which waited for: 12 -> 6; matrix products, arithmetic and copies ran while one was open for 3% -> 3% of each run, Pallas kernels for 0% -> 39%
where the time goes in v2:
time: 93.5 us; the launch traced here: 92.3 us
  Pallas kernels  40.5 us (43%)
  starting transfers between devices  29.5 us (32%)
  waiting for transfers between devices  15.7 us (17%)
  local copies, waits for them, and re-layouts  5.43 us (6%)
    pallas_call x6, Pallas kernels, multiply(): pl.pallas_call(functools.partial(multiply_kernel, rows, first_chunk, part...  24.8 us
    ppermute x2, starting transfers between devices, far(): lax.ppermute(rising[lo:mid], 'wave', up)  13.5 us
    pallas_call x1, Pallas kernels, on_device(): pl.pallas_call(functools.partial(order_kernel, chips, at), out_shape=(jax...  9.48 us
    ppermute x2, waiting for transfers between devices, far(): lax.ppermute(falling[mid:hi], 'wave', down)  8.48 us
    ppermute x6, starting transfers between devices, send(): return lax.ppermute(x[:-1], 'env', [(i, i ^ d) for i in range(nenv)])  7.24 us
    unnamed x30, local copies, waits for them, and re-layouts  5.18 us
    ppermute x1, waiting for transfers between devices, ring(): rising = lax.ppermute(rising, 'wave', up)  4.32 us
    pallas_call x2, Pallas kernels, on_device(): pl.pallas_call(functools.partial(sum_kernel, part, nenv), grid=(1,), out_...  4.24 us
  transfers between devices with their start and end apart: 19, of which 6 were waited for; matrix products, arithmetic and copies ran while one was open for 3% of the time, Pallas kernels for 39%

profile of v2, /device:TPU:0, one launch (start us, length us, event | category | flops | bytes accessed | tf_op | source)
XLA Modules:
  0.0 92.3 jit_solution(1343219198263884248)
XLA Ops:
  0.0 0.6 pad_add_fusion.place
  0.6 2.0 %shard_map.74 = bf16[80,32,128]{2,1,0:T(8,128)(2,1)} custom-call(s32[3]{0:T(128)} %pad_add_fusion.place, bf16[10,128,128]{2,1,0:T(8,128)(2,1)} %bitcast.71, bf16[10,128,128]{2,1,0:T(8,128)(2,1)} %bitcast.72), custom_call_target="tpu_custom_call" | custom-call | tf_op jit(solution)/shard_map/pallas_call | solution.py:280
  2.6 3.0 %collective-permute-start.3 = (bf16[80,32,128]{2,1,0:T(8,128)(2,1)}, bf16[80,32,128]{2,1,0:T(8,128)(2,1)S(1)}, u32[]{:S(2)}, u32[]{:S(2)}) collective-permute-start(bf16[80,32,128]{2,1,0:T(8,128)(2,1)} %shard_map.74), channel_id=1, source_target_pairs={{0,2},{1,3},{2,4},{3,5},{4,6},{5,7},{6,0},{7,1},{8,10},{9,11},{10,... | collective-permute-start | bytes 1966088 | tf_op jit(solution)/shard_map/ppermute | solution.py:225
  5.6 2.0 %collective-permute-start.1 = (bf16[80,32,128]{2,1,0:T(8,128)(2,1)}, bf16[80,32,128]{2,1,0:T(8,128)(2,1)S(1)}, u32[]{:S(2)}, u32[]{:S(2)}) collective-permute-start(bf16[80,32,128]{2,1,0:T(8,128)(2,1)} %shard_map.74), channel_id=1, source_target_pairs={{2,0},{3,1},{4,2},{5,3},{6,4},{7,5},{0,6},{1,7},{10,8},{11,9},{12,... | collective-permute-start | bytes 1966088 | tf_op jit(solution)/shard_map/ppermute | solution.py:226
  7.6 0.0 collective-permute-start
  7.6 9.5 %shard_map.73 = (s32[364]{0:T(512)}, bf16[48,128,256]{2,1,0:T(8,128)(2,1)}) custom-call(s32[3]{0:T(128)} %pad_add_fusion.place, s32[64]{0:T(128)} %bitcast.73, s32[64]{0:T(128)} %bitcast.76, s32[8]{0:T(128)} %owner.1, s32[8]{0:T(128)} %live.5, bf16[64,128,128]{2,1,0:T(8,128)(2,1)} %psi.1), custom_call_target="tpu_custom_call" | custom-call | tf_op jit(solution)/shard_map/pallas_call | solution.py:245
  17.1 1.0 %fusion.13 = bf16[8,30,32,128]{3,2,1,0:T(8,128)(2,1)S(1)} fusion(bf16[80,32,128]{2,1,0:T(8,128)(2,1)} %shard_map.74), kind=kLoop, calls=%fused_computation.27 | loop fusion | bytes 491520
  18.1 1.0 %fusion.5 = bf16[8,50,32,128]{3,2,1,0:T(8,128)(2,1)S(1)} fusion(bf16[80,32,128]{2,1,0:T(8,128)(2,1)} %shard_map.74), kind=kLoop, calls=%fused_computation.11 | loop fusion | bytes 819200
  19.1 4.3 %collective-permute-done.3 = bf16[80,32,128]{2,1,0:T(8,128)(2,1)S(1)} collective-permute-done((bf16[80,32,128]{2,1,0:T(8,128)(2,1)}, bf16[80,32,128]{2,1,0:T(8,128)(2,1)S(1)}, u32[]{:S(2)}, u32[]{:S(2)}) %collective-permute-start.3) | collective-permute-done | bytes 655392 | tf_op jit(solution)/shard_map/ppermute | solution.py:225
  23.5 0.1 collective-permute-start.9
  23.5 13.4 %collective-permute-start.4 = (bf16[25,32,128]{2,1,0:T(8,128)(2,1)S(1)}, bf16[25,32,128]{2,1,0:T(8,128)(2,1)S(1)}, u32[]{:S(2)}, u32[]{:S(2)}) collective-permute-start(bf16[25,32,128]{2,1,0:T(8,128)(2,1)S(1)} %slice.92), channel_id=1, source_target_pairs={{0,2},{1,3},{2,4},{3,5},{4,6},{5,7},{6,0},{7,1},{8,10},{9,11},{10,... | collective-permute-start | bytes 614408 | tf_op jit(solution)/shard_map/ppermute | solution.py:232
  37.0 2.4 %collective-permute-start.10 = (bf16[15,32,128]{2,1,0:T(8,128)(2,1)S(1)}, bf16[15,32,128]{2,1,0:T(8,128)(2,1)S(1)}, u32[]{:S(2)}, u32[]{:S(2)}) collective-permute-start(bf16[15,32,128]{2,1,0:T(8,128)(2,1)S(1)} %slice.101), channel_id=1, source_target_pairs={{2,0},{3,1},{4,2},{5,3},{6,4},{7,5},{0,6},{1,7},{10,8},{11,9},{12,... | collective-permute-start | bytes 368648 | tf_op jit(solution)/shard_map/ppermute | solution.py:232
  39.4 0.3 collective-permute-start.5
  39.7 0.1 fusion.4
  39.8 0.0 copy-start.3
  39.8 0.1 fusion.3
  40.0 1.7 %collective-permute-done.9 = bf16[15,32,128]{2,1,0:T(8,128)(2,1)S(1)} collective-permute-done((bf16[15,32,128]{2,1,0:T(8,128)(2,1)S(1)}, bf16[15,32,128]{2,1,0:T(8,128)(2,1)S(1)}, u32[]{:S(2)}, u32[]{:S(2)}) %collective-permute-start.9) | collective-permute-done | bytes 122912 | tf_op jit(solution)/shard_map/ppermute | solution.py:232
  41.7 4.7 %collective-permute-done.10 = bf16[15,32,128]{2,1,0:T(8,128)(2,1)S(1)} collective-permute-done((bf16[15,32,128]{2,1,0:T(8,128)(2,1)S(1)}, bf16[15,32,128]{2,1,0:T(8,128)(2,1)S(1)}, u32[]{:S(2)}, u32[]{:S(2)}) %collective-permute-start.10) | collective-permute-done | bytes 122912 | tf_op jit(solution)/shard_map/ppermute | solution.py:232
  46.4 0.0 collective-permute-start.11
  46.4 0.5 collective-permute-start.12
  46.9 3.8 %collective-permute-done.5 = bf16[25,32,128]{2,1,0:T(8,128)(2,1)S(1)} collective-permute-done((bf16[25,32,128]{2,1,0:T(8,128)(2,1)S(1)}, bf16[25,32,128]{2,1,0:T(8,128)(2,1)S(1)}, u32[]{:S(2)}, u32[]{:S(2)}) %collective-permute-start.5) | collective-permute-done | bytes 204832 | tf_op jit(solution)/shard_map/ppermute | solution.py:232
  50.7 0.0 collective-permute-start.6
  50.7 0.5 collective-permute-start.7
  51.2 0.1 fusion.2
  51.3 0.1 fusion.6
  51.3 0.8 collective-permute-done.6
  52.2 0.3 collective-permute-done.7
  52.4 0.1 fusion.7
  52.5 0.1 fusion.1
  52.6 0.1 fusion.right.left
  52.7 3.4 %shard_map.76 = bf16[33,32,128]{2,1,0:T(8,128)(2,1)S(1)} custom-call(s32[364]{0:T(512)S(1)} %copy-done.3, bf16[48,128,256]{2,1,0:T(8,128)(2,1)S(1)} %copy-done, bf16[8,50,32,128]{3,2,1,0:T(8,128)(2,1)S(1)} %fusion.right.left, bf16[8,50,32,128]{3,2,1,0:T(8,128)(2,1)S(1)} %fusion.right.left), custom_call_target="tpu_custom_call" | custom-call | tf_op jit(solution)/shard_map/pallas_call | solution.py:261
  56.1 2.5 %collective-permute-start.13 = (bf16[32,32,128]{2,1,0:T(8,128)(2,1)S(1)}, bf16[32,32,128]{2,1,0:T(8,128)(2,1)S(1)}, u32[]{:S(2)}, u32[]{:S(2)}) collective-permute-start(bf16[32,32,128]{2,1,0:T(8,128)(2,1)S(1)} %slice.104), channel_id=1, source_target_pairs={{0,24},{8,16},{16,8},{24,0},{1,25},{9,17},{17,9},{25,1},{2,26},{10... | collective-permute-start | bytes 786440 | tf_op jit(solution)/shard_map/ppermute | solution.py:272
  58.8 3.4 %shard_map.75 = bf16[33,32,128]{2,1,0:T(8,128)(2,1)S(1)} custom-call(s32[364]{0:T(512)S(1)} %copy-done.3, bf16[48,128,256]{2,1,0:T(8,128)(2,1)S(1)} %copy-done, bf16[8,50,32,128]{3,2,1,0:T(8,128)(2,1)S(1)} %fusion.right.left, bf16[8,50,32,128]{3,2,1,0:T(8,128)(2,1)S(1)} %fusion.right.left), custom_call_target="tpu_custom_call" | custom-call | tf_op jit(solution)/shard_map/pallas_call | solution.py:261
  62.3 0.5 collective-permute-start.14
  62.8 5.6 %shard_map.78 = (bf16[33,32,128]{2,1,0:T(8,128)(2,1)S(1)}, bf16[33,32,128]{2,1,0:T(8,128)(2,1)S(1)}) custom-call(s32[364]{0:T(512)S(1)} %copy-done.3, bf16[48,128,256]{2,1,0:T(8,128)(2,1)S(1)} %copy-done, bf16[8,50,32,128]{3,2,1,0:T(8,128)(2,1)S(1)} %fusion.right.left, bf16[8,30,32,128]{3,2,1,0:T(8,128)(2,1)S(1)} %fusion.8.left), custom_call_target="tpu_custom_call" | custom-call | tf_op jit(solution)/shard_map/pallas_call | solution.py:261
  68.5 1.6 %collective-permute-start.16 = (bf16[32,32,128]{2,1,0:T(8,128)(2,1)S(1)}, bf16[32,32,128]{2,1,0:T(8,128)(2,1)S(1)}, u32[]{:S(2)}, u32[]{:S(2)}) collective-permute-start(bf16[32,32,128]{2,1,0:T(8,128)(2,1)S(1)} %slice.85), channel_id=1, source_target_pairs={{0,8},{8,0},{16,24},{24,16},{1,9},{9,1},{17,25},{25,17},{2,10},{10... | collective-permute-start | bytes 786440 | tf_op jit(solution)/shard_map/ppermute | solution.py:272
  70.0 1.5 %collective-permute-start.15 = (bf16[32,32,128]{2,1,0:T(8,128)(2,1)S(1)}, bf16[32,32,128]{2,1,0:T(8,128)(2,1)S(1)}, u32[]{:S(2)}, u32[]{:S(2)}) collective-permute-start(bf16[32,32,128]{2,1,0:T(8,128)(2,1)S(1)} %slice.84), channel_id=1, source_target_pairs={{0,16},{8,24},{16,0},{24,8},{1,17},{9,25},{17,1},{25,9},{2,18},{10... | collective-permute-start | bytes 786440 | tf_op jit(solution)/shard_map/ppermute | solution.py:272
  71.6 5.6 %shard_map.77 = (bf16[33,32,128]{2,1,0:T(8,128)(2,1)S(1)}, bf16[33,32,128]{2,1,0:T(8,128)(2,1)S(1)}) custom-call(s32[364]{0:T(512)S(1)} %copy-done.3, bf16[48,128,256]{2,1,0:T(8,128)(2,1)S(1)} %copy-done, bf16[8,50,32,128]{3,2,1,0:T(8,128)(2,1)S(1)} %fusion.right.left, bf16[8,30,32,128]{3,2,1,0:T(8,128)(2,1)S(1)} %fusion.8.left), custom_call_target="tpu_custom_call" | custom-call | tf_op jit(solution)/shard_map/pallas_call | solution.py:261
  77.2 0.6 collective-permute-start.18
  77.8 0.5 collective-permute-start.17
  78.4 3.4 %shard_map.80.rest_0_ = bf16[33,32,128]{2,1,0:T(8,128)(2,1)S(1)} custom-call(s32[364]{0:T(512)S(1)} %copy-done.3, bf16[48,128,256]{2,1,0:T(8,128)(2,1)S(1)} %copy-done, bf16[8,50,32,128]{3,2,1,0:T(8,128)(2,1)S(1)} %fusion.right.left, bf16[8,30,32,128]{3,2,1,0:T(8,128)(2,1)S(1)} %fusion.8.left), custom_call_target="tpu_custom_call" | custom-call | tf_op jit(solution)/shard_map/pallas_call | solution.py:261
  81.8 0.7 copy-done.2
  82.5 3.4 %shard_map.79.rest_0_ = bf16[33,32,128]{2,1,0:T(8,128)(2,1)S(1)} custom-call(s32[364]{0:T(512)S(1)} %copy-done.3, bf16[48,128,256]{2,1,0:T(8,128)(2,1)S(1)} %copy-done, bf16[8,50,32,128]{3,2,1,0:T(8,128)(2,1)S(1)} %fusion.right.left, bf16[8,30,32,128]{3,2,1,0:T(8,128)(2,1)S(1)} %fusion.8.left), custom_call_target="tpu_custom_call" | custom-call | tf_op jit(solution)/shard_map/pallas_call | solution.py:261
  85.9 0.7 copy-done.1
  86.6 2.1 %shard_map.81.rest_4_ = bf16[64,32,128]{2,1,0:T(8,128)(2,1)} custom-call(s32[3]{0:T(128)} %pad_add_fusion.place, s32[64]{0:T(128)} %bitcast.74, s32[64]{0:T(128)} %bitcast.77, s32[8]{0:T(128)} %live.5, bf16[33,32,128]{2,1,0:T(8,128)(2,1)} %copy-done.2, bf16[32,32,128]{2,1,0:T(8,128)(2,1)} %copy-done.8, bf16[32,32,128]{2,1,0:T(8,128)(2,1)} %copy-done.9, ...), custom_call_target="tpu_custom_call" | custom-call | tf_op jit(solution)/shard_map/pallas_call | solution.py:322
  88.8 0.7 copy-done.5
  89.5 0.7 copy-done.6
  90.2 2.1 %shard_map.82 = bf16[64,32,128]{2,1,0:T(8,128)(2,1)} custom-call(s32[3]{0:T(128)} %pad_add_fusion.place, s32[64]{0:T(128)} %bitcast.75, s32[64]{0:T(128)} %bitcast.78, s32[8]{0:T(128)} %live.5, bf16[33,32,128]{2,1,0:T(8,128)(2,1)} %copy-done.1, bf16[32,32,128]{2,1,0:T(8,128)(2,1)} %copy-done.6, ...), custom_call_target="tpu_custom_call", output_to_operand_aliasing={{}: (8, {})} | custom-call | tf_op jit(solution)/shard_map/pallas_call | solution.py:322
  (47 shorter events, 0.5 us)
Async XLA Ops:
  2.6 20.9 %collective-permute-start.3 = (bf16[80,32,128]{2,1,0:T(8,128)(2,1)}, bf16[80,32,128]{2,1,0:T(8,128)(2,1)S(1)}, u32[]{:S(2)}, u32[]{:S(2)}) collective-permute-start(bf16[80,32,128]{2,1,0:T(8,128)(2,1)} %shard_map.74), channel_id=1, source_target_pairs={{0,2},{1,3},{2,4},{3,5},{4,6},{5,7},{6,0},{7,1},{8,10},{9,11},{10,... | collective-permute-start | bytes 1966088 | tf_op jit(solution)/shard_map/ppermute | solution.py:225
  5.6 31.3 %collective-permute-start.1 = (bf16[80,32,128]{2,1,0:T(8,128)(2,1)}, bf16[80,32,128]{2,1,0:T(8,128)(2,1)S(1)}, u32[]{:S(2)}, u32[]{:S(2)}) collective-permute-start(bf16[80,32,128]{2,1,0:T(8,128)(2,1)} %shard_map.74), channel_id=1, source_target_pairs={{2,0},{3,1},{4,2},{5,3},{6,4},{7,5},{0,6},{1,7},{10,8},{11,9},{12,... | collective-permute-start | bytes 1966088 | tf_op jit(solution)/shard_map/ppermute | solution.py:226
  7.6 32.1 %collective-permute-start = (bf16[80,32,128]{2,1,0:T(8,128)(2,1)}, bf16[80,32,128]{2,1,0:T(8,128)(2,1)S(1)}, u32[]{:S(2)}, u32[]{:S(2)}) collective-permute-start(bf16[80,32,128]{2,1,0:T(8,128)(2,1)} %shard_map.74), channel_id=1, source_target_pairs={{0,1},{1,0},{2,3},{3,2},{4,5},{5,4},{6,7},{7,6},{8,9},{9,8},{10,11... | collective-permute-start | bytes 1966088 | tf_op jit(solution)/shard_map/ppermute | solution.py:216
  23.5 18.2 %collective-permute-start.9 = (bf16[15,32,128]{2,1,0:T(8,128)(2,1)S(1)}, bf16[15,32,128]{2,1,0:T(8,128)(2,1)S(1)}, u32[]{:S(2)}, u32[]{:S(2)}) collective-permute-start(bf16[15,32,128]{2,1,0:T(8,128)(2,1)S(1)} %slice.100), channel_id=1, source_target_pairs={{0,2},{1,3},{2,4},{3,5},{4,6},{5,7},{6,0},{7,1},{8,10},{9,11},{10,... | collective-permute-start | bytes 368648 | tf_op jit(solution)/shard_map/ppermute | solution.py:232
  23.5 22.9 %collective-permute-start.4 = (bf16[25,32,128]{2,1,0:T(8,128)(2,1)S(1)}, bf16[25,32,128]{2,1,0:T(8,128)(2,1)S(1)}, u32[]{:S(2)}, u32[]{:S(2)}) collective-permute-start(bf16[25,32,128]{2,1,0:T(8,128)(2,1)S(1)} %slice.92), channel_id=1, source_target_pairs={{0,2},{1,3},{2,4},{3,5},{4,6},{5,7},{6,0},{7,1},{8,10},{9,11},{10,... | collective-permute-start | bytes 614408 | tf_op jit(solution)/shard_map/ppermute | solution.py:232
  37.0 9.5 %collective-permute-start.10 = (bf16[15,32,128]{2,1,0:T(8,128)(2,1)S(1)}, bf16[15,32,128]{2,1,0:T(8,128)(2,1)S(1)}, u32[]{:S(2)}, u32[]{:S(2)}) collective-permute-start(bf16[15,32,128]{2,1,0:T(8,128)(2,1)S(1)} %slice.101), channel_id=1, source_target_pairs={{2,0},{3,1},{4,2},{5,3},{6,4},{7,5},{0,6},{1,7},{10,8},{11,9},{12,... | collective-permute-start | bytes 368648 | tf_op jit(solution)/shard_map/ppermute | solution.py:232
  39.4 11.3 %collective-permute-start.5 = (bf16[25,32,128]{2,1,0:T(8,128)(2,1)S(1)}, bf16[25,32,128]{2,1,0:T(8,128)(2,1)S(1)}, u32[]{:S(2)}, u32[]{:S(2)}) collective-permute-start(bf16[25,32,128]{2,1,0:T(8,128)(2,1)S(1)} %slice.93), channel_id=1, source_target_pairs={{2,0},{3,1},{4,2},{5,3},{6,4},{7,5},{0,6},{1,7},{10,8},{11,9},{12,... | collective-permute-start | bytes 614408 | tf_op jit(solution)/shard_map/ppermute | solution.py:232
  39.7 11.0 %collective-permute-start.2 = (bf16[80,32,128]{2,1,0:T(8,128)(2,1)S(1)}, bf16[80,32,128]{2,1,0:T(8,128)(2,1)S(1)}, u32[]{:S(2)}, u32[]{:S(2)}) collective-permute-start(bf16[80,32,128]{2,1,0:T(8,128)(2,1)S(1)} %collective-permute-done.1), channel_id=1, source_target_pairs={{0,1},{1,0},{2,3},{3,2},{4,5},{5,4},{6,7},{7,6},{8,9},{9,8},{10,11... | collective-permute-start | bytes 1966088 | tf_op jit(solution)/shard_map/ppermute | solution.py:216
  39.8 12.9 %copy-start = (bf16[48,128,256]{2,1,0:T(8,128)(2,1)S(1)}, bf16[48,128,256]{2,1,0:T(8,128)(2,1)}, u32[]{:S(2)}) copy-start(bf16[48,128,256]{2,1,0:T(8,128)(2,1)} %get-tuple-element.25.halves) | copy-start | bytes 9437188
  39.8 12.9 %copy-start.3 = (s32[364]{0:T(512)S(1)}, s32[364]{0:T(512)}, u32[]{:S(2)}) copy-start(s32[364]{0:T(512)} %get-tuple-element.24.lists) | copy-start | bytes 4372
  41.7 10.9 %collective-permute-start.8 = (bf16[80,32,128]{2,1,0:T(8,128)(2,1)S(1)}, bf16[80,32,128]{2,1,0:T(8,128)(2,1)S(1)}, u32[]{:S(2)}, u32[]{:S(2)}) collective-permute-start(bf16[80,32,128]{2,1,0:T(8,128)(2,1)S(1)} %collective-permute-done.3), channel_id=1, source_target_pairs={{0,1},{1,0},{2,3},{3,2},{4,5},{5,4},{6,7},{7,6},{8,9},{9,8},{10,11... | collective-permute-start | bytes 1966088 | tf_op jit(solution)/shard_map/ppermute | solution.py:216
  46.4 12.3 %collective-permute-start.11 = (bf16[15,32,128]{2,1,0:T(8,128)(2,1)S(1)}, bf16[15,32,128]{2,1,0:T(8,128)(2,1)S(1)}, u32[]{:S(2)}, u32[]{:S(2)}) collective-permute-start(bf16[15,32,128]{2,1,0:T(8,128)(2,1)S(1)} %collective-permute-done.9), channel_id=1, source_target_pairs={{0,1},{1,0},{2,3},{3,2},{4,5},{5,4},{6,7},{7,6},{8,9},{9,8},{10,11... | collective-permute-start | bytes 368648 | tf_op jit(solution)/shard_map/ppermute | solution.py:216
  46.4 12.3 %collective-permute-start.12 = (bf16[15,32,128]{2,1,0:T(8,128)(2,1)S(1)}, bf16[15,32,128]{2,1,0:T(8,128)(2,1)S(1)}, u32[]{:S(2)}, u32[]{:S(2)}) collective-permute-start(bf16[15,32,128]{2,1,0:T(8,128)(2,1)S(1)} %collective-permute-done.10), channel_id=1, source_target_pairs={{0,1},{1,0},{2,3},{3,2},{4,5},{5,4},{6,7},{7,6},{8,9},{9,8},{10,11... | collective-permute-start | bytes 368648 | tf_op jit(solution)/shard_map/ppermute | solution.py:216
  50.7 1.5 %collective-permute-start.6 = (bf16[25,32,128]{2,1,0:T(8,128)(2,1)S(1)}, bf16[25,32,128]{2,1,0:T(8,128)(2,1)S(1)}, u32[]{:S(2)}, u32[]{:S(2)}) collective-permute-start(bf16[25,32,128]{2,1,0:T(8,128)(2,1)S(1)} %collective-permute-done.4), channel_id=1, source_target_pairs={{0,1},{1,0},{2,3},{3,2},{4,5},{5,4},{6,7},{7,6},{8,9},{9,8},{10,11... | collective-permute-start | bytes 614408 | tf_op jit(solution)/shard_map/ppermute | solution.py:216
  50.7 1.7 %collective-permute-start.7 = (bf16[25,32,128]{2,1,0:T(8,128)(2,1)S(1)}, bf16[25,32,128]{2,1,0:T(8,128)(2,1)S(1)}, u32[]{:S(2)}, u32[]{:S(2)}) collective-permute-start(bf16[25,32,128]{2,1,0:T(8,128)(2,1)S(1)} %collective-permute-done.5), channel_id=1, source_target_pairs={{0,1},{1,0},{2,3},{3,2},{4,5},{5,4},{6,7},{7,6},{8,9},{9,8},{10,11... | collective-permute-start | bytes 614408 | tf_op jit(solution)/shard_map/ppermute | solution.py:216
  56.1 15.5 %collective-permute-start.13 = (bf16[32,32,128]{2,1,0:T(8,128)(2,1)S(1)}, bf16[32,32,128]{2,1,0:T(8,128)(2,1)S(1)}, u32[]{:S(2)}, u32[]{:S(2)}) collective-permute-start(bf16[32,32,128]{2,1,0:T(8,128)(2,1)S(1)} %slice.104), channel_id=1, source_target_pairs={{0,24},{8,16},{16,8},{24,0},{1,25},{9,17},{17,9},{25,1},{2,26},{10... | collective-permute-start | bytes 786440 | tf_op jit(solution)/shard_map/ppermute | solution.py:272
  62.3 16.1 %collective-permute-start.14 = (bf16[32,32,128]{2,1,0:T(8,128)(2,1)S(1)}, bf16[32,32,128]{2,1,0:T(8,128)(2,1)S(1)}, u32[]{:S(2)}, u32[]{:S(2)}) collective-permute-start(bf16[32,32,128]{2,1,0:T(8,128)(2,1)S(1)} %slice.83), channel_id=1, source_target_pairs={{0,24},{8,16},{16,8},{24,0},{1,25},{9,17},{17,9},{25,1},{2,26},{10... | collective-permute-start | bytes 786440 | tf_op jit(solution)/shard_map/ppermute | solution.py:272
  68.5 14.0 %collective-permute-start.16 = (bf16[32,32,128]{2,1,0:T(8,128)(2,1)S(1)}, bf16[32,32,128]{2,1,0:T(8,128)(2,1)S(1)}, u32[]{:S(2)}, u32[]{:S(2)}) collective-permute-start(bf16[32,32,128]{2,1,0:T(8,128)(2,1)S(1)} %slice.85), channel_id=1, source_target_pairs={{0,8},{8,0},{16,24},{24,16},{1,9},{9,1},{17,25},{25,17},{2,10},{10... | collective-permute-start | bytes 786440 | tf_op jit(solution)/shard_map/ppermute | solution.py:272
  70.0 12.4 %collective-permute-start.15 = (bf16[32,32,128]{2,1,0:T(8,128)(2,1)S(1)}, bf16[32,32,128]{2,1,0:T(8,128)(2,1)S(1)}, u32[]{:S(2)}, u32[]{:S(2)}) collective-permute-start(bf16[32,32,128]{2,1,0:T(8,128)(2,1)S(1)} %slice.84), channel_id=1, source_target_pairs={{0,16},{8,24},{16,0},{24,8},{1,17},{9,25},{17,1},{25,9},{2,18},{10... | collective-permute-start | bytes 786440 | tf_op jit(solution)/shard_map/ppermute | solution.py:272
  71.6 5.6 %copy-start.7 = (bf16[32,32,128]{2,1,0:T(8,128)(2,1)}, bf16[32,32,128]{2,1,0:T(8,128)(2,1)S(1)}, u32[]{:S(2)}) copy-start(bf16[32,32,128]{2,1,0:T(8,128)(2,1)S(1)} %collective-permute-done.13.rest_3_) | copy-start | bytes 786436
  77.2 11.5 %collective-permute-start.18 = (bf16[32,32,128]{2,1,0:T(8,128)(2,1)S(1)}, bf16[32,32,128]{2,1,0:T(8,128)(2,1)S(1)}, u32[]{:S(2)}, u32[]{:S(2)}) collective-permute-start(bf16[32,32,128]{2,1,0:T(8,128)(2,1)S(1)} %slice.87), channel_id=1, source_target_pairs={{0,16},{8,24},{16,0},{24,8},{1,17},{9,25},{17,1},{25,9},{2,18},{10... | collective-permute-start | bytes 786440 | tf_op jit(solution)/shard_map/ppermute | solution.py:272
  77.8 10.9 %collective-permute-start.17 = (bf16[32,32,128]{2,1,0:T(8,128)(2,1)S(1)}, bf16[32,32,128]{2,1,0:T(8,128)(2,1)S(1)}, u32[]{:S(2)}, u32[]{:S(2)}) collective-permute-start(bf16[32,32,128]{2,1,0:T(8,128)(2,1)S(1)} %slice.86), channel_id=1, source_target_pairs={{0,8},{8,0},{16,24},{24,16},{1,9},{9,1},{17,25},{25,17},{2,10},{10... | collective-permute-start | bytes 786440 | tf_op jit(solution)/shard_map/ppermute | solution.py:272
  78.4 3.4 %copy-start.4 = (bf16[32,32,128]{2,1,0:T(8,128)(2,1)}, bf16[32,32,128]{2,1,0:T(8,128)(2,1)S(1)}, u32[]{:S(2)}) copy-start(bf16[32,32,128]{2,1,0:T(8,128)(2,1)S(1)} %collective-permute-done.14.rest_3_) | copy-start | bytes 786436
  81.8 0.7 copy-start.2
  82.5 3.4 %copy-start.9 = (bf16[32,32,128]{2,1,0:T(8,128)(2,1)}, bf16[32,32,128]{2,1,0:T(8,128)(2,1)S(1)}, u32[]{:S(2)}) copy-start(bf16[32,32,128]{2,1,0:T(8,128)(2,1)S(1)} %collective-permute-done.15.rest_2_) | copy-start | bytes 786436
  82.5 3.4 %copy-start.8 = (bf16[32,32,128]{2,1,0:T(8,128)(2,1)}, bf16[32,32,128]{2,1,0:T(8,128)(2,1)S(1)}, u32[]{:S(2)}) copy-start(bf16[32,32,128]{2,1,0:T(8,128)(2,1)S(1)} %collective-permute-done.16.rest_1_) | copy-start | bytes 786436
  85.9 0.7 copy-start.1
  88.7 0.7 copy-start.5
  89.5 0.7 copy-start.6

commit v3 on v1

v3 whole, which is shorter than its diff:
```python
import functools

import jax
import jax.numpy as jnp
from jax import lax
from jax.experimental import pallas as pl
from jax.experimental.pallas import tpu as pltpu
from jax.sharding import PartitionSpec as P

CORES = 2
DEPTH = 2
PARTS = (2, 2)
BATCH = 8
NO_COST = pl.CostEstimate(flops=0, bytes_accessed=0, transcendentals=0)
SMEM = pl.BlockSpec(memory_space=pltpu.SMEM)
VMEM = pl.BlockSpec(memory_space=pltpu.VMEM)


class Lists:
    def __init__(self, count, sectors, chips):
        self.count = count
        self.sectors = sectors
        self.chips = chips
        self.sizes = [count // n for n in PARTS]
        self.starts = [sum(self.sizes[:i]) for i in range(len(PARTS))]
        self.pairs = [((n + min(sectors, n)) // 2 + DEPTH - 1) // DEPTH * DEPTH for n in self.sizes]
        self.firsts = [sum(self.pairs[:i]) for i in range(len(PARTS))]
        self.all_pairs = sum(self.pairs)
        self.far = chips // 2 if chips % 2 == 0 else chips
        self.groups = 0
        self.left = self.groups + len(PARTS)
        self.right = self.left + self.all_pairs
        self.position = self.right + 2 * self.all_pairs
        self.origin = self.position + 2 * self.all_pairs
        self.rows = self.origin + count
        self.columns = self.rows + count
        self.length = self.columns + count


def order_kernel(at, place, lsec, rsec, owner, live, psi, lists, halves, base, rank, source):
    width = psi.shape[1]
    chips = at.chips
    chip, core = place[0], place[1]
    row = lax.broadcasted_iota(jnp.int32, (width, width), 0)
    col = lax.broadcasted_iota(jnp.int32, (width, width), 1)
    zero = jnp.int32(0)

    def slot_of(sector):
        where = owner[sector]
        away = lax.rem(where // CORES - chip + chips, chips)
        away = jnp.where(away == at.far, chips - 1, jnp.where(away > at.far, away - 1, away))
        return away * CORES + lax.rem(where + core, CORES)

    def clear_slot(s, carry):
        base[s] = 0
        return carry

    def count(k, carry):
        slot = slot_of(lsec[k])
        rank[k] = base[slot]
        base[slot] = base[slot] + 1
        return carry

    def begin(s, first):
        members = base[s]
        base[s] = first
        return first + members

    def enter(k, carry):
        lists[at.origin + base[slot_of(lsec[k])] + rank[k]] = k
        return carry

    lax.fori_loop(0, at.sectors, clear_slot, 0)
    lax.fori_loop(0, at.count, count, 0)
    lax.fori_loop(0, at.sectors, begin, zero)
    lax.fori_loop(0, at.count, enter, 0)

    for part, (start, size, first) in enumerate(zip(at.starts, at.sizes, at.firsts)):
        def clear_pair(p, carry):
            lists[at.left + p] = 0
            for h in range(2):
                lists[at.right + 2 * p + h] = 0
                lists[at.position + 2 * p + h] = size
                source[2 * p + h] = 0
            return carry

        def pair_up(i, carry):
            pair, filled, before = carry
            k = lists[at.origin + start + i]
            left, right = lsec[k], rsec[k]
            same = (filled == 1) & (left == before)
            pair = jnp.where(same, pair, pair + 1)
            filled = jnp.where(same, 2, 1)
            half = 2 * pair + filled - 1
            lists[at.left + pair] = slot_of(left)
            lists[at.right + half] = slot_of(right)
            lists[at.position + half] = i
            lists[at.rows + start + i] = live[left]
            lists[at.columns + start + i] = live[right]
            source[half] = k
            return pair, filled, left

        lax.fori_loop(first, first + at.pairs[part], clear_pair, 0)
        last, _, _ = lax.fori_loop(0, size, pair_up, (zero + first - 1, zero, zero - 1))
        groups = (last - first + DEPTH) // DEPTH
        lists[at.groups + part] = groups

        def fill(i, carry):
            for u in range(DEPTH):
                p = first + i * DEPTH + u
                for h in range(2):
                    k = source[2 * p + h]
                    mask = (row < live[lsec[k]]) & (col < live[rsec[k]])
                    block = psi[k]
                    halves[p, :, h * width:(h + 1) * width] = jnp.where(mask, block, jnp.zeros_like(block))
            return carry

        lax.fori_loop(0, groups, fill, 0)


def multiply_kernel(part, at, place, lists, halves, right, left, *rest):
    outs, inner = rest[:-1], rest[-1]
    width = halves.shape[1]
    rows = outs[0].shape[1]
    channels = left.shape[1]
    first = at.firsts[part]
    groups = lists[at.groups + part]

    def one(group, side):
        for u in range(DEPTH):
            pair = first + group * DEPTH + u
            for h in range(2):
                slot = lists[at.right + 2 * pair + h]
                wide = jnp.concatenate([right[slot, w] for w in range(channels)], axis=1)
                block = halves[pair, :, h * width:(h + 1) * width]
                z = jnp.dot(block, wide, preferred_element_type=jnp.float32).astype(jnp.bfloat16)
                for w in range(channels):
                    inner[side * DEPTH + u, w * width:(w + 1) * width, h * width:(h + 1) * width] = (
                        z[:, w * width:(w + 1) * width]
                    )

    def two(group, side):
        for u in range(DEPTH):
            pair = first + group * DEPTH + u
            slot = lists[at.left + pair]
            wide = []
            for d in range(len(outs)):
                start = pl.multiple_of((place[2] ^ d) * rows, rows)
                wide.append(jnp.concatenate([left[slot, w, pl.ds(start, rows), :] for w in range(channels)], axis=1))
            wide = jnp.concatenate(wide, axis=0)
            result = jnp.dot(wide, inner[side * DEPTH + u], preferred_element_type=jnp.float32).astype(jnp.bfloat16)
            for h in range(2):
                where = lists[at.position + 2 * pair + h]
                for d, out in enumerate(outs):
                    out[where] = result[d * rows:(d + 1) * rows, h * width:(h + 1) * width]

    def body(i, carry):
        one(2 * i + 1, 1)
        two(2 * i, 0)
        one(2 * i + 2, 0)
        two(2 * i + 1, 1)
        return carry

    one(0, 0)
    turns = (groups - 1) // 2
    lax.fori_loop(0, turns, body, 0)

    @pl.when(2 * turns + 1 == groups)
    def _():
        two(2 * turns, 0)

    @pl.when(2 * turns + 1 != groups)
    def _():
        one(2 * turns + 1, 1)
        two(2 * turns, 0)
        two(2 * turns + 1, 1)


def place_kernel(at, place, lists, *rest):
    out, totals = rest[-1], rest[:-1]
    rows, width = out.shape[1], out.shape[2]
    row = place[2] * rows + lax.broadcasted_iota(jnp.int32, (rows, width), 0)
    col = lax.broadcasted_iota(jnp.int32, (rows, width), 1)

    for start, total in zip(at.starts, totals):
        def body(i, carry):
            blocks = []
            for u in range(BATCH):
                k = start + i * BATCH + u
                mask = (row < lists[at.rows + k]) & (col < lists[at.columns + k])
                block = total[i * BATCH + u].astype(jnp.float32)
                blocks.append(jnp.where(mask, block, jnp.zeros_like(block)).astype(jnp.bfloat16))
            for u in range(BATCH):
                out[lists[at.origin + start + i * BATCH + u]] = blocks[u]
            return carry

        lax.fori_loop(0, total.shape[0] // BATCH, body, 0)


def on_device(psi, left_env, right_env, left_sector, right_sector, sector_owner, sector_rows):
    nwave = lax.axis_size("wave")
    nenv = lax.axis_size("env")
    count, width = psi.shape[0], psi.shape[1]
    channels = left_env.shape[0]
    sectors = sector_owner.shape[0]
    chips = nwave // CORES
    rows = width // nenv
    wave = lax.axis_index("wave")
    env = lax.axis_index("env")
    place = jnp.stack([wave // CORES, wave % CORES, env]).astype(jnp.int32)

    up = [(i, (i + CORES) % nwave) for i in range(nwave)]
    down = [((i + CORES) % nwave, i) for i in range(nwave)]
    other = [(i, i ^ 1) for i in range(nwave)]
    at = Lists(count, sectors, chips)

    def swap(x):
        return lax.ppermute(x, "wave", other)

    def gate(*values):
        return lax.optimization_barrier(values)

    def ring(own):
        held = {0: own}
        rising = falling = own
        for r in range(1, (chips - 1) // 2 + 1):
            rising = lax.ppermute(rising, "wave", up)
            falling = lax.ppermute(falling, "wave", down)
            held[chips - r], held[r] = rising, falling
        return held, rising, falling

    def far(rising, falling, lo, hi):
        mid = (lo + hi) // 2
        return [lax.ppermute(rising[lo:mid], "wave", up), lax.ppermute(falling[mid:hi], "wave", down)]

    def far_pieces(last):
        return [jnp.concatenate(last), jnp.concatenate([swap(x) for x in last])]

    held, rising, falling = ring(jnp.concatenate([right_env[:, 0], left_env[:, 0]]))
    pieces = [piece for d in range(chips) if d in held for piece in (held[d], swap(held[d]))]
    right = [piece[:channels] for piece in pieces]
    near = jnp.stack([piece[channels:] for piece in pieces])
    if chips % 2 == 0:
        right += far_pieces(far(rising, falling, 0, channels))
        last = far(rising, falling, channels, 2 * channels)
    right = jnp.stack(right)

    lists, halves = pl.pallas_call(
        functools.partial(order_kernel, at),
        out_shape=(
            jax.ShapeDtypeStruct((at.length,), jnp.int32),
            jax.ShapeDtypeStruct((at.all_pairs, width, 2 * width), jnp.bfloat16),
        ),
        in_specs=[SMEM] * 5 + [VMEM],
        out_specs=(SMEM, VMEM),
        scratch_shapes=[pltpu.SMEM((n,), jnp.int32) for n in (sectors, count, 2 * at.all_pairs)],
        compiler_params=pltpu.CompilerParams(vmem_limit_bytes=2 * (psi.size + 2 * at.all_pairs * width * width) + (4 << 20)),
    )(place, left_sector[:, 0], right_sector[:, 0], sector_owner, sector_rows, psi)

    def multiply(part, right, left):
        need = right.size + left.size + halves.size + count * width * width
        need = 2 * (need + 4 * DEPTH * channels * width * width) + (8 << 20)
        return list(pl.pallas_call(
            functools.partial(multiply_kernel, part, at),
            out_shape=[jax.ShapeDtypeStruct((at.sizes[part] + 1, rows, width), jnp.bfloat16)] * nenv,
            in_specs=[SMEM] * 2 + [VMEM] * 3,
            out_specs=[VMEM] * nenv,
            scratch_shapes=[pltpu.VMEM((2 * DEPTH, channels * width, 2 * width), jnp.bfloat16)],
            compiler_params=pltpu.CompilerParams(vmem_limit_bytes=min(need, 60 << 20)),
            cost_estimate=NO_COST,
        )(place, lists, halves, right, left))

    def exchange(parts):
        total = parts[0][:-1].astype(jnp.float32)
        for d in range(nenv - 1, 0, -1):
            arrived = lax.ppermute(parts[d][:-1], "env", [(i, i ^ d) for i in range(nenv)])
            total = total + arrived.astype(jnp.float32)
        return total.astype(jnp.bfloat16)

    parts = multiply(0, right, near)
    if chips % 2 == 0:
        parts[0], *last = gate(parts[0], *last)
        whole = jnp.concatenate([near, jnp.stack(far_pieces(last))])
    else:
        whole = near
    terms = [exchange(parts)]
    for part in range(1, len(PARTS)):
        terms.append(exchange(multiply(part, right, whole)))
    return pl.pallas_call(
        functools.partial(place_kernel, at),
        out_shape=jax.ShapeDtypeStruct((count, rows, width), jnp.bfloat16),
        in_specs=[SMEM] * 2 + [VMEM] * len(terms),
        out_specs=VMEM,
        compiler_params=pltpu.CompilerParams(vmem_limit_bytes=4 * count * rows * width + (4 << 20)),
        cost_estimate=NO_COST,
    )(place, lists, *terms)


def solution(mesh):
    return jax.shard_map(
        on_device,
        mesh=mesh,
        in_specs=(
            P("wave", None, None),
            P("env", "wave", None, None),
            P("env", "wave", None, None),
            P("wave", None),
            P("wave", None),
            P(),
            P(),
        ),
        out_specs=P("wave", "env", None),
        check_vma=False,
    )
```

time: 117 us -> 79.8 us (0.68)
  waiting for transfers between devices: 51.5 us -> 31 us
  Pallas kernels: 31.3 us -> 22.5 us
  starting transfers between devices: 25.1 us -> 18.2 us
  other arithmetic: 5.17 us -> 1.73 us
  local copies, waits for them, and re-layouts: 4.03 us -> 5.81 us
    ppermute x21 -> x19, waiting for transfers between devices: 51.5 us -> 31 us  [the longest x6 13.1 us: exchange(): lax.ppermute(parts[d][:-1], 'env', [(i, i ^ d) for i in range(nenv)])]
    pallas_call x4, Pallas kernels: 31.3 us -> 22.5 us  [the longest x2 11.9 us: multiply(): pl.pallas_call(functools.partial(multiply_kernel, part, at), out_shape=[j...]
    ppermute x21 -> x19, starting transfers between devices: 25.1 us -> 18.2 us  [the longest x6 7.37 us: exchange(): lax.ppermute(parts[d][:-1], 'env', [(i, i ^ d) for i in range(nenv)])]
    unnamed x12 -> x20, local copies, waits for them, and re-layouts: 2.74 us -> 5.66 us
    unnamed x3 -> x2, other arithmetic: 1.32 us -> 0.09 us
  transfers between devices with their start and end apart: 21 -> 19, of which waited for: 12 -> 9; matrix products, arithmetic and copies ran while one was open for 3% -> 2% of each run, Pallas kernels for 0% -> 26%
where the time goes in v3:
time: 79.8 us; the launch traced here: 79.6 us
  waiting for transfers between devices  31 us (39%)
  Pallas kernels  22.5 us (28%)
  starting transfers between devices  18.2 us (23%)
  local copies, waits for them, and re-layouts  5.81 us (7%)
  other arithmetic  1.73 us (2%)
    ppermute x6, waiting for transfers between devices, exchange(): lax.ppermute(parts[d][:-1], 'env', [(i, i ^ d) for i in range(nenv)])  13.1 us
    ppermute x1, waiting for transfers between devices, ring(): falling = lax.ppermute(falling, 'wave', down)  12.7 us
    pallas_call x2, Pallas kernels, multiply(): pl.pallas_call(functools.partial(multiply_kernel, part, at), out_shape=[j...  11.9 us
    pallas_call x1, Pallas kernels, on_device(): pl.pallas_call(functools.partial(order_kernel, at), out_shape=(jax.ShapeD...  9.07 us
    ppermute x6, starting transfers between devices, exchange(): lax.ppermute(parts[d][:-1], 'env', [(i, i ^ d) for i in range(nenv)])  7.37 us
    unnamed x20, local copies, waits for them, and re-layouts  5.66 us
    ppermute x2, starting transfers between devices, far(): lax.ppermute(falling[mid:hi], 'wave', down)  3.32 us
    ppermute x1, starting transfers between devices, ring(): rising = lax.ppermute(rising, 'wave', up)  3.08 us
  transfers between devices with their start and end apart: 19, of which 9 were waited for; matrix products, arithmetic and copies ran while one was open for 2% of the time, Pallas kernels for 26%

profile of v3, /device:TPU:0, one launch (start us, length us, event | category | flops | bytes accessed | tf_op | source)
XLA Modules:
  0.0 79.6 jit_solution(17888245926939050483)
XLA Ops:
  0.0 1.2 %pad_maximum_fusion = bf16[20,128,128]{2,1,0:T(8,128)(2,1)S(1)} fusion(bf16[10,128,128]{2,1,0:T(8,128)(2,1)} %bitcast.80, bf16[10,128,128]{2,1,0:T(8,128)(2,1)} %bitcast.81), kind=kLoop, calls=%fused_computation | loop fusion | flops 327680 | bytes 1310720 | tf_op jit(solution)/shard_map/concatenate | solution.py:239
  1.2 3.1 %collective-permute-start.3 = (bf16[20,128,128]{2,1,0:T(8,128)(2,1)S(1)}, bf16[20,128,128]{2,1,0:T(8,128)(2,1)S(1)}, u32[]{:S(2)}, u32[]{:S(2)}) collective-permute-start(bf16[20,128,128]{2,1,0:T(8,128)(2,1)S(1)} %pad_maximum_fusion), channel_id=1, source_target_pairs={{0,2},{1,3},{2,4},{3,5},{4,6},{5,7},{6,0},{7,1},{8,10},{9,11},{10,... | collective-permute-start | bytes 1966088 | tf_op jit(solution)/shard_map/ppermute | solution.py:227
  4.3 2.1 %collective-permute-start.1 = (bf16[20,128,128]{2,1,0:T(8,128)(2,1)S(1)}, bf16[20,128,128]{2,1,0:T(8,128)(2,1)S(1)}, u32[]{:S(2)}, u32[]{:S(2)}) collective-permute-start(bf16[20,128,128]{2,1,0:T(8,128)(2,1)S(1)} %pad_maximum_fusion), channel_id=1, source_target_pairs={{2,0},{3,1},{4,2},{5,3},{6,4},{7,5},{0,6},{1,7},{10,8},{11,9},{12,... | collective-permute-start | bytes 1966088 | tf_op jit(solution)/shard_map/ppermute | solution.py:228
  6.4 0.0 collective-permute-start
  6.4 0.1 pad_add_fusion.place
  6.5 1.6 %copy-done = bf16[64,128,128]{2,1,0:T(8,128)(2,1)S(1)} copy-done((bf16[64,128,128]{2,1,0:T(8,128)(2,1)S(1)}, bf16[64,128,128]{2,1,0:T(8,128)(2,1)}, u32[]{:S(2)}) %copy-start) | copy-done | bytes 2097176
  8.0 0.7 copy-done.1
  8.7 0.7 copy-done.2
  9.4 0.7 copy-done.3
  10.0 0.7 copy-done.4
  10.7 9.1 %shard_map.73 = (s32[394]{0:T(512)S(1)}, bf16[40,128,256]{2,1,0:T(8,128)(2,1)S(1)}) custom-call(s32[3]{0:T(128)S(1)} %pad_add_fusion.place, s32[64]{0:T(128)S(1)} %bitcast.78, s32[64]{0:T(128)S(1)} %bitcast.79, s32[8]{0:T(128)S(1)} %copy-done.3, s32[8]{0:T(128)S(1)} %copy-done.4, bf16[64,128,128]{2,1,0:T(8,128)(2,1)S(1)} %copy-done), custom_call_target="tpu_custom_call" | custom-call | tf_op jit(solution)/shard_map/pallas_call | solution.py:248
  19.8 0.2 bitcast_dynamic-update-slice_fusion
  19.9 2.0 %collective-permute-done.3 = bf16[20,128,128]{2,1,0:T(8,128)(2,1)S(1)} collective-permute-done((bf16[20,128,128]{2,1,0:T(8,128)(2,1)S(1)}, bf16[20,128,128]{2,1,0:T(8,128)(2,1)S(1)}, u32[]{:S(2)}, u32[]{:S(2)}) %collective-permute-start.3) | collective-permute-done | bytes 655392 | tf_op jit(solution)/shard_map/ppermute | solution.py:227
  21.9 0.1 collective-permute-start.5
  22.0 12.7 %collective-permute-done.1 = bf16[20,128,128]{2,1,0:T(8,128)(2,1)S(1)} collective-permute-done((bf16[20,128,128]{2,1,0:T(8,128)(2,1)S(1)}, bf16[20,128,128]{2,1,0:T(8,128)(2,1)S(1)}, u32[]{:S(2)}, u32[]{:S(2)}) %collective-permute-start.1) | collective-permute-done | bytes 655392 | tf_op jit(solution)/shard_map/ppermute | solution.py:228
  34.7 0.0 collective-permute-start.2
  34.8 3.1 %collective-permute-start.6 = (bf16[5,128,128]{2,1,0:T(8,128)(2,1)S(1)}, bf16[5,128,128]{2,1,0:T(8,128)(2,1)S(1)}, u32[]{:S(2)}, u32[]{:S(2)}) collective-permute-start(bf16[5,128,128]{2,1,0:T(8,128)(2,1)S(1)} %get-tuple-element.47), channel_id=1, source_target_pairs={{2,0},{3,1},{4,2},{5,3},{6,4},{7,5},{0,6},{1,7},{10,8},{11,9},{12,... | collective-permute-start | bytes 491528 | tf_op jit(solution)/shard_map/ppermute | solution.py:234
  37.9 0.2 collective-permute-start.10
  38.1 0.1 collective-permute-start.4
  38.2 0.2 fusion.9
  38.4 0.2 fusion.11
  38.7 0.7 collective-permute-done.5
  39.3 1.1 %collective-permute-start.9 = (bf16[5,128,128]{2,1,0:T(8,128)(2,1)S(1)}, bf16[5,128,128]{2,1,0:T(8,128)(2,1)S(1)}, u32[]{:S(2)}, u32[]{:S(2)}) collective-permute-start(bf16[5,128,128]{2,1,0:T(8,128)(2,1)S(1)} %get-tuple-element.48), channel_id=1, source_target_pairs={{0,2},{1,3},{2,4},{3,5},{4,6},{5,7},{6,0},{7,1},{8,10},{9,11},{10,... | collective-permute-start | bytes 491528 | tf_op jit(solution)/shard_map/ppermute | solution.py:234
  40.5 2.3 %collective-permute-done.6 = bf16[5,128,128]{2,1,0:T(8,128)(2,1)S(1)} collective-permute-done((bf16[5,128,128]{2,1,0:T(8,128)(2,1)S(1)}, bf16[5,128,128]{2,1,0:T(8,128)(2,1)S(1)}, u32[]{:S(2)}, u32[]{:S(2)}) %collective-permute-start.6) | collective-permute-done | bytes 163872 | tf_op jit(solution)/shard_map/ppermute | solution.py:234
  42.8 0.0 collective-permute-start.7
  42.8 0.5 collective-permute-start.8
  43.3 0.3 fusion.13
  43.6 0.2 fusion.15
  43.9 0.2 fusion.17
  44.2 0.0 collective-permute-done.7
  44.2 0.2 collective-permute-done.8
  44.5 6.3 %shard_map.74 = (bf16[33,32,128]{2,1,0:T(8,128)(2,1)S(1)}, bf16[33,32,128]{2,1,0:T(8,128)(2,1)S(1)}, bf16[33,32,128]{2,1,0:T(8,128)(2,1)S(1)}, bf16[33,32,128]{2,1,0:T(8,128)(2,1)S(1)}) custom-call(s32[3]{0:T(128)S(1)} %pad_add_fusion.place, s32[394]{0:T(512)S(1)} %get-tuple-element.18.lists, bf16[40,128,256]{2,1,0:T(8,128)(2,1)S(1)} %get-tuple-element.19.halves, ...), custom_call_target="tpu_custom_call" | custom-call | tf_op jit(solution)/shard_map/pallas_call | solution.py:263
  50.8 0.3 collective-permute-start.14
  51.1 0.2 collective-permute-start.15
  51.4 2.5 %collective-permute-start.11 = (bf16[32,32,128]{2,1,0:T(8,128)(2,1)S(1)}, bf16[32,32,128]{2,1,0:T(8,128)(2,1)S(1)}, u32[]{:S(2)}, u32[]{:S(2)}) collective-permute-start(bf16[32,32,128]{2,1,0:T(8,128)(2,1)S(1)} %slice.81), channel_id=1, source_target_pairs={{0,24},{8,16},{16,8},{24,0},{1,25},{9,17},{17,9},{25,1},{2,26},{10... | collective-permute-start | bytes 786440 | tf_op jit(solution)/shard_map/ppermute | solution.py:276
  53.9 0.6 collective-permute-start.12
  54.5 0.6 collective-permute-start.13
  55.2 5.6 %shard_map.75 = (bf16[33,32,128]{2,1,0:T(8,128)(2,1)S(1)}, bf16[33,32,128]{2,1,0:T(8,128)(2,1)S(1)}, bf16[33,32,128]{2,1,0:T(8,128)(2,1)S(1)}, bf16[33,32,128]{2,1,0:T(8,128)(2,1)S(1)}) custom-call(s32[3]{0:T(128)S(1)} %pad_add_fusion.place, s32[394]{0:T(512)S(1)} %get-tuple-element.18.lists, bf16[40,128,256]{2,1,0:T(8,128)(2,1)S(1)} %get-tuple-element.19.halves, ...), custom_call_target="tpu_custom_call" | custom-call | tf_op jit(solution)/shard_map/pallas_call | solution.py:263
  60.8 2.5 %collective-permute-start.16 = (bf16[32,32,128]{2,1,0:T(8,128)(2,1)S(1)}, bf16[32,32,128]{2,1,0:T(8,128)(2,1)S(1)}, u32[]{:S(2)}, u32[]{:S(2)}) collective-permute-start(bf16[32,32,128]{2,1,0:T(8,128)(2,1)S(1)} %slice.85), channel_id=1, source_target_pairs={{0,24},{8,16},{16,8},{24,0},{1,25},{9,17},{17,9},{25,1},{2,26},{10... | collective-permute-start | bytes 786440 | tf_op jit(solution)/shard_map/ppermute | solution.py:276
  63.4 0.6 collective-permute-start.17
  64.0 0.6 collective-permute-start.18
  64.6 2.6 %collective-permute-done.12 = bf16[32,32,128]{2,1,0:T(8,128)(2,1)S(1)} collective-permute-done((bf16[32,32,128]{2,1,0:T(8,128)(2,1)S(1)}, bf16[32,32,128]{2,1,0:T(8,128)(2,1)S(1)}, u32[]{:S(2)}, u32[]{:S(2)}) %collective-permute-start.12) | collective-permute-done | bytes 262176 | tf_op jit(solution)/shard_map/ppermute | solution.py:276
  67.2 0.1 add_convert_fusion.1.rest_0_
  67.3 5.5 %collective-permute-done.16 = bf16[32,32,128]{2,1,0:T(8,128)(2,1)S(1)} collective-permute-done((bf16[32,32,128]{2,1,0:T(8,128)(2,1)S(1)}, bf16[32,32,128]{2,1,0:T(8,128)(2,1)S(1)}, u32[]{:S(2)}, u32[]{:S(2)}) %collective-permute-start.16) | collective-permute-done | bytes 262176 | tf_op jit(solution)/shard_map/ppermute | solution.py:276
  72.8 4.9 %collective-permute-done.17 = bf16[32,32,128]{2,1,0:T(8,128)(2,1)S(1)} collective-permute-done((bf16[32,32,128]{2,1,0:T(8,128)(2,1)S(1)}, bf16[32,32,128]{2,1,0:T(8,128)(2,1)S(1)}, u32[]{:S(2)}, u32[]{:S(2)}) %collective-permute-start.17) | collective-permute-done | bytes 262176 | tf_op jit(solution)/shard_map/ppermute | solution.py:276
  77.7 0.1 collective-permute-done.18
  77.8 0.1 add_convert_fusion.rest_1_
  78.0 1.6 %shard_map.76 = bf16[64,32,128]{2,1,0:T(8,128)(2,1)} custom-call(s32[3]{0:T(128)S(1)} %pad_add_fusion.place, s32[394]{0:T(512)S(1)} %get-tuple-element.18.lists, bf16[32,32,128]{2,1,0:T(8,128)(2,1)S(1)} %add_convert_fusion.1.rest_0_, bf16[32,32,128]{2,1,0:T(8,128)(2,1)S(1)} %add_convert_fusion.rest_1_), custom_call_target="tpu_custom_call" | custom-call | tf_op jit(solution)/shard_map/pallas_call | solution.py:289
  (30 shorter events, 0.4 us)
Async XLA Ops:
  0.0 19.7 %copy-start.6 = (bf16[10,1,128,128]{3,2,1,0:T(8,128)(2,1)S(1)}, bf16[10,1,128,128]{3,2,1,0:T(8,128)(2,1)}, u32[]{:S(2)}) copy-start(bf16[10,1,128,128]{3,2,1,0:T(8,128)(2,1)} %param.9) | copy-start | bytes 983044
  0.0 19.8 %copy-start.5 = (bf16[10,1,128,128]{3,2,1,0:T(8,128)(2,1)S(1)}, bf16[10,1,128,128]{3,2,1,0:T(8,128)(2,1)}, u32[]{:S(2)}) copy-start(bf16[10,1,128,128]{3,2,1,0:T(8,128)(2,1)} %param.8) | copy-start | bytes 983044
  1.2 20.7 %collective-permute-start.3 = (bf16[20,128,128]{2,1,0:T(8,128)(2,1)S(1)}, bf16[20,128,128]{2,1,0:T(8,128)(2,1)S(1)}, u32[]{:S(2)}, u32[]{:S(2)}) collective-permute-start(bf16[20,128,128]{2,1,0:T(8,128)(2,1)S(1)} %pad_maximum_fusion), channel_id=1, source_target_pairs={{0,2},{1,3},{2,4},{3,5},{4,6},{5,7},{6,0},{7,1},{8,10},{9,11},{10,... | collective-permute-start | bytes 1966088 | tf_op jit(solution)/shard_map/ppermute | solution.py:227
  4.3 30.5 %collective-permute-start.1 = (bf16[20,128,128]{2,1,0:T(8,128)(2,1)S(1)}, bf16[20,128,128]{2,1,0:T(8,128)(2,1)S(1)}, u32[]{:S(2)}, u32[]{:S(2)}) collective-permute-start(bf16[20,128,128]{2,1,0:T(8,128)(2,1)S(1)} %pad_maximum_fusion), channel_id=1, source_target_pairs={{2,0},{3,1},{4,2},{5,3},{6,4},{7,5},{0,6},{1,7},{10,8},{11,9},{12,... | collective-permute-start | bytes 1966088 | tf_op jit(solution)/shard_map/ppermute | solution.py:228
  6.4 31.7 %collective-permute-start = (bf16[20,128,128]{2,1,0:T(8,128)(2,1)S(1)}, bf16[20,128,128]{2,1,0:T(8,128)(2,1)S(1)}, u32[]{:S(2)}, u32[]{:S(2)}) collective-permute-start(bf16[20,128,128]{2,1,0:T(8,128)(2,1)S(1)} %pad_maximum_fusion), channel_id=1, source_target_pairs={{0,1},{1,0},{2,3},{3,2},{4,5},{5,4},{6,7},{7,6},{8,9},{9,8},{10,11... | collective-permute-start | bytes 1966088 | tf_op jit(solution)/shard_map/ppermute | solution.py:218
  6.5 1.6 %copy-start = (bf16[64,128,128]{2,1,0:T(8,128)(2,1)S(1)}, bf16[64,128,128]{2,1,0:T(8,128)(2,1)}, u32[]{:S(2)}) copy-start(bf16[64,128,128]{2,1,0:T(8,128)(2,1)} %psi.1) | copy-start | bytes 6291460
  8.0 0.7 copy-start.1
  8.7 0.7 copy-start.2
  9.4 0.7 copy-start.3
  10.0 0.7 copy-start.4
  21.9 17.4 %collective-permute-start.5 = (bf16[5,128,128]{2,1,0:T(8,128)(2,1)S(1)}, bf16[5,128,128]{2,1,0:T(8,128)(2,1)S(1)}, u32[]{:S(2)}, u32[]{:S(2)}) collective-permute-start(bf16[5,128,128]{2,1,0:T(8,128)(2,1)S(1)} %get-tuple-element.49), channel_id=1, source_target_pairs={{0,2},{1,3},{2,4},{3,5},{4,6},{5,7},{6,0},{7,1},{8,10},{9,11},{10,... | collective-permute-start | bytes 491528 | tf_op jit(solution)/shard_map/ppermute | solution.py:234
  34.7 8.1 %collective-permute-start.2 = (bf16[20,128,128]{2,1,0:T(8,128)(2,1)S(1)}, bf16[20,128,128]{2,1,0:T(8,128)(2,1)S(1)}, u32[]{:S(2)}, u32[]{:S(2)}) collective-permute-start(bf16[20,128,128]{2,1,0:T(8,128)(2,1)S(1)} %collective-permute-done.1), channel_id=1, source_target_pairs={{0,1},{1,0},{2,3},{3,2},{4,5},{5,4},{6,7},{7,6},{8,9},{9,8},{10,11... | collective-permute-start | bytes 1966088 | tf_op jit(solution)/shard_map/ppermute | solution.py:218
  34.8 8.0 %collective-permute-start.6 = (bf16[5,128,128]{2,1,0:T(8,128)(2,1)S(1)}, bf16[5,128,128]{2,1,0:T(8,128)(2,1)S(1)}, u32[]{:S(2)}, u32[]{:S(2)}) collective-permute-start(bf16[5,128,128]{2,1,0:T(8,128)(2,1)S(1)} %get-tuple-element.47), channel_id=1, source_target_pairs={{2,0},{3,1},{4,2},{5,3},{6,4},{7,5},{0,6},{1,7},{10,8},{11,9},{12,... | collective-permute-start | bytes 491528 | tf_op jit(solution)/shard_map/ppermute | solution.py:234
  37.9 12.9 %collective-permute-start.10 = (bf16[5,128,128]{2,1,0:T(8,128)(2,1)S(1)}, bf16[5,128,128]{2,1,0:T(8,128)(2,1)S(1)}, u32[]{:S(2)}, u32[]{:S(2)}) collective-permute-start(bf16[5,128,128]{2,1,0:T(8,128)(2,1)S(1)} %get-tuple-element.46), channel_id=1, source_target_pairs={{2,0},{3,1},{4,2},{5,3},{6,4},{7,5},{0,6},{1,7},{10,8},{11,9},{12,... | collective-permute-start | bytes 491528 | tf_op jit(solution)/shard_map/ppermute | solution.py:234
  38.1 5.8 %collective-permute-start.4 = (bf16[20,128,128]{2,1,0:T(8,128)(2,1)S(1)}, bf16[20,128,128]{2,1,0:T(8,128)(2,1)S(1)}, u32[]{:S(2)}, u32[]{:S(2)}) collective-permute-start(bf16[20,128,128]{2,1,0:T(8,128)(2,1)S(1)} %collective-permute-done.3), channel_id=1, source_target_pairs={{0,1},{1,0},{2,3},{3,2},{4,5},{5,4},{6,7},{7,6},{8,9},{9,8},{10,11... | collective-permute-start | bytes 1966088 | tf_op jit(solution)/shard_map/ppermute | solution.py:218
  39.3 11.4 %collective-permute-start.9 = (bf16[5,128,128]{2,1,0:T(8,128)(2,1)S(1)}, bf16[5,128,128]{2,1,0:T(8,128)(2,1)S(1)}, u32[]{:S(2)}, u32[]{:S(2)}) collective-permute-start(bf16[5,128,128]{2,1,0:T(8,128)(2,1)S(1)} %get-tuple-element.48), channel_id=1, source_target_pairs={{0,2},{1,3},{2,4},{3,5},{4,6},{5,7},{6,0},{7,1},{8,10},{9,11},{10,... | collective-permute-start | bytes 491528 | tf_op jit(solution)/shard_map/ppermute | solution.py:234
  42.8 1.4 %collective-permute-start.7 = (bf16[5,128,128]{2,1,0:T(8,128)(2,1)S(1)}, bf16[5,128,128]{2,1,0:T(8,128)(2,1)S(1)}, u32[]{:S(2)}, u32[]{:S(2)}) collective-permute-start(bf16[5,128,128]{2,1,0:T(8,128)(2,1)S(1)} %collective-permute-done.5), channel_id=1, source_target_pairs={{0,1},{1,0},{2,3},{3,2},{4,5},{5,4},{6,7},{7,6},{8,9},{9,8},{10,11... | collective-permute-start | bytes 491528 | tf_op jit(solution)/shard_map/ppermute | solution.py:218
  42.8 1.6 %collective-permute-start.8 = (bf16[5,128,128]{2,1,0:T(8,128)(2,1)S(1)}, bf16[5,128,128]{2,1,0:T(8,128)(2,1)S(1)}, u32[]{:S(2)}, u32[]{:S(2)}) collective-permute-start(bf16[5,128,128]{2,1,0:T(8,128)(2,1)S(1)} %collective-permute-done.6), channel_id=1, source_target_pairs={{0,1},{1,0},{2,3},{3,2},{4,5},{5,4},{6,7},{7,6},{8,9},{9,8},{10,11... | collective-permute-start | bytes 491528 | tf_op jit(solution)/shard_map/ppermute | solution.py:218
  50.8 4.4 %collective-permute-start.14 = (bf16[5,128,128]{2,1,0:T(8,128)(2,1)S(1)}, bf16[5,128,128]{2,1,0:T(8,128)(2,1)S(1)}, u32[]{:S(2)}, u32[]{:S(2)}) collective-permute-start(bf16[5,128,128]{2,1,0:T(8,128)(2,1)S(1)} %collective-permute-done.9), channel_id=1, source_target_pairs={{0,1},{1,0},{2,3},{3,2},{4,5},{5,4},{6,7},{7,6},{8,9},{9,8},{10,11... | collective-permute-start | bytes 491528 | tf_op jit(solution)/shard_map/ppermute | solution.py:218
  51.1 4.0 %collective-permute-start.15 = (bf16[5,128,128]{2,1,0:T(8,128)(2,1)S(1)}, bf16[5,128,128]{2,1,0:T(8,128)(2,1)S(1)}, u32[]{:S(2)}, u32[]{:S(2)}) collective-permute-start(bf16[5,128,128]{2,1,0:T(8,128)(2,1)S(1)} %collective-permute-done.10), channel_id=1, source_target_pairs={{0,1},{1,0},{2,3},{3,2},{4,5},{5,4},{6,7},{7,6},{8,9},{9,8},{10,11... | collective-permute-start | bytes 491528 | tf_op jit(solution)/shard_map/ppermute | solution.py:218
  51.4 12.6 %collective-permute-start.11 = (bf16[32,32,128]{2,1,0:T(8,128)(2,1)S(1)}, bf16[32,32,128]{2,1,0:T(8,128)(2,1)S(1)}, u32[]{:S(2)}, u32[]{:S(2)}) collective-permute-start(bf16[32,32,128]{2,1,0:T(8,128)(2,1)S(1)} %slice.81), channel_id=1, source_target_pairs={{0,24},{8,16},{16,8},{24,0},{1,25},{9,17},{17,9},{25,1},{2,26},{10... | collective-permute-start | bytes 786440 | tf_op jit(solution)/shard_map/ppermute | solution.py:276
  53.9 13.3 %collective-permute-start.12 = (bf16[32,32,128]{2,1,0:T(8,128)(2,1)S(1)}, bf16[32,32,128]{2,1,0:T(8,128)(2,1)S(1)}, u32[]{:S(2)}, u32[]{:S(2)}) collective-permute-start(bf16[32,32,128]{2,1,0:T(8,128)(2,1)S(1)} %slice.82), channel_id=1, source_target_pairs={{0,16},{8,24},{16,0},{24,8},{1,17},{9,25},{17,1},{25,9},{2,18},{10... | collective-permute-start | bytes 786440 | tf_op jit(solution)/shard_map/ppermute | solution.py:276
  54.5 12.7 %collective-permute-start.13 = (bf16[32,32,128]{2,1,0:T(8,128)(2,1)S(1)}, bf16[32,32,128]{2,1,0:T(8,128)(2,1)S(1)}, u32[]{:S(2)}, u32[]{:S(2)}) collective-permute-start(bf16[32,32,128]{2,1,0:T(8,128)(2,1)S(1)} %slice.83), channel_id=1, source_target_pairs={{0,8},{8,0},{16,24},{24,16},{1,9},{9,1},{17,25},{25,17},{2,10},{10... | collective-permute-start | bytes 786440 | tf_op jit(solution)/shard_map/ppermute | solution.py:276
  60.8 12.0 %collective-permute-start.16 = (bf16[32,32,128]{2,1,0:T(8,128)(2,1)S(1)}, bf16[32,32,128]{2,1,0:T(8,128)(2,1)S(1)}, u32[]{:S(2)}, u32[]{:S(2)}) collective-permute-start(bf16[32,32,128]{2,1,0:T(8,128)(2,1)S(1)} %slice.85), channel_id=1, source_target_pairs={{0,24},{8,16},{16,8},{24,0},{1,25},{9,17},{17,9},{25,1},{2,26},{10... | collective-permute-start | bytes 786440 | tf_op jit(solution)/shard_map/ppermute | solution.py:276
  63.4 14.3 %collective-permute-start.17 = (bf16[32,32,128]{2,1,0:T(8,128)(2,1)S(1)}, bf16[32,32,128]{2,1,0:T(8,128)(2,1)S(1)}, u32[]{:S(2)}, u32[]{:S(2)}) collective-permute-start(bf16[32,32,128]{2,1,0:T(8,128)(2,1)S(1)} %slice.86), channel_id=1, source_target_pairs={{0,16},{8,24},{16,0},{24,8},{1,17},{9,25},{17,1},{25,9},{2,18},{10... | collective-permute-start | bytes 786440 | tf_op jit(solution)/shard_map/ppermute | solution.py:276
  64.0 13.9 %collective-permute-start.18 = (bf16[32,32,128]{2,1,0:T(8,128)(2,1)S(1)}, bf16[32,32,128]{2,1,0:T(8,128)(2,1)S(1)}, u32[]{:S(2)}, u32[]{:S(2)}) collective-permute-start(bf16[32,32,128]{2,1,0:T(8,128)(2,1)S(1)} %slice.87), channel_id=1, source_target_pairs={{0,8},{8,0},{16,24},{24,16},{1,9},{9,1},{17,25},{25,17},{2,10},{10... | collective-permute-start | bytes 786440 | tf_op jit(solution)/shard_map/ppermute | solution.py:276

commit v4 on v3

--- a/solution.py
+++ b/solution.py
@@ -23,7 +23,7 @@
         self.chips = chips
         self.sizes = [count // n for n in PARTS]
         self.starts = [sum(self.sizes[:i]) for i in range(len(PARTS))]
-        self.pairs = [((n + min(sectors, n)) // 2 + DEPTH - 1) // DEPTH * DEPTH for n in self.sizes]
+        self.pairs = [((n + min(sectors, n) + 2) // 2 + DEPTH - 1) // DEPTH * DEPTH for n in self.sizes]
         self.firsts = [sum(self.pairs[:i]) for i in range(len(PARTS))]
         self.all_pairs = sum(self.pairs)
         self.far = chips // 2 if chips % 2 == 0 else chips
@@ -88,7 +88,7 @@
             pair, filled, before = carry
             k = lists[at.origin + start + i]
             left, right = lsec[k], rsec[k]
-            same = (filled == 1) & (left == before)
+            same = (filled == 1) & (left == before) & (i != size // 2)
             pair = jnp.where(same, pair, pair + 1)
             filled = jnp.where(same, 2, 1)
             half = 2 * pair + filled - 1
@@ -118,10 +118,9 @@
         lax.fori_loop(0, groups, fill, 0)
 
 
-def multiply_kernel(part, at, place, lists, halves, right, left, *rest):
-    outs, inner = rest[:-1], rest[-1]
+def multiply_kernel(part, at, place, lists, halves, right, left, own, ahead, later, inner):
     width = halves.shape[1]
-    rows = outs[0].shape[1]
+    rows = own.shape[1]
     channels = left.shape[1]
     first = at.firsts[part]
     groups = lists[at.groups + part]
@@ -143,16 +142,20 @@
         for u in range(DEPTH):
             pair = first + group * DEPTH + u
             slot = lists[at.left + pair]
+            second = lists[at.position + 2 * pair] >= at.sizes[part] // 2
+            ways = (0, jnp.where(second, 2, 1), 3, jnp.where(second, 1, 2))
             wide = []
-            for d in range(len(outs)):
-                start = pl.multiple_of((place[2] ^ d) * rows, rows)
+            for way in ways:
+                start = pl.multiple_of((place[2] ^ way) * rows, rows)
                 wide.append(jnp.concatenate([left[slot, w, pl.ds(start, rows), :] for w in range(channels)], axis=1))
             wide = jnp.concatenate(wide, axis=0)
             result = jnp.dot(wide, inner[side * DEPTH + u], preferred_element_type=jnp.float32).astype(jnp.bfloat16)
             for h in range(2):
                 where = lists[at.position + 2 * pair + h]
-                for d, out in enumerate(outs):
-                    out[where] = result[d * rows:(d + 1) * rows, h * width:(h + 1) * width]
+                columns = slice(h * width, (h + 1) * width)
+                own[where] = result[0:rows, columns]
+                ahead[where] = result[rows:3 * rows, columns]
+                later[where] = result[3 * rows:4 * rows, columns]
 
     def body(i, carry):
         one(2 * i + 1, 1)
@@ -182,7 +185,8 @@
     row = place[2] * rows + lax.broadcasted_iota(jnp.int32, (rows, width), 0)
     col = lax.broadcasted_iota(jnp.int32, (rows, width), 1)
 
-    for start, total in zip(at.starts, totals):
+    starts = [sum(t.shape[0] for t in totals[:i]) for i in range(len(totals))]
+    for start, total in zip(starts, totals):
         def body(i, carry):
             blocks = []
             for u in range(BATCH):
@@ -262,20 +266,29 @@
         need = 2 * (need + 4 * DEPTH * channels * width * width) + (8 << 20)
         return list(pl.pallas_call(
             functools.partial(multiply_kernel, part, at),
-            out_shape=[jax.ShapeDtypeStruct((at.sizes[part] + 1, rows, width), jnp.bfloat16)] * nenv,
+            out_shape=[
+                jax.ShapeDtypeStruct((at.sizes[part] + 1, n * rows, width), jnp.bfloat16) for n in (1, 2, 1)
+            ],
             in_specs=[SMEM] * 2 + [VMEM] * 3,
-            out_specs=[VMEM] * nenv,
+            out_specs=[VMEM] * 3,
             scratch_shapes=[pltpu.VMEM((2 * DEPTH, channels * width, 2 * width), jnp.bfloat16)],
             compiler_params=pltpu.CompilerParams(vmem_limit_bytes=min(need, 60 << 20)),
             cost_estimate=NO_COST,
         )(place, lists, halves, right, left))
 
-    def exchange(parts):
-        total = parts[0][:-1].astype(jnp.float32)
-        for d in range(nenv - 1, 0, -1):
-            arrived = lax.ppermute(parts[d][:-1], "env", [(i, i ^ d) for i in range(nenv)])
-            total = total + arrived.astype(jnp.float32)
-        return total.astype(jnp.bfloat16)
+    def pass_on(x, d):
+        return lax.ppermute(x, "env", [(i, i ^ d) for i in range(nenv)])
+
+    def exchange(part, parts):
+        own, ahead, later = parts
+        middle, end = at.sizes[part] // 2, at.sizes[part]
+        wide = lambda x: x.astype(jnp.float32)
+        totals = []
+        arrived = [pass_on(ahead[0:middle], 1), pass_on(ahead[middle:end], 2)]
+        for (lo, hi), first, d in zip(((0, middle), (middle, end)), arrived, (2, 1)):
+            second = pass_on((wide(later[lo:hi]) + wide(first[:, rows:])).astype(jnp.bfloat16), d)
+            totals.append((wide(own[lo:hi]) + wide(first[:, :rows]) + wide(second)).astype(jnp.bfloat16))
+        return totals
 
     parts = multiply(0, right, near)
     if chips % 2 == 0:
@@ -283,9 +296,9 @@
         whole = jnp.concatenate([near, jnp.stack(far_pieces(last))])
     else:
         whole = near
-    terms = [exchange(parts)]
+    terms = exchange(0, parts)
     for part in range(1, len(PARTS)):
-        terms.append(exchange(multiply(part, right, whole)))
+        terms += exchange(part, multiply(part, right, whole))
     return pl.pallas_call(
         functools.partial(place_kernel, at),
         out_shape=jax.ShapeDtypeStruct((count, rows, width), jnp.bfloat16),

time: 79.8 us -> 78.2 us (0.980)
  waiting for transfers between devices: 31 us -> 26.6 us
  starting transfers between devices: 18.2 us -> 20.2 us
  Pallas kernels: 22.5 us -> 23.4 us
    ppermute x6 -> x8, waiting for transfers between devices: 13.1 us -> 8.89 us  [pass_on(): return lax.ppermute(x, 'env', [(i, i ^ d) for i in range(nenv)])]
    ppermute x6 -> x8, starting transfers between devices: 7.37 us -> 9.29 us  [pass_on(): return lax.ppermute(x, 'env', [(i, i ^ d) for i in range(nenv)])]
  transfers between devices with their start and end apart: 19 -> 21, of which waited for: 9 -> 10; matrix products, arithmetic and copies ran while one was open for 2% -> 3% of each run, Pallas kernels for 26% -> 28%
where the time goes in v4:
time: 78.2 us; the launch traced here: 78 us
  waiting for transfers between devices  26.6 us (34%)
  Pallas kernels  23.4 us (30%)
  starting transfers between devices  20.2 us (26%)
  local copies, waits for them, and re-layouts  5.75 us (7%)
  other arithmetic  1.83 us (2%)
    ppermute x1, waiting for transfers between devices, ring(): falling = lax.ppermute(falling, 'wave', down)  12.7 us
    pallas_call x2, Pallas kernels, multiply(): pl.pallas_call(functools.partial(multiply_kernel, part, at), out_shape=[j...  12.6 us
    ppermute x8, starting transfers between devices, pass_on(): return lax.ppermute(x, 'env', [(i, i ^ d) for i in range(nenv)])  9.29 us
    pallas_call x1, Pallas kernels, on_device(): pl.pallas_call(functools.partial(order_kernel, at), out_shape=(jax.ShapeD...  9.26 us
    ppermute x8, waiting for transfers between devices, pass_on(): return lax.ppermute(x, 'env', [(i, i ^ d) for i in range(nenv)])  8.89 us
    unnamed x20, local copies, waits for them, and re-layouts  5.63 us
    ppermute x2, starting transfers between devices, far(): lax.ppermute(falling[mid:hi], 'wave', down)  3.32 us
    ppermute x1, starting transfers between devices, ring(): rising = lax.ppermute(rising, 'wave', up)  3.08 us
  transfers between devices with their start and end apart: 21, of which 10 were waited for; matrix products, arithmetic and copies ran while one was open for 3% of the time, Pallas kernels for 28%

profile of v4, /device:TPU:0, one launch (start us, length us, event | category | flops | bytes accessed | tf_op | source)
XLA Modules:
  0.0 78.0 jit_solution(15597600352842791222)
XLA Ops:
  0.0 1.2 %pad_maximum_fusion = bf16[20,128,128]{2,1,0:T(8,128)(2,1)S(1)} fusion(bf16[10,128,128]{2,1,0:T(8,128)(2,1)} %bitcast.80, bf16[10,128,128]{2,1,0:T(8,128)(2,1)} %bitcast.81), kind=kLoop, calls=%fused_computation | loop fusion | flops 327680 | bytes 1310720 | tf_op jit(solution)/shard_map/concatenate | solution.py:243
  1.2 3.1 %collective-permute-start.3 = (bf16[20,128,128]{2,1,0:T(8,128)(2,1)S(1)}, bf16[20,128,128]{2,1,0:T(8,128)(2,1)S(1)}, u32[]{:S(2)}, u32[]{:S(2)}) collective-permute-start(bf16[20,128,128]{2,1,0:T(8,128)(2,1)S(1)} %pad_maximum_fusion), channel_id=1, source_target_pairs={{0,2},{1,3},{2,4},{3,5},{4,6},{5,7},{6,0},{7,1},{8,10},{9,11},{10,... | collective-permute-start | bytes 1966088 | tf_op jit(solution)/shard_map/ppermute | solution.py:231
  4.3 2.1 %collective-permute-start.1 = (bf16[20,128,128]{2,1,0:T(8,128)(2,1)S(1)}, bf16[20,128,128]{2,1,0:T(8,128)(2,1)S(1)}, u32[]{:S(2)}, u32[]{:S(2)}) collective-permute-start(bf16[20,128,128]{2,1,0:T(8,128)(2,1)S(1)} %pad_maximum_fusion), channel_id=1, source_target_pairs={{2,0},{3,1},{4,2},{5,3},{6,4},{7,5},{0,6},{1,7},{10,8},{11,9},{12,... | collective-permute-start | bytes 1966088 | tf_op jit(solution)/shard_map/ppermute | solution.py:232
  6.4 0.1 pad_add_fusion.place
  6.5 1.6 %copy-done = bf16[64,128,128]{2,1,0:T(8,128)(2,1)S(1)} copy-done((bf16[64,128,128]{2,1,0:T(8,128)(2,1)S(1)}, bf16[64,128,128]{2,1,0:T(8,128)(2,1)}, u32[]{:S(2)}) %copy-start) | copy-done | bytes 2097176
  8.0 0.7 copy-done.1
  8.7 0.7 copy-done.2
  9.4 0.7 copy-done.3
  10.0 0.7 copy-done.4
  10.7 9.3 %shard_map.73 = (s32[414]{0:T(512)S(1)}, bf16[44,128,256]{2,1,0:T(8,128)(2,1)S(1)}) custom-call(s32[3]{0:T(128)S(1)} %pad_add_fusion.place, s32[64]{0:T(128)S(1)} %bitcast.78, s32[64]{0:T(128)S(1)} %bitcast.79, s32[8]{0:T(128)S(1)} %copy-done.3, s32[8]{0:T(128)S(1)} %copy-done.4, bf16[64,128,128]{2,1,0:T(8,128)(2,1)S(1)} %copy-done), custom_call_target="tpu_custom_call" | custom-call | tf_op jit(solution)/shard_map/pallas_call | solution.py:252
  20.0 0.2 bitcast_dynamic-update-slice_fusion
  20.1 1.8 %collective-permute-done.3 = bf16[20,128,128]{2,1,0:T(8,128)(2,1)S(1)} collective-permute-done((bf16[20,128,128]{2,1,0:T(8,128)(2,1)S(1)}, bf16[20,128,128]{2,1,0:T(8,128)(2,1)S(1)}, u32[]{:S(2)}, u32[]{:S(2)}) %collective-permute-start.3) | collective-permute-done | bytes 655392 | tf_op jit(solution)/shard_map/ppermute | solution.py:231
  22.0 12.7 %collective-permute-done.1 = bf16[20,128,128]{2,1,0:T(8,128)(2,1)S(1)} collective-permute-done((bf16[20,128,128]{2,1,0:T(8,128)(2,1)S(1)}, bf16[20,128,128]{2,1,0:T(8,128)(2,1)S(1)}, u32[]{:S(2)}, u32[]{:S(2)}) %collective-permute-start.1) | collective-permute-done | bytes 655392 | tf_op jit(solution)/shard_map/ppermute | solution.py:232
  34.8 3.1 %collective-permute-start.6 = (bf16[5,128,128]{2,1,0:T(8,128)(2,1)S(1)}, bf16[5,128,128]{2,1,0:T(8,128)(2,1)S(1)}, u32[]{:S(2)}, u32[]{:S(2)}) collective-permute-start(bf16[5,128,128]{2,1,0:T(8,128)(2,1)S(1)} %get-tuple-element.43), channel_id=1, source_target_pairs={{2,0},{3,1},{4,2},{5,3},{6,4},{7,5},{0,6},{1,7},{10,8},{11,9},{12,... | collective-permute-start | bytes 491528 | tf_op jit(solution)/shard_map/ppermute | solution.py:238
  37.9 0.2 collective-permute-start.10
  38.1 0.1 collective-permute-start.4
  38.2 0.2 fusion.9
  38.4 0.2 fusion.11
  38.7 0.7 collective-permute-done.5
  39.3 1.1 %collective-permute-start.9 = (bf16[5,128,128]{2,1,0:T(8,128)(2,1)S(1)}, bf16[5,128,128]{2,1,0:T(8,128)(2,1)S(1)}, u32[]{:S(2)}, u32[]{:S(2)}) collective-permute-start(bf16[5,128,128]{2,1,0:T(8,128)(2,1)S(1)} %get-tuple-element.44), channel_id=1, source_target_pairs={{0,2},{1,3},{2,4},{3,5},{4,6},{5,7},{6,0},{7,1},{8,10},{9,11},{10,... | collective-permute-start | bytes 491528 | tf_op jit(solution)/shard_map/ppermute | solution.py:238
  40.5 2.3 %collective-permute-done.6 = bf16[5,128,128]{2,1,0:T(8,128)(2,1)S(1)} collective-permute-done((bf16[5,128,128]{2,1,0:T(8,128)(2,1)S(1)}, bf16[5,128,128]{2,1,0:T(8,128)(2,1)S(1)}, u32[]{:S(2)}, u32[]{:S(2)}) %collective-permute-start.6) | collective-permute-done | bytes 163872 | tf_op jit(solution)/shard_map/ppermute | solution.py:238
  42.8 0.5 collective-permute-start.8
  43.3 0.2 fusion.13
  43.6 0.2 fusion.15
  43.8 0.2 fusion.17
  44.2 0.2 collective-permute-done.8
  44.5 6.3 %shard_map.74 = (bf16[33,32,128]{2,1,0:T(8,128)(2,1)S(1)}, bf16[33,64,128]{2,1,0:T(8,128)(2,1)S(1)}, bf16[33,32,128]{2,1,0:T(8,128)(2,1)S(1)}) custom-call(s32[3]{0:T(128)S(1)} %pad_add_fusion.place, s32[414]{0:T(512)S(1)} %get-tuple-element.16.lists, bf16[44,128,256]{2,1,0:T(8,128)(2,1)S(1)} %get-tuple-element.17.halves, ...), custom_call_target="tpu_custom_call" | custom-call | tf_op jit(solution)/shard_map/pallas_call | solution.py:267
  50.8 0.3 collective-permute-start.15
  51.1 0.2 collective-permute-start.16
  51.4 1.5 %collective-permute-start.11 = (bf16[16,64,128]{2,1,0:T(8,128)(2,1)S(1)}, bf16[16,64,128]{2,1,0:T(8,128)(2,1)S(1)}, u32[]{:S(2)}, u32[]{:S(2)}) collective-permute-start(bf16[16,64,128]{2,1,0:T(8,128)(2,1)S(1)} %get-tuple-element.49), channel_id=1, source_target_pairs={{0,8},{8,0},{16,24},{24,16},{1,9},{9,1},{17,25},{25,17},{2,10},{10... | collective-permute-start | bytes 786440 | tf_op jit(solution)/shard_map/ppermute | solution.py:280
  52.9 1.5 %collective-permute-start.13 = (bf16[16,64,128]{2,1,0:T(8,128)(2,1)S(1)}, bf16[16,64,128]{2,1,0:T(8,128)(2,1)S(1)}, u32[]{:S(2)}, u32[]{:S(2)}) collective-permute-start(bf16[16,64,128]{2,1,0:T(8,128)(2,1)S(1)} %get-tuple-element.48), channel_id=1, source_target_pairs={{0,16},{8,24},{16,0},{24,8},{1,17},{9,25},{17,1},{25,9},{2,18},{10... | collective-permute-start | bytes 786440 | tf_op jit(solution)/shard_map/ppermute | solution.py:280
  54.6 6.3 %shard_map.75 = (bf16[33,32,128]{2,1,0:T(8,128)(2,1)S(1)}, bf16[33,64,128]{2,1,0:T(8,128)(2,1)S(1)}, bf16[33,32,128]{2,1,0:T(8,128)(2,1)S(1)}) custom-call(s32[3]{0:T(128)S(1)} %pad_add_fusion.place, s32[414]{0:T(512)S(1)} %get-tuple-element.16.lists, bf16[44,128,256]{2,1,0:T(8,128)(2,1)S(1)} %get-tuple-element.17.halves, ...), custom_call_target="tpu_custom_call" | custom-call | tf_op jit(solution)/shard_map/pallas_call | solution.py:267
  60.9 0.6 collective-permute-start.17
  61.5 0.5 collective-permute-start.19
  62.0 0.1 add_convert_fusion.5
  62.1 1.6 %collective-permute-start.12 = (bf16[16,32,128]{2,1,0:T(8,128)(2,1)S(1)}, bf16[16,32,128]{2,1,0:T(8,128)(2,1)S(1)}, u32[]{:S(2)}, u32[]{:S(2)}) collective-permute-start(bf16[16,32,128]{2,1,0:T(8,128)(2,1)S(1)} %get-tuple-element.59), channel_id=1, source_target_pairs={{0,16},{8,24},{16,0},{24,8},{1,17},{9,25},{17,1},{25,9},{2,18},{10... | collective-permute-start | bytes 393224 | tf_op jit(solution)/shard_map/ppermute | solution.py:280
  63.7 1.5 %collective-permute-start.14 = (bf16[16,32,128]{2,1,0:T(8,128)(2,1)S(1)}, bf16[16,32,128]{2,1,0:T(8,128)(2,1)S(1)}, u32[]{:S(2)}, u32[]{:S(2)}) collective-permute-start(bf16[16,32,128]{2,1,0:T(8,128)(2,1)S(1)} %get-tuple-element.58), channel_id=1, source_target_pairs={{0,8},{8,0},{16,24},{24,16},{1,9},{9,1},{17,25},{25,17},{2,10},{10... | collective-permute-start | bytes 393224 | tf_op jit(solution)/shard_map/ppermute | solution.py:280
  65.2 5.0 %collective-permute-done.17 = bf16[16,64,128]{2,1,0:T(8,128)(2,1)S(1)} collective-permute-done((bf16[16,64,128]{2,1,0:T(8,128)(2,1)S(1)}, bf16[16,64,128]{2,1,0:T(8,128)(2,1)S(1)}, u32[]{:S(2)}, u32[]{:S(2)}) %collective-permute-start.17) | collective-permute-done | bytes 262176 | tf_op jit(solution)/shard_map/ppermute | solution.py:280
  70.2 0.4 collective-permute-done.19
  70.6 0.1 add_convert_fusion.1
  70.7 0.7 collective-permute-start.18
  71.4 1.4 %collective-permute-start.20 = (bf16[16,32,128]{2,1,0:T(8,128)(2,1)S(1)}, bf16[16,32,128]{2,1,0:T(8,128)(2,1)S(1)}, u32[]{:S(2)}, u32[]{:S(2)}) collective-permute-start(bf16[16,32,128]{2,1,0:T(8,128)(2,1)S(1)} %get-tuple-element.54), channel_id=1, source_target_pairs={{0,8},{8,0},{16,24},{24,16},{1,9},{9,1},{17,25},{25,17},{2,10},{10... | collective-permute-start | bytes 393224 | tf_op jit(solution)/shard_map/ppermute | solution.py:280
  72.7 0.7 collective-permute-done.12
  73.4 0.1 add_convert_fusion.4
  73.5 2.2 %collective-permute-done.18 = bf16[16,32,128]{2,1,0:T(8,128)(2,1)S(1)} collective-permute-done((bf16[16,32,128]{2,1,0:T(8,128)(2,1)S(1)}, bf16[16,32,128]{2,1,0:T(8,128)(2,1)S(1)}, u32[]{:S(2)}, u32[]{:S(2)}) %collective-permute-start.18) | collective-permute-done | bytes 131104 | tf_op jit(solution)/shard_map/ppermute | solution.py:280
  75.7 0.6 collective-permute-done.20
  76.3 0.1 add_convert_fusion
  76.5 1.6 %shard_map.76 = bf16[64,32,128]{2,1,0:T(8,128)(2,1)} custom-call(s32[3]{0:T(128)S(1)} %pad_add_fusion.place, s32[414]{0:T(512)S(1)} %get-tuple-element.16.lists, bf16[16,32,128]{2,1,0:T(8,128)(2,1)S(1)} %get-tuple-element.57.rest_0_, bf16[16,32,128]{2,1,0:T(8,128)(2,1)S(1)} %get-tuple-element.56.rest_1_, bf16[16,32,128]{2,1,0:T(8,128)(2,1)S(1)} %get-tuple-element.53.rest_2_, ...), custom_call_target="tpu_custom_call" | custom-call | tf_op jit(solution)/shard_map/pallas_call | solution.py:302
  (32 shorter events, 0.5 us)
Async XLA Ops:
  0.0 19.9 %copy-start.6 = (bf16[10,1,128,128]{3,2,1,0:T(8,128)(2,1)S(1)}, bf16[10,1,128,128]{3,2,1,0:T(8,128)(2,1)}, u32[]{:S(2)}) copy-start(bf16[10,1,128,128]{3,2,1,0:T(8,128)(2,1)} %param.9) | copy-start | bytes 983044
  0.0 19.9 %copy-start.5 = (bf16[10,1,128,128]{3,2,1,0:T(8,128)(2,1)S(1)}, bf16[10,1,128,128]{3,2,1,0:T(8,128)(2,1)}, u32[]{:S(2)}) copy-start(bf16[10,1,128,128]{3,2,1,0:T(8,128)(2,1)} %param.8) | copy-start | bytes 983044
  1.2 20.7 %collective-permute-start.3 = (bf16[20,128,128]{2,1,0:T(8,128)(2,1)S(1)}, bf16[20,128,128]{2,1,0:T(8,128)(2,1)S(1)}, u32[]{:S(2)}, u32[]{:S(2)}) collective-permute-start(bf16[20,128,128]{2,1,0:T(8,128)(2,1)S(1)} %pad_maximum_fusion), channel_id=1, source_target_pairs={{0,2},{1,3},{2,4},{3,5},{4,6},{5,7},{6,0},{7,1},{8,10},{9,11},{10,... | collective-permute-start | bytes 1966088 | tf_op jit(solution)/shard_map/ppermute | solution.py:231
  4.3 30.5 %collective-permute-start.1 = (bf16[20,128,128]{2,1,0:T(8,128)(2,1)S(1)}, bf16[20,128,128]{2,1,0:T(8,128)(2,1)S(1)}, u32[]{:S(2)}, u32[]{:S(2)}) collective-permute-start(bf16[20,128,128]{2,1,0:T(8,128)(2,1)S(1)} %pad_maximum_fusion), channel_id=1, source_target_pairs={{2,0},{3,1},{4,2},{5,3},{6,4},{7,5},{0,6},{1,7},{10,8},{11,9},{12,... | collective-permute-start | bytes 1966088 | tf_op jit(solution)/shard_map/ppermute | solution.py:232
  6.4 31.7 %collective-permute-start = (bf16[20,128,128]{2,1,0:T(8,128)(2,1)S(1)}, bf16[20,128,128]{2,1,0:T(8,128)(2,1)S(1)}, u32[]{:S(2)}, u32[]{:S(2)}) collective-permute-start(bf16[20,128,128]{2,1,0:T(8,128)(2,1)S(1)} %pad_maximum_fusion), channel_id=1, source_target_pairs={{0,1},{1,0},{2,3},{3,2},{4,5},{5,4},{6,7},{7,6},{8,9},{9,8},{10,11... | collective-permute-start | bytes 1966088 | tf_op jit(solution)/shard_map/ppermute | solution.py:222
  6.5 1.6 %copy-start = (bf16[64,128,128]{2,1,0:T(8,128)(2,1)S(1)}, bf16[64,128,128]{2,1,0:T(8,128)(2,1)}, u32[]{:S(2)}) copy-start(bf16[64,128,128]{2,1,0:T(8,128)(2,1)} %psi.1) | copy-start | bytes 6291460
  8.0 0.7 copy-start.1
  8.7 0.7 copy-start.2
  9.4 0.7 copy-start.3
  10.0 0.7 copy-start.4
  21.9 17.4 %collective-permute-start.5 = (bf16[5,128,128]{2,1,0:T(8,128)(2,1)S(1)}, bf16[5,128,128]{2,1,0:T(8,128)(2,1)S(1)}, u32[]{:S(2)}, u32[]{:S(2)}) collective-permute-start(bf16[5,128,128]{2,1,0:T(8,128)(2,1)S(1)} %get-tuple-element.45), channel_id=1, source_target_pairs={{0,2},{1,3},{2,4},{3,5},{4,6},{5,7},{6,0},{7,1},{8,10},{9,11},{10,... | collective-permute-start | bytes 491528 | tf_op jit(solution)/shard_map/ppermute | solution.py:238
  34.7 8.1 %collective-permute-start.2 = (bf16[20,128,128]{2,1,0:T(8,128)(2,1)S(1)}, bf16[20,128,128]{2,1,0:T(8,128)(2,1)S(1)}, u32[]{:S(2)}, u32[]{:S(2)}) collective-permute-start(bf16[20,128,128]{2,1,0:T(8,128)(2,1)S(1)} %collective-permute-done.1), channel_id=1, source_target_pairs={{0,1},{1,0},{2,3},{3,2},{4,5},{5,4},{6,7},{7,6},{8,9},{9,8},{10,11... | collective-permute-start | bytes 1966088 | tf_op jit(solution)/shard_map/ppermute | solution.py:222
  34.8 8.0 %collective-permute-start.6 = (bf16[5,128,128]{2,1,0:T(8,128)(2,1)S(1)}, bf16[5,128,128]{2,1,0:T(8,128)(2,1)S(1)}, u32[]{:S(2)}, u32[]{:S(2)}) collective-permute-start(bf16[5,128,128]{2,1,0:T(8,128)(2,1)S(1)} %get-tuple-element.43), channel_id=1, source_target_pairs={{2,0},{3,1},{4,2},{5,3},{6,4},{7,5},{0,6},{1,7},{10,8},{11,9},{12,... | collective-permute-start | bytes 491528 | tf_op jit(solution)/shard_map/ppermute | solution.py:238
  37.9 12.9 %collective-permute-start.10 = (bf16[5,128,128]{2,1,0:T(8,128)(2,1)S(1)}, bf16[5,128,128]{2,1,0:T(8,128)(2,1)S(1)}, u32[]{:S(2)}, u32[]{:S(2)}) collective-permute-start(bf16[5,128,128]{2,1,0:T(8,128)(2,1)S(1)} %get-tuple-element.42), channel_id=1, source_target_pairs={{2,0},{3,1},{4,2},{5,3},{6,4},{7,5},{0,6},{1,7},{10,8},{11,9},{12,... | collective-permute-start | bytes 491528 | tf_op jit(solution)/shard_map/ppermute | solution.py:238
  38.1 5.7 %collective-permute-start.4 = (bf16[20,128,128]{2,1,0:T(8,128)(2,1)S(1)}, bf16[20,128,128]{2,1,0:T(8,128)(2,1)S(1)}, u32[]{:S(2)}, u32[]{:S(2)}) collective-permute-start(bf16[20,128,128]{2,1,0:T(8,128)(2,1)S(1)} %collective-permute-done.3), channel_id=1, source_target_pairs={{0,1},{1,0},{2,3},{3,2},{4,5},{5,4},{6,7},{7,6},{8,9},{9,8},{10,11... | collective-permute-start | bytes 1966088 | tf_op jit(solution)/shard_map/ppermute | solution.py:222
  39.3 11.4 %collective-permute-start.9 = (bf16[5,128,128]{2,1,0:T(8,128)(2,1)S(1)}, bf16[5,128,128]{2,1,0:T(8,128)(2,1)S(1)}, u32[]{:S(2)}, u32[]{:S(2)}) collective-permute-start(bf16[5,128,128]{2,1,0:T(8,128)(2,1)S(1)} %get-tuple-element.44), channel_id=1, source_target_pairs={{0,2},{1,3},{2,4},{3,5},{4,6},{5,7},{6,0},{7,1},{8,10},{9,11},{10,... | collective-permute-start | bytes 491528 | tf_op jit(solution)/shard_map/ppermute | solution.py:238
  42.8 1.4 %collective-permute-start.7 = (bf16[5,128,128]{2,1,0:T(8,128)(2,1)S(1)}, bf16[5,128,128]{2,1,0:T(8,128)(2,1)S(1)}, u32[]{:S(2)}, u32[]{:S(2)}) collective-permute-start(bf16[5,128,128]{2,1,0:T(8,128)(2,1)S(1)} %collective-permute-done.5), channel_id=1, source_target_pairs={{0,1},{1,0},{2,3},{3,2},{4,5},{5,4},{6,7},{7,6},{8,9},{9,8},{10,11... | collective-permute-start | bytes 491528 | tf_op jit(solution)/shard_map/ppermute | solution.py:222
  42.8 1.6 %collective-permute-start.8 = (bf16[5,128,128]{2,1,0:T(8,128)(2,1)S(1)}, bf16[5,128,128]{2,1,0:T(8,128)(2,1)S(1)}, u32[]{:S(2)}, u32[]{:S(2)}) collective-permute-start(bf16[5,128,128]{2,1,0:T(8,128)(2,1)S(1)} %collective-permute-done.6), channel_id=1, source_target_pairs={{0,1},{1,0},{2,3},{3,2},{4,5},{5,4},{6,7},{7,6},{8,9},{9,8},{10,11... | collective-permute-start | bytes 491528 | tf_op jit(solution)/shard_map/ppermute | solution.py:222
  50.8 3.7 %collective-permute-start.15 = (bf16[5,128,128]{2,1,0:T(8,128)(2,1)S(1)}, bf16[5,128,128]{2,1,0:T(8,128)(2,1)S(1)}, u32[]{:S(2)}, u32[]{:S(2)}) collective-permute-start(bf16[5,128,128]{2,1,0:T(8,128)(2,1)S(1)} %collective-permute-done.9), channel_id=1, source_target_pairs={{0,1},{1,0},{2,3},{3,2},{4,5},{5,4},{6,7},{7,6},{8,9},{9,8},{10,11... | collective-permute-start | bytes 491528 | tf_op jit(solution)/shard_map/ppermute | solution.py:222
  51.1 3.4 %collective-permute-start.16 = (bf16[5,128,128]{2,1,0:T(8,128)(2,1)S(1)}, bf16[5,128,128]{2,1,0:T(8,128)(2,1)S(1)}, u32[]{:S(2)}, u32[]{:S(2)}) collective-permute-start(bf16[5,128,128]{2,1,0:T(8,128)(2,1)S(1)} %collective-permute-done.10), channel_id=1, source_target_pairs={{0,1},{1,0},{2,3},{3,2},{4,5},{5,4},{6,7},{7,6},{8,9},{9,8},{10,11... | collective-permute-start | bytes 491528 | tf_op jit(solution)/shard_map/ppermute | solution.py:222
  51.4 10.6 %collective-permute-start.11 = (bf16[16,64,128]{2,1,0:T(8,128)(2,1)S(1)}, bf16[16,64,128]{2,1,0:T(8,128)(2,1)S(1)}, u32[]{:S(2)}, u32[]{:S(2)}) collective-permute-start(bf16[16,64,128]{2,1,0:T(8,128)(2,1)S(1)} %get-tuple-element.49), channel_id=1, source_target_pairs={{0,8},{8,0},{16,24},{24,16},{1,9},{9,1},{17,25},{25,17},{2,10},{10... | collective-permute-start | bytes 786440 | tf_op jit(solution)/shard_map/ppermute | solution.py:280
  52.9 9.1 %collective-permute-start.13 = (bf16[16,64,128]{2,1,0:T(8,128)(2,1)S(1)}, bf16[16,64,128]{2,1,0:T(8,128)(2,1)S(1)}, u32[]{:S(2)}, u32[]{:S(2)}) collective-permute-start(bf16[16,64,128]{2,1,0:T(8,128)(2,1)S(1)} %get-tuple-element.48), channel_id=1, source_target_pairs={{0,16},{8,24},{16,0},{24,8},{1,17},{9,25},{17,1},{25,9},{2,18},{10... | collective-permute-start | bytes 786440 | tf_op jit(solution)/shard_map/ppermute | solution.py:280
  60.9 9.3 %collective-permute-start.17 = (bf16[16,64,128]{2,1,0:T(8,128)(2,1)S(1)}, bf16[16,64,128]{2,1,0:T(8,128)(2,1)S(1)}, u32[]{:S(2)}, u32[]{:S(2)}) collective-permute-start(bf16[16,64,128]{2,1,0:T(8,128)(2,1)S(1)} %get-tuple-element.47), channel_id=1, source_target_pairs={{0,8},{8,0},{16,24},{24,16},{1,9},{9,1},{17,25},{25,17},{2,10},{10... | collective-permute-start | bytes 786440 | tf_op jit(solution)/shard_map/ppermute | solution.py:280
  61.5 9.1 %collective-permute-start.19 = (bf16[16,64,128]{2,1,0:T(8,128)(2,1)S(1)}, bf16[16,64,128]{2,1,0:T(8,128)(2,1)S(1)}, u32[]{:S(2)}, u32[]{:S(2)}) collective-permute-start(bf16[16,64,128]{2,1,0:T(8,128)(2,1)S(1)} %get-tuple-element.46), channel_id=1, source_target_pairs={{0,16},{8,24},{16,0},{24,8},{1,17},{9,25},{17,1},{25,9},{2,18},{10... | collective-permute-start | bytes 786440 | tf_op jit(solution)/shard_map/ppermute | solution.py:280
  62.1 11.3 %collective-permute-start.12 = (bf16[16,32,128]{2,1,0:T(8,128)(2,1)S(1)}, bf16[16,32,128]{2,1,0:T(8,128)(2,1)S(1)}, u32[]{:S(2)}, u32[]{:S(2)}) collective-permute-start(bf16[16,32,128]{2,1,0:T(8,128)(2,1)S(1)} %get-tuple-element.59), channel_id=1, source_target_pairs={{0,16},{8,24},{16,0},{24,8},{1,17},{9,25},{17,1},{25,9},{2,18},{10... | collective-permute-start | bytes 393224 | tf_op jit(solution)/shard_map/ppermute | solution.py:280
  63.7 9.7 %collective-permute-start.14 = (bf16[16,32,128]{2,1,0:T(8,128)(2,1)S(1)}, bf16[16,32,128]{2,1,0:T(8,128)(2,1)S(1)}, u32[]{:S(2)}, u32[]{:S(2)}) collective-permute-start(bf16[16,32,128]{2,1,0:T(8,128)(2,1)S(1)} %get-tuple-element.58), channel_id=1, source_target_pairs={{0,8},{8,0},{16,24},{24,16},{1,9},{9,1},{17,25},{25,17},{2,10},{10... | collective-permute-start | bytes 393224 | tf_op jit(solution)/shard_map/ppermute | solution.py:280
  70.7 5.0 %collective-permute-start.18 = (bf16[16,32,128]{2,1,0:T(8,128)(2,1)S(1)}, bf16[16,32,128]{2,1,0:T(8,128)(2,1)S(1)}, u32[]{:S(2)}, u32[]{:S(2)}) collective-permute-start(bf16[16,32,128]{2,1,0:T(8,128)(2,1)S(1)} %get-tuple-element.55), channel_id=1, source_target_pairs={{0,16},{8,24},{16,0},{24,8},{1,17},{9,25},{17,1},{25,9},{2,18},{10... | collective-permute-start | bytes 393224 | tf_op jit(solution)/shard_map/ppermute | solution.py:280
  71.4 5.0 %collective-permute-start.20 = (bf16[16,32,128]{2,1,0:T(8,128)(2,1)S(1)}, bf16[16,32,128]{2,1,0:T(8,128)(2,1)S(1)}, u32[]{:S(2)}, u32[]{:S(2)}) collective-permute-start(bf16[16,32,128]{2,1,0:T(8,128)(2,1)S(1)} %get-tuple-element.54), channel_id=1, source_target_pairs={{0,8},{8,0},{16,24},{24,16},{1,9},{9,1},{17,25},{25,17},{2,10},{10... | collective-permute-start | bytes 393224 | tf_op jit(solution)/shard_map/ppermute | solution.py:280

commit v5 on v4

--- a/solution.py
+++ b/solution.py
@@ -8,7 +8,7 @@
 from jax.sharding import PartitionSpec as P
 
 CORES = 2
-DEPTH = 2
+DEPTH = 3
 PARTS = (2, 2)
 BATCH = 8
 NO_COST = pl.CostEstimate(flops=0, bytes_accessed=0, transcendentals=0)

time: 78.2 us -> 77.6 us (level)
  transfers between devices with their start and end apart: 21 -> 21, of which waited for: 10 -> 10; matrix products, arithmetic and copies ran while one was open for 3% -> 3% of each run, Pallas kernels for 28% -> 27%
where the time goes in v5:
time: 77.6 us; the launch traced here: 77.4 us
  waiting for transfers between devices  26.7 us (34%)
  Pallas kernels  22.7 us (29%)
  starting transfers between devices  20.2 us (26%)
  local copies, waits for them, and re-layouts  5.75 us (7%)
  other arithmetic  1.83 us (2%)
    ppermute x1, waiting for transfers between devices, ring(): falling = lax.ppermute(falling, 'wave', down)  12.7 us
    pallas_call x2, Pallas kernels, multiply(): pl.pallas_call(functools.partial(multiply_kernel, part, at), out_shape=[j...  12 us
    ppermute x8, starting transfers between devices, pass_on(): return lax.ppermute(x, 'env', [(i, i ^ d) for i in range(nenv)])  9.29 us
    pallas_call x1, Pallas kernels, on_device(): pl.pallas_call(functools.partial(order_kernel, at), out_shape=(jax.ShapeD...  9.18 us
    ppermute x8, waiting for transfers between devices, pass_on(): return lax.ppermute(x, 'env', [(i, i ^ d) for i in range(nenv)])  8.89 us
    unnamed x20, local copies, waits for them, and re-layouts  5.63 us
    ppermute x2, starting transfers between devices, far(): lax.ppermute(falling[mid:hi], 'wave', down)  3.32 us
    ppermute x1, starting transfers between devices, ring(): rising = lax.ppermute(rising, 'wave', up)  3.08 us
  transfers between devices with their start and end apart: 21, of which 10 were waited for; matrix products, arithmetic and copies ran while one was open for 3% of the time, Pallas kernels for 27%

profile of v5, /device:TPU:0, one launch (start us, length us, event | category | flops | bytes accessed | tf_op | source)
XLA Modules:
  0.0 77.4 jit_solution(7060072985592729720)
XLA Ops:
  0.0 1.2 %pad_maximum_fusion = bf16[20,128,128]{2,1,0:T(8,128)(2,1)S(1)} fusion(bf16[10,128,128]{2,1,0:T(8,128)(2,1)} %bitcast.80, bf16[10,128,128]{2,1,0:T(8,128)(2,1)} %bitcast.81), kind=kLoop, calls=%fused_computation | loop fusion | flops 327680 | bytes 1310720 | tf_op jit(solution)/shard_map/concatenate | solution.py:243
  1.2 3.1 %collective-permute-start.3 = (bf16[20,128,128]{2,1,0:T(8,128)(2,1)S(1)}, bf16[20,128,128]{2,1,0:T(8,128)(2,1)S(1)}, u32[]{:S(2)}, u32[]{:S(2)}) collective-permute-start(bf16[20,128,128]{2,1,0:T(8,128)(2,1)S(1)} %pad_maximum_fusion), channel_id=1, source_target_pairs={{0,2},{1,3},{2,4},{3,5},{4,6},{5,7},{6,0},{7,1},{8,10},{9,11},{10,... | collective-permute-start | bytes 1966088 | tf_op jit(solution)/shard_map/ppermute | solution.py:231
  4.3 2.1 %collective-permute-start.1 = (bf16[20,128,128]{2,1,0:T(8,128)(2,1)S(1)}, bf16[20,128,128]{2,1,0:T(8,128)(2,1)S(1)}, u32[]{:S(2)}, u32[]{:S(2)}) collective-permute-start(bf16[20,128,128]{2,1,0:T(8,128)(2,1)S(1)} %pad_maximum_fusion), channel_id=1, source_target_pairs={{2,0},{3,1},{4,2},{5,3},{6,4},{7,5},{0,6},{1,7},{10,8},{11,9},{12,... | collective-permute-start | bytes 1966088 | tf_op jit(solution)/shard_map/ppermute | solution.py:232
  6.4 0.1 pad_add_fusion.place
  6.5 1.6 %copy-done = bf16[64,128,128]{2,1,0:T(8,128)(2,1)S(1)} copy-done((bf16[64,128,128]{2,1,0:T(8,128)(2,1)S(1)}, bf16[64,128,128]{2,1,0:T(8,128)(2,1)}, u32[]{:S(2)}) %copy-start) | copy-done | bytes 2097176
  8.0 0.7 copy-done.1
  8.7 0.7 copy-done.2
  9.4 0.7 copy-done.3
  10.0 0.7 copy-done.4
  10.7 9.2 %shard_map.73 = (s32[404]{0:T(512)S(1)}, bf16[42,128,256]{2,1,0:T(8,128)(2,1)S(1)}) custom-call(s32[3]{0:T(128)S(1)} %pad_add_fusion.place, s32[64]{0:T(128)S(1)} %bitcast.78, s32[64]{0:T(128)S(1)} %bitcast.79, s32[8]{0:T(128)S(1)} %copy-done.3, s32[8]{0:T(128)S(1)} %copy-done.4, bf16[64,128,128]{2,1,0:T(8,128)(2,1)S(1)} %copy-done), custom_call_target="tpu_custom_call" | custom-call | tf_op jit(solution)/shard_map/pallas_call | solution.py:252
  19.9 0.2 bitcast_dynamic-update-slice_fusion
  20.1 1.9 %collective-permute-done.3 = bf16[20,128,128]{2,1,0:T(8,128)(2,1)S(1)} collective-permute-done((bf16[20,128,128]{2,1,0:T(8,128)(2,1)S(1)}, bf16[20,128,128]{2,1,0:T(8,128)(2,1)S(1)}, u32[]{:S(2)}, u32[]{:S(2)}) %collective-permute-start.3) | collective-permute-done | bytes 655392 | tf_op jit(solution)/shard_map/ppermute | solution.py:231
  22.0 12.7 %collective-permute-done.1 = bf16[20,128,128]{2,1,0:T(8,128)(2,1)S(1)} collective-permute-done((bf16[20,128,128]{2,1,0:T(8,128)(2,1)S(1)}, bf16[20,128,128]{2,1,0:T(8,128)(2,1)S(1)}, u32[]{:S(2)}, u32[]{:S(2)}) %collective-permute-start.1) | collective-permute-done | bytes 655392 | tf_op jit(solution)/shard_map/ppermute | solution.py:232
  34.8 3.1 %collective-permute-start.6 = (bf16[5,128,128]{2,1,0:T(8,128)(2,1)S(1)}, bf16[5,128,128]{2,1,0:T(8,128)(2,1)S(1)}, u32[]{:S(2)}, u32[]{:S(2)}) collective-permute-start(bf16[5,128,128]{2,1,0:T(8,128)(2,1)S(1)} %get-tuple-element.43), channel_id=1, source_target_pairs={{2,0},{3,1},{4,2},{5,3},{6,4},{7,5},{0,6},{1,7},{10,8},{11,9},{12,... | collective-permute-start | bytes 491528 | tf_op jit(solution)/shard_map/ppermute | solution.py:238
  37.9 0.2 collective-permute-start.10
  38.1 0.1 collective-permute-start.4
  38.2 0.2 fusion.9
  38.4 0.2 fusion.11
  38.7 0.7 collective-permute-done.5
  39.3 1.1 %collective-permute-start.9 = (bf16[5,128,128]{2,1,0:T(8,128)(2,1)S(1)}, bf16[5,128,128]{2,1,0:T(8,128)(2,1)S(1)}, u32[]{:S(2)}, u32[]{:S(2)}) collective-permute-start(bf16[5,128,128]{2,1,0:T(8,128)(2,1)S(1)} %get-tuple-element.44), channel_id=1, source_target_pairs={{0,2},{1,3},{2,4},{3,5},{4,6},{5,7},{6,0},{7,1},{8,10},{9,11},{10,... | collective-permute-start | bytes 491528 | tf_op jit(solution)/shard_map/ppermute | solution.py:238
  40.5 2.3 %collective-permute-done.6 = bf16[5,128,128]{2,1,0:T(8,128)(2,1)S(1)} collective-permute-done((bf16[5,128,128]{2,1,0:T(8,128)(2,1)S(1)}, bf16[5,128,128]{2,1,0:T(8,128)(2,1)S(1)}, u32[]{:S(2)}, u32[]{:S(2)}) %collective-permute-start.6) | collective-permute-done | bytes 163872 | tf_op jit(solution)/shard_map/ppermute | solution.py:238
  42.8 0.5 collective-permute-start.8
  43.3 0.2 fusion.13
  43.6 0.2 fusion.15
  43.8 0.2 fusion.17
  44.2 0.2 collective-permute-done.8
  44.5 6.0 %shard_map.74 = (bf16[33,32,128]{2,1,0:T(8,128)(2,1)S(1)}, bf16[33,64,128]{2,1,0:T(8,128)(2,1)S(1)}, bf16[33,32,128]{2,1,0:T(8,128)(2,1)S(1)}) custom-call(s32[3]{0:T(128)S(1)} %pad_add_fusion.place, s32[404]{0:T(512)S(1)} %get-tuple-element.16.lists, bf16[42,128,256]{2,1,0:T(8,128)(2,1)S(1)} %get-tuple-element.17.halves, ...), custom_call_target="tpu_custom_call" | custom-call | tf_op jit(solution)/shard_map/pallas_call | solution.py:267
  50.5 0.3 collective-permute-start.15
  50.8 0.2 collective-permute-start.16
  51.1 1.5 %collective-permute-start.11 = (bf16[16,64,128]{2,1,0:T(8,128)(2,1)S(1)}, bf16[16,64,128]{2,1,0:T(8,128)(2,1)S(1)}, u32[]{:S(2)}, u32[]{:S(2)}) collective-permute-start(bf16[16,64,128]{2,1,0:T(8,128)(2,1)S(1)} %get-tuple-element.49), channel_id=1, source_target_pairs={{0,8},{8,0},{16,24},{24,16},{1,9},{9,1},{17,25},{25,17},{2,10},{10... | collective-permute-start | bytes 786440 | tf_op jit(solution)/shard_map/ppermute | solution.py:280
  52.6 1.5 %collective-permute-start.13 = (bf16[16,64,128]{2,1,0:T(8,128)(2,1)S(1)}, bf16[16,64,128]{2,1,0:T(8,128)(2,1)S(1)}, u32[]{:S(2)}, u32[]{:S(2)}) collective-permute-start(bf16[16,64,128]{2,1,0:T(8,128)(2,1)S(1)} %get-tuple-element.48), channel_id=1, source_target_pairs={{0,16},{8,24},{16,0},{24,8},{1,17},{9,25},{17,1},{25,9},{2,18},{10... | collective-permute-start | bytes 786440 | tf_op jit(solution)/shard_map/ppermute | solution.py:280
  54.3 6.0 %shard_map.75 = (bf16[33,32,128]{2,1,0:T(8,128)(2,1)S(1)}, bf16[33,64,128]{2,1,0:T(8,128)(2,1)S(1)}, bf16[33,32,128]{2,1,0:T(8,128)(2,1)S(1)}) custom-call(s32[3]{0:T(128)S(1)} %pad_add_fusion.place, s32[404]{0:T(512)S(1)} %get-tuple-element.16.lists, bf16[42,128,256]{2,1,0:T(8,128)(2,1)S(1)} %get-tuple-element.17.halves, ...), custom_call_target="tpu_custom_call" | custom-call | tf_op jit(solution)/shard_map/pallas_call | solution.py:267
  60.3 0.6 collective-permute-start.17
  60.9 0.5 collective-permute-start.19
  61.4 0.1 add_convert_fusion.5
  61.5 1.6 %collective-permute-start.12 = (bf16[16,32,128]{2,1,0:T(8,128)(2,1)S(1)}, bf16[16,32,128]{2,1,0:T(8,128)(2,1)S(1)}, u32[]{:S(2)}, u32[]{:S(2)}) collective-permute-start(bf16[16,32,128]{2,1,0:T(8,128)(2,1)S(1)} %get-tuple-element.59), channel_id=1, source_target_pairs={{0,16},{8,24},{16,0},{24,8},{1,17},{9,25},{17,1},{25,9},{2,18},{10... | collective-permute-start | bytes 393224 | tf_op jit(solution)/shard_map/ppermute | solution.py:280
  63.1 1.5 %collective-permute-start.14 = (bf16[16,32,128]{2,1,0:T(8,128)(2,1)S(1)}, bf16[16,32,128]{2,1,0:T(8,128)(2,1)S(1)}, u32[]{:S(2)}, u32[]{:S(2)}) collective-permute-start(bf16[16,32,128]{2,1,0:T(8,128)(2,1)S(1)} %get-tuple-element.58), channel_id=1, source_target_pairs={{0,8},{8,0},{16,24},{24,16},{1,9},{9,1},{17,25},{25,17},{2,10},{10... | collective-permute-start | bytes 393224 | tf_op jit(solution)/shard_map/ppermute | solution.py:280
  64.6 5.0 %collective-permute-done.17 = bf16[16,64,128]{2,1,0:T(8,128)(2,1)S(1)} collective-permute-done((bf16[16,64,128]{2,1,0:T(8,128)(2,1)S(1)}, bf16[16,64,128]{2,1,0:T(8,128)(2,1)S(1)}, u32[]{:S(2)}, u32[]{:S(2)}) %collective-permute-start.17) | collective-permute-done | bytes 262176 | tf_op jit(solution)/shard_map/ppermute | solution.py:280
  69.6 0.4 collective-permute-done.19
  70.0 0.1 add_convert_fusion.1
  70.1 0.7 collective-permute-start.18
  70.7 1.4 %collective-permute-start.20 = (bf16[16,32,128]{2,1,0:T(8,128)(2,1)S(1)}, bf16[16,32,128]{2,1,0:T(8,128)(2,1)S(1)}, u32[]{:S(2)}, u32[]{:S(2)}) collective-permute-start(bf16[16,32,128]{2,1,0:T(8,128)(2,1)S(1)} %get-tuple-element.54), channel_id=1, source_target_pairs={{0,8},{8,0},{16,24},{24,16},{1,9},{9,1},{17,25},{25,17},{2,10},{10... | collective-permute-start | bytes 393224 | tf_op jit(solution)/shard_map/ppermute | solution.py:280
  72.1 0.7 collective-permute-done.12
  72.8 0.1 add_convert_fusion.4
  72.9 2.2 %collective-permute-done.18 = bf16[16,32,128]{2,1,0:T(8,128)(2,1)S(1)} collective-permute-done((bf16[16,32,128]{2,1,0:T(8,128)(2,1)S(1)}, bf16[16,32,128]{2,1,0:T(8,128)(2,1)S(1)}, u32[]{:S(2)}, u32[]{:S(2)}) %collective-permute-start.18) | collective-permute-done | bytes 131104 | tf_op jit(solution)/shard_map/ppermute | solution.py:280
  75.1 0.6 collective-permute-done.20
  75.7 0.1 add_convert_fusion
  75.8 1.6 %shard_map.76 = bf16[64,32,128]{2,1,0:T(8,128)(2,1)} custom-call(s32[3]{0:T(128)S(1)} %pad_add_fusion.place, s32[404]{0:T(512)S(1)} %get-tuple-element.16.lists, bf16[16,32,128]{2,1,0:T(8,128)(2,1)S(1)} %get-tuple-element.57.rest_0_, bf16[16,32,128]{2,1,0:T(8,128)(2,1)S(1)} %get-tuple-element.56.rest_1_, bf16[16,32,128]{2,1,0:T(8,128)(2,1)S(1)} %get-tuple-element.53.rest_2_, ...), custom_call_target="tpu_custom_call" | custom-call | tf_op jit(solution)/shard_map/pallas_call | solution.py:302
  (32 shorter events, 0.5 us)
Async XLA Ops:
  0.0 19.9 %copy-start.6 = (bf16[10,1,128,128]{3,2,1,0:T(8,128)(2,1)S(1)}, bf16[10,1,128,128]{3,2,1,0:T(8,128)(2,1)}, u32[]{:S(2)}) copy-start(bf16[10,1,128,128]{3,2,1,0:T(8,128)(2,1)} %param.9) | copy-start | bytes 983044
  0.0 19.9 %copy-start.5 = (bf16[10,1,128,128]{3,2,1,0:T(8,128)(2,1)S(1)}, bf16[10,1,128,128]{3,2,1,0:T(8,128)(2,1)}, u32[]{:S(2)}) copy-start(bf16[10,1,128,128]{3,2,1,0:T(8,128)(2,1)} %param.8) | copy-start | bytes 983044
  1.2 20.7 %collective-permute-start.3 = (bf16[20,128,128]{2,1,0:T(8,128)(2,1)S(1)}, bf16[20,128,128]{2,1,0:T(8,128)(2,1)S(1)}, u32[]{:S(2)}, u32[]{:S(2)}) collective-permute-start(bf16[20,128,128]{2,1,0:T(8,128)(2,1)S(1)} %pad_maximum_fusion), channel_id=1, source_target_pairs={{0,2},{1,3},{2,4},{3,5},{4,6},{5,7},{6,0},{7,1},{8,10},{9,11},{10,... | collective-permute-start | bytes 1966088 | tf_op jit(solution)/shard_map/ppermute | solution.py:231
  4.3 30.5 %collective-permute-start.1 = (bf16[20,128,128]{2,1,0:T(8,128)(2,1)S(1)}, bf16[20,128,128]{2,1,0:T(8,128)(2,1)S(1)}, u32[]{:S(2)}, u32[]{:S(2)}) collective-permute-start(bf16[20,128,128]{2,1,0:T(8,128)(2,1)S(1)} %pad_maximum_fusion), channel_id=1, source_target_pairs={{2,0},{3,1},{4,2},{5,3},{6,4},{7,5},{0,6},{1,7},{10,8},{11,9},{12,... | collective-permute-start | bytes 1966088 | tf_op jit(solution)/shard_map/ppermute | solution.py:232
  6.4 31.7 %collective-permute-start = (bf16[20,128,128]{2,1,0:T(8,128)(2,1)S(1)}, bf16[20,128,128]{2,1,0:T(8,128)(2,1)S(1)}, u32[]{:S(2)}, u32[]{:S(2)}) collective-permute-start(bf16[20,128,128]{2,1,0:T(8,128)(2,1)S(1)} %pad_maximum_fusion), channel_id=1, source_target_pairs={{0,1},{1,0},{2,3},{3,2},{4,5},{5,4},{6,7},{7,6},{8,9},{9,8},{10,11... | collective-permute-start | bytes 1966088 | tf_op jit(solution)/shard_map/ppermute | solution.py:222
  6.5 1.6 %copy-start = (bf16[64,128,128]{2,1,0:T(8,128)(2,1)S(1)}, bf16[64,128,128]{2,1,0:T(8,128)(2,1)}, u32[]{:S(2)}) copy-start(bf16[64,128,128]{2,1,0:T(8,128)(2,1)} %psi.1) | copy-start | bytes 6291460
  8.0 0.7 copy-start.1
  8.7 0.7 copy-start.2
  9.4 0.7 copy-start.3
  10.0 0.7 copy-start.4
  21.9 17.4 %collective-permute-start.5 = (bf16[5,128,128]{2,1,0:T(8,128)(2,1)S(1)}, bf16[5,128,128]{2,1,0:T(8,128)(2,1)S(1)}, u32[]{:S(2)}, u32[]{:S(2)}) collective-permute-start(bf16[5,128,128]{2,1,0:T(8,128)(2,1)S(1)} %get-tuple-element.45), channel_id=1, source_target_pairs={{0,2},{1,3},{2,4},{3,5},{4,6},{5,7},{6,0},{7,1},{8,10},{9,11},{10,... | collective-permute-start | bytes 491528 | tf_op jit(solution)/shard_map/ppermute | solution.py:238
  34.7 8.1 %collective-permute-start.2 = (bf16[20,128,128]{2,1,0:T(8,128)(2,1)S(1)}, bf16[20,128,128]{2,1,0:T(8,128)(2,1)S(1)}, u32[]{:S(2)}, u32[]{:S(2)}) collective-permute-start(bf16[20,128,128]{2,1,0:T(8,128)(2,1)S(1)} %collective-permute-done.1), channel_id=1, source_target_pairs={{0,1},{1,0},{2,3},{3,2},{4,5},{5,4},{6,7},{7,6},{8,9},{9,8},{10,11... | collective-permute-start | bytes 1966088 | tf_op jit(solution)/shard_map/ppermute | solution.py:222
  34.8 8.0 %collective-permute-start.6 = (bf16[5,128,128]{2,1,0:T(8,128)(2,1)S(1)}, bf16[5,128,128]{2,1,0:T(8,128)(2,1)S(1)}, u32[]{:S(2)}, u32[]{:S(2)}) collective-permute-start(bf16[5,128,128]{2,1,0:T(8,128)(2,1)S(1)} %get-tuple-element.43), channel_id=1, source_target_pairs={{2,0},{3,1},{4,2},{5,3},{6,4},{7,5},{0,6},{1,7},{10,8},{11,9},{12,... | collective-permute-start | bytes 491528 | tf_op jit(solution)/shard_map/ppermute | solution.py:238
  37.9 12.6 %collective-permute-start.10 = (bf16[5,128,128]{2,1,0:T(8,128)(2,1)S(1)}, bf16[5,128,128]{2,1,0:T(8,128)(2,1)S(1)}, u32[]{:S(2)}, u32[]{:S(2)}) collective-permute-start(bf16[5,128,128]{2,1,0:T(8,128)(2,1)S(1)} %get-tuple-element.42), channel_id=1, source_target_pairs={{2,0},{3,1},{4,2},{5,3},{6,4},{7,5},{0,6},{1,7},{10,8},{11,9},{12,... | collective-permute-start | bytes 491528 | tf_op jit(solution)/shard_map/ppermute | solution.py:238
  38.1 5.7 %collective-permute-start.4 = (bf16[20,128,128]{2,1,0:T(8,128)(2,1)S(1)}, bf16[20,128,128]{2,1,0:T(8,128)(2,1)S(1)}, u32[]{:S(2)}, u32[]{:S(2)}) collective-permute-start(bf16[20,128,128]{2,1,0:T(8,128)(2,1)S(1)} %collective-permute-done.3), channel_id=1, source_target_pairs={{0,1},{1,0},{2,3},{3,2},{4,5},{5,4},{6,7},{7,6},{8,9},{9,8},{10,11... | collective-permute-start | bytes 1966088 | tf_op jit(solution)/shard_map/ppermute | solution.py:222
  39.3 11.1 %collective-permute-start.9 = (bf16[5,128,128]{2,1,0:T(8,128)(2,1)S(1)}, bf16[5,128,128]{2,1,0:T(8,128)(2,1)S(1)}, u32[]{:S(2)}, u32[]{:S(2)}) collective-permute-start(bf16[5,128,128]{2,1,0:T(8,128)(2,1)S(1)} %get-tuple-element.44), channel_id=1, source_target_pairs={{0,2},{1,3},{2,4},{3,5},{4,6},{5,7},{6,0},{7,1},{8,10},{9,11},{10,... | collective-permute-start | bytes 491528 | tf_op jit(solution)/shard_map/ppermute | solution.py:238
  42.8 1.4 %collective-permute-start.7 = (bf16[5,128,128]{2,1,0:T(8,128)(2,1)S(1)}, bf16[5,128,128]{2,1,0:T(8,128)(2,1)S(1)}, u32[]{:S(2)}, u32[]{:S(2)}) collective-permute-start(bf16[5,128,128]{2,1,0:T(8,128)(2,1)S(1)} %collective-permute-done.5), channel_id=1, source_target_pairs={{0,1},{1,0},{2,3},{3,2},{4,5},{5,4},{6,7},{7,6},{8,9},{9,8},{10,11... | collective-permute-start | bytes 491528 | tf_op jit(solution)/shard_map/ppermute | solution.py:222
  42.8 1.6 %collective-permute-start.8 = (bf16[5,128,128]{2,1,0:T(8,128)(2,1)S(1)}, bf16[5,128,128]{2,1,0:T(8,128)(2,1)S(1)}, u32[]{:S(2)}, u32[]{:S(2)}) collective-permute-start(bf16[5,128,128]{2,1,0:T(8,128)(2,1)S(1)} %collective-permute-done.6), channel_id=1, source_target_pairs={{0,1},{1,0},{2,3},{3,2},{4,5},{5,4},{6,7},{7,6},{8,9},{9,8},{10,11... | collective-permute-start | bytes 491528 | tf_op jit(solution)/shard_map/ppermute | solution.py:222
  50.5 3.7 %collective-permute-start.15 = (bf16[5,128,128]{2,1,0:T(8,128)(2,1)S(1)}, bf16[5,128,128]{2,1,0:T(8,128)(2,1)S(1)}, u32[]{:S(2)}, u32[]{:S(2)}) collective-permute-start(bf16[5,128,128]{2,1,0:T(8,128)(2,1)S(1)} %collective-permute-done.9), channel_id=1, source_target_pairs={{0,1},{1,0},{2,3},{3,2},{4,5},{5,4},{6,7},{7,6},{8,9},{9,8},{10,11... | collective-permute-start | bytes 491528 | tf_op jit(solution)/shard_map/ppermute | solution.py:222
  50.8 3.4 %collective-permute-start.16 = (bf16[5,128,128]{2,1,0:T(8,128)(2,1)S(1)}, bf16[5,128,128]{2,1,0:T(8,128)(2,1)S(1)}, u32[]{:S(2)}, u32[]{:S(2)}) collective-permute-start(bf16[5,128,128]{2,1,0:T(8,128)(2,1)S(1)} %collective-permute-done.10), channel_id=1, source_target_pairs={{0,1},{1,0},{2,3},{3,2},{4,5},{5,4},{6,7},{7,6},{8,9},{9,8},{10,11... | collective-permute-start | bytes 491528 | tf_op jit(solution)/shard_map/ppermute | solution.py:222
  51.1 10.3 %collective-permute-start.11 = (bf16[16,64,128]{2,1,0:T(8,128)(2,1)S(1)}, bf16[16,64,128]{2,1,0:T(8,128)(2,1)S(1)}, u32[]{:S(2)}, u32[]{:S(2)}) collective-permute-start(bf16[16,64,128]{2,1,0:T(8,128)(2,1)S(1)} %get-tuple-element.49), channel_id=1, source_target_pairs={{0,8},{8,0},{16,24},{24,16},{1,9},{9,1},{17,25},{25,17},{2,10},{10... | collective-permute-start | bytes 786440 | tf_op jit(solution)/shard_map/ppermute | solution.py:280
  52.6 8.8 %collective-permute-start.13 = (bf16[16,64,128]{2,1,0:T(8,128)(2,1)S(1)}, bf16[16,64,128]{2,1,0:T(8,128)(2,1)S(1)}, u32[]{:S(2)}, u32[]{:S(2)}) collective-permute-start(bf16[16,64,128]{2,1,0:T(8,128)(2,1)S(1)} %get-tuple-element.48), channel_id=1, source_target_pairs={{0,16},{8,24},{16,0},{24,8},{1,17},{9,25},{17,1},{25,9},{2,18},{10... | collective-permute-start | bytes 786440 | tf_op jit(solution)/shard_map/ppermute | solution.py:280
  60.3 9.3 %collective-permute-start.17 = (bf16[16,64,128]{2,1,0:T(8,128)(2,1)S(1)}, bf16[16,64,128]{2,1,0:T(8,128)(2,1)S(1)}, u32[]{:S(2)}, u32[]{:S(2)}) collective-permute-start(bf16[16,64,128]{2,1,0:T(8,128)(2,1)S(1)} %get-tuple-element.47), channel_id=1, source_target_pairs={{0,8},{8,0},{16,24},{24,16},{1,9},{9,1},{17,25},{25,17},{2,10},{10... | collective-permute-start | bytes 786440 | tf_op jit(solution)/shard_map/ppermute | solution.py:280
  60.9 9.1 %collective-permute-start.19 = (bf16[16,64,128]{2,1,0:T(8,128)(2,1)S(1)}, bf16[16,64,128]{2,1,0:T(8,128)(2,1)S(1)}, u32[]{:S(2)}, u32[]{:S(2)}) collective-permute-start(bf16[16,64,128]{2,1,0:T(8,128)(2,1)S(1)} %get-tuple-element.46), channel_id=1, source_target_pairs={{0,16},{8,24},{16,0},{24,8},{1,17},{9,25},{17,1},{25,9},{2,18},{10... | collective-permute-start | bytes 786440 | tf_op jit(solution)/shard_map/ppermute | solution.py:280
  61.5 11.3 %collective-permute-start.12 = (bf16[16,32,128]{2,1,0:T(8,128)(2,1)S(1)}, bf16[16,32,128]{2,1,0:T(8,128)(2,1)S(1)}, u32[]{:S(2)}, u32[]{:S(2)}) collective-permute-start(bf16[16,32,128]{2,1,0:T(8,128)(2,1)S(1)} %get-tuple-element.59), channel_id=1, source_target_pairs={{0,16},{8,24},{16,0},{24,8},{1,17},{9,25},{17,1},{25,9},{2,18},{10... | collective-permute-start | bytes 393224 | tf_op jit(solution)/shard_map/ppermute | solution.py:280
  63.1 9.7 %collective-permute-start.14 = (bf16[16,32,128]{2,1,0:T(8,128)(2,1)S(1)}, bf16[16,32,128]{2,1,0:T(8,128)(2,1)S(1)}, u32[]{:S(2)}, u32[]{:S(2)}) collective-permute-start(bf16[16,32,128]{2,1,0:T(8,128)(2,1)S(1)} %get-tuple-element.58), channel_id=1, source_target_pairs={{0,8},{8,0},{16,24},{24,16},{1,9},{9,1},{17,25},{25,17},{2,10},{10... | collective-permute-start | bytes 393224 | tf_op jit(solution)/shard_map/ppermute | solution.py:280
  70.1 5.0 %collective-permute-start.18 = (bf16[16,32,128]{2,1,0:T(8,128)(2,1)S(1)}, bf16[16,32,128]{2,1,0:T(8,128)(2,1)S(1)}, u32[]{:S(2)}, u32[]{:S(2)}) collective-permute-start(bf16[16,32,128]{2,1,0:T(8,128)(2,1)S(1)} %get-tuple-element.55), channel_id=1, source_target_pairs={{0,16},{8,24},{16,0},{24,8},{1,17},{9,25},{17,1},{25,9},{2,18},{10... | collective-permute-start | bytes 393224 | tf_op jit(solution)/shard_map/ppermute | solution.py:280
  70.7 5.0 %collective-permute-start.20 = (bf16[16,32,128]{2,1,0:T(8,128)(2,1)S(1)}, bf16[16,32,128]{2,1,0:T(8,128)(2,1)S(1)}, u32[]{:S(2)}, u32[]{:S(2)}) collective-permute-start(bf16[16,32,128]{2,1,0:T(8,128)(2,1)S(1)} %get-tuple-element.54), channel_id=1, source_target_pairs={{0,8},{8,0},{16,24},{24,16},{1,9},{9,1},{17,25},{25,17},{2,10},{10... | collective-permute-start | bytes 393224 | tf_op jit(solution)/shard_map/ppermute | solution.py:280
